TPU v7x, 32 devices: a whole 2x2x4 slice. The times are simulated.
32 devices in a mesh: expert: 4 (over y, x), cuts: 2 (over core), dp: 4 (over z).
Axes of the slice: x: 2, y: 2, z: 4, core: 2. Of those that a mesh axis runs over, the one named last changes fastest.
Arguments:
- activations: bfloat16 [2048, 2048], P(('expert', 'dp')), may hold values from -6 to 6
- out_grad: bfloat16 [2048, 2048], P(('expert', 'dp')), may hold values from -6 to 6
- expert_ids: int32 [2048, 1], P(('expert', 'dp')), may hold values from 0 to 3; in each aligned block of 128 rows (0 to 127, 128 to 255, ...) at most 40 rows name the same one
- gate_up_weight: bfloat16 [4, 2048, 2, 768], P('expert', None, None, 'cuts'), may hold values from -0.125 to 0.125
- down_weight: bfloat16 [4, 2048, 768], P('expert', None, 'cuts'), may hold values from -0.21875 to 0.21875
- master_weight: float32 [4, 2048, 3, 768], P('expert', 'dp', None, 'cuts'), may hold values from -6 to 6
- first_moment: bfloat16 [4, 2048, 3, 768], P('expert', 'dp', None, 'cuts'), may hold values from -6 to 6
- second_moment: bfloat16 [4, 2048, 3, 768], P('expert', 'dp', None, 'cuts'), may hold values from 0.5 to 8
- new_owner: int32 [4, 4], replicated, may hold values from 0 to 3, each once within a row
Outputs:
- input_grad: bfloat16 [2048, 2048], P(('expert', 'dp'), 'cuts')
- moved_master: float32 [4, 4, 512, 3, 768], P('expert', None, 'dp', None, 'cuts')
- moved_first: bfloat16 [4, 4, 512, 3, 768], P('expert', None, 'dp', None, 'cuts')
- moved_second: bfloat16 [4, 4, 512, 3, 768], P('expert', None, 'dp', None, 'cuts')
Inputs may be any that keep to these rules, and one draw needn't show every extreme that they name: `expert_ids`: within the 128 rows of one device no expert is named by more than 40 rows, and in every draw some device names some expert exactly 40 times. `new_owner`: each row names every owner index exactly once.
All inputs are finite; a program needn't handle non-finite values.
Results may differ from a plain program's by a relative error of at most 0.019.
Values may be sent and summed in bfloat16 or wider, within the bound.
No kernel may reach another device: no remote copies, remote signals or barrier semaphores. Data moves between devices by JAX's collectives and lax.ppermute only.
A program may use at most 64 MiB of HBM per device.

v0:
```python
import jax
import jax.numpy as jnp
from jax import lax
from jax.sharding import PartitionSpec as P

beta_first = 0.9
beta_second = 0.95
learn_rate = 0.01
decay_rate = 0.1
epsilon = 1e-08


def adam_update(master, first_old, second_old, gradient):
    first_new = beta_first * first_old.astype(jnp.float32) + (1.0 - beta_first) * gradient
    second_new = (
        beta_second * second_old.astype(jnp.float32) + (1.0 - beta_second) * gradient * gradient
    )
    master_new = master - learn_rate * (
        first_new / (jnp.sqrt(second_new) + epsilon) + decay_rate * master
    )
    return (master_new, first_new, second_new)


def local(
    activations,
    out_grad,
    expert_ids,
    gate_up_weight,
    down_weight,
    master_weight,
    first_moment,
    second_moment,
    new_owner,
):
    experts = lax.axis_size("expert")
    dp_count = lax.axis_size("dp")
    row_count = activations.shape[0]
    model_width = activations.shape[1]
    capacity = row_count // experts + max(1, row_count // (4 * experts))
    shard_rows = model_width // dp_count
    slice_rows = shard_rows // experts
    unit_count = master_weight.shape[3]
    expert_index = lax.axis_index("expert")
    owners = lax.dynamic_slice_in_dim(new_owner, expert_index, 1, 0)[0]
    send_order = jnp.argsort(owners)

    def arrange(tensor):
        return jnp.take(tensor.reshape(experts, slice_rows, 3, unit_count), send_order, axis=0)

    early_master = lax.all_to_all(
        arrange(master_weight[0]).astype(jnp.bfloat16),
        "expert",
        split_axis=0,
        concat_axis=0,
        tiled=True,
    ).astype(jnp.float32)
    early_first, early_second = (
        lax.all_to_all(arrange(first_moment[0]), "expert", split_axis=0, concat_axis=0, tiled=True),
        lax.all_to_all(
            arrange(second_moment[0]), "expert", split_axis=0, concat_axis=0, tiled=True
        ),
    )
    row_expert = expert_ids[:, 0]
    onehot = (row_expert[:, None] == jnp.arange(experts, dtype=jnp.int32)[None, :]).astype(
        jnp.int32
    )
    within = jnp.sum(jnp.cumsum(onehot, axis=0) * onehot, axis=1) - 1
    target = row_expert * capacity + within
    dispatch = (jnp.arange(experts * capacity, dtype=jnp.int32)[:, None] == target[None, :]).astype(
        jnp.bfloat16
    )
    send_in = jnp.dot(dispatch, activations, preferred_element_type=jnp.float32).astype(
        jnp.bfloat16
    )
    send_grad = jnp.dot(dispatch, out_grad, preferred_element_type=jnp.float32).astype(jnp.bfloat16)
    got_in, got_grad = (
        lax.all_to_all(
            send_in.reshape(experts, capacity, model_width),
            "expert",
            split_axis=0,
            concat_axis=0,
            tiled=True,
        ),
        lax.all_to_all(
            send_grad.reshape(experts, capacity, model_width),
            "expert",
            split_axis=0,
            concat_axis=0,
            tiled=True,
        ),
    )
    slots_in = got_in.reshape(experts * capacity, model_width)
    slots_grad = got_grad.reshape(experts * capacity, model_width)
    gate_up = gate_up_weight[0].reshape(model_width, -1)
    projected = jnp.dot(slots_in, gate_up, preferred_element_type=jnp.float32)
    gate_value = projected[:, :unit_count]
    lift_value = projected[:, unit_count:]
    sigmoid_gate = jax.nn.sigmoid(gate_value)
    silu_gate = gate_value * sigmoid_gate
    hidden = (silu_gate * lift_value).astype(jnp.bfloat16)
    hidden_grad = jnp.dot(slots_grad, down_weight[0], preferred_element_type=jnp.float32)
    lift_grad = (hidden_grad * silu_gate).astype(jnp.bfloat16)
    gate_grad = (
        hidden_grad * lift_value * sigmoid_gate * (1.0 + gate_value * (1.0 - sigmoid_gate))
    ).astype(jnp.bfloat16)
    pair_grad = jnp.concatenate([gate_grad, lift_grad], axis=1)
    slot_grad = lax.dot_general(
        pair_grad, gate_up, (((1,), (1,)), ((), ())), preferred_element_type=jnp.float32
    )
    returned = lax.all_to_all(
        slot_grad.astype(jnp.bfloat16).reshape(experts, capacity, model_width),
        "expert",
        split_axis=0,
        concat_axis=0,
        tiled=True,
    )
    row_grad = lax.dot_general(
        dispatch,
        returned.reshape(experts * capacity, model_width),
        (((0,), (0,)), ((), ())),
        preferred_element_type=jnp.float32,
    )
    input_grad = lax.psum_scatter(
        row_grad.astype(jnp.bfloat16), "cuts", scatter_dimension=1, tiled=True
    )
    paired = lax.dot_general(
        slots_in, pair_grad, (((0,), (0,)), ((), ())), preferred_element_type=jnp.float32
    )
    downed = lax.dot_general(
        slots_grad, hidden, (((0,), (0,)), ((), ())), preferred_element_type=jnp.float32
    )
    summed = lax.psum_scatter(
        jnp.concatenate([paired, downed], axis=1).astype(jnp.bfloat16),
        "dp",
        scatter_dimension=0,
        tiled=True,
    ).astype(jnp.float32)
    gradient = summed.reshape(shard_rows, 3, unit_count) / dp_count
    moved_gradient = lax.all_to_all(
        arrange(gradient).astype(jnp.bfloat16), "expert", split_axis=0, concat_axis=0, tiled=True
    ).astype(jnp.float32)
    moved_master, first_new, second_new = adam_update(
        early_master, early_first, early_second, moved_gradient
    )
    moved_first = first_new.astype(jnp.bfloat16)
    moved_second = second_new.astype(jnp.bfloat16)
    return (input_grad, moved_master[None], moved_first[None], moved_second[None])


def solution(mesh):
    in_specs = (
        P(("expert", "dp"), None),
        P(("expert", "dp"), None),
        P(("expert", "dp"), None),
        P("expert", None, None, "cuts"),
        P("expert", None, "cuts"),
        P("expert", "dp", None, "cuts"),
        P("expert", "dp", None, "cuts"),
        P("expert", "dp", None, "cuts"),
        P(),
    )
    out_specs = (
        P(("expert", "dp"), "cuts"),
        P("expert", None, "dp", None, "cuts"),
        P("expert", None, "dp", None, "cuts"),
        P("expert", None, "dp", None, "cuts"),
    )
    return jax.shard_map(local, mesh=mesh, in_specs=in_specs, out_specs=out_specs, check_vma=False)
```

profile of v0, /device:TPU:0, one launch (start us, length us, event | category | flops | bytes accessed | tf_op | source)
XLA Modules:
  0.0 232.7 jit_solution(882180027524556096)
XLA Ops:
  10.6 2.2 convolution_convert_fusion.3
  12.8 5.2 %all-to-all-start.1 = ((bf16[4,40,2048]{2,1,0:T(8,128)(2,1)}), bf16[4,40,2048]{2,1,0:T(8,128)(2,1)S(1)}, u32[]{:S(2)}, u32[]{:S(2)}) async-start(bf16[4,40,2048]{2,1,0:T(8,128)(2,1)} %bitcast.45), calls=%async_computation.1 | async-start | bytes 1310720 | tf_op jit(solution)/shard_map/all_to_all | solution.py:77
  19.1 8.2 %all-to-all-done.1 = bf16[4,40,2048]{2,1,0:T(8,128)(2,1)S(1)} async-done(((bf16[4,40,2048]{2,1,0:T(8,128)(2,1)}), bf16[4,40,2048]{2,1,0:T(8,128)(2,1)S(1)}, u32[]{:S(2)}, u32[]{:S(2)}) %all-to-all-start.1) | async-done | bytes 655392 | tf_op jit(solution)/shard_map/all_to_all | solution.py:77
  27.4 4.2 %all-to-all-start = ((bf16[4,40,2048]{2,1,0:T(8,128)(2,1)}), bf16[4,40,2048]{2,1,0:T(8,128)(2,1)}, u32[]{:S(2)}, u32[]{:S(2)}) async-start(bf16[4,40,2048]{2,1,0:T(8,128)(2,1)} %bitcast.44), calls=%async_computation | async-start | bytes 1310720 | tf_op jit(solution)/shard_map/all_to_all | solution.py:84
  31.6 2.5 %copy.14 = bf16[256,8,2,384]{3,1,2,0:T(8,128)(2,1)S(1)} copy(bf16[256,8,2,384]{3,2,1,0:T(2,128)(2,1)} %bitcast.43) | data formatting | bytes 6291456
  36.5 4.0 %all-to-all-done = bf16[4,40,2048]{2,1,0:T(8,128)(2,1)} async-done(((bf16[4,40,2048]{2,1,0:T(8,128)(2,1)}), bf16[4,40,2048]{2,1,0:T(8,128)(2,1)}, u32[]{:S(2)}, u32[]{:S(2)}) %all-to-all-start) | async-done | bytes 655392 | tf_op jit(solution)/shard_map/all_to_all | solution.py:84
  45.1 2.5 %pad_maximum_fusion = bf16[2048,1152]{0,1:T(8,128)(2,1)} fusion(bf16[2048,384]{0,1:T(8,128)(2,1)S(1)} %convolution_convert_fusion.1, bf16[2048,768]{0,1:T(8,128)(2,1)S(1)} %convolution_convert_fusion), kind=kLoop, calls=%fused_computation.4 | loop fusion | flops 9437184 | bytes 9437184 | tf_op jit(solution)/shard_map/concatenate | solution.py:133
  49.1 2.1 gather_fusion.3
  51.1 3.0 %gather_fusion.1 = bf16[4,128,3,384]{3,1,2,0:T(8,128)(2,1)} fusion(bf16[4,128,3,384]{3,1,0,2:T(8,128)(2,1)} %bitcast.48, s32[1024]{0:T(1024)S(1)} %pad_clamp_fusion), kind=kCustom, calls=%fused_computation.1.clone | custom fusion | bytes 2359312 | tf_op jit(solution)/shard_map/jit(_take)/gather | solution.py:48
  55.8 4.1 %convolution_convert_fusion.2 = bf16[160,2048]{1,0:T(8,128)(2,1)} fusion(bf16[2048,768]{1,0:T(8,128)(2,1)} %bitcast.40, bf16[160,384]{1,0:T(8,128)(2,1)} %copy-done.6, bf16[160,384]{1,0:T(8,128)(2,1)} %copy-done.5), kind=kOutput, calls=%fused_computation.11 | convolution fusion | flops 504135680 | bytes 4046848 | tf_op jit(solution)/shard_map/dot_general | solution.py:107
  59.9 4.2 %all-to-all-start.2 = ((bf16[4,40,2048]{2,1,0:T(8,128)(2,1)}), bf16[4,40,2048]{2,1,0:T(8,128)(2,1)}, u32[]{:S(2)}, u32[]{:S(2)}) async-start(bf16[4,40,2048]{2,1,0:T(8,128)(2,1)} %bitcast.46), calls=%async_computation.2 | async-start | bytes 1310720 | tf_op jit(solution)/shard_map/all_to_all | solution.py:110
  64.1 69.2 %reduce-scatter.5.cloned.1.call-done = bf16[512,1152]{0,1:T(8,128)(2,1)} async-done(((bf16[2048,1152]{0,1:T(8,128)(2,1)}), bf16[512,1152]{0,1:T(8,128)(2,1)}) %reduce-scatter.5.cloned.1.call-update) | async-done | bytes 1179664 | tf_op jit(solution)/shard_map/reduce_scatter | solution.py:132
  133.3 2.5 %convert_multiply_fusion.2 = bf16[512,1152]{0,1:T(8,128)(2,1)} fusion(bf16[512,1152]{0,1:T(8,128)(2,1)} %reduce-scatter.5.cloned.1.call-done), kind=kLoop, calls=%fused_computation.22 | loop fusion | flops 1769472 | bytes 2359296 | tf_op jit(solution)/shard_map/div | solution.py:138
  135.8 3.3 %div.17 = bf16[4,128,3,384]{1,0,3,2:T(4,128)(2,1)} reshape(bf16[512,1152]{0,1:T(8,128)(2,1)} %convert_multiply_fusion.2) | data formatting | bytes 2359296 | tf_op jit(solution)/shard_map/div | solution.py:138
  139.1 3.4 %copy.13 = bf16[4,128,3,384]{3,1,2,0:T(8,128)(2,1)} copy(bf16[4,128,3,384]{1,0,3,2:T(4,128)(2,1)} %div.17) | data formatting | bytes 2359296 | tf_op jit(solution)/shard_map/div | solution.py:138
  142.5 3.0 %gather_fusion.2 = bf16[4,128,3,384]{3,1,2,0:T(8,128)(2,1)} fusion(bf16[4,128,3,384]{3,1,2,0:T(8,128)(2,1)} %copy.13, s32[1024]{0:T(1024)S(1)} %pad_clamp_fusion), kind=kCustom, calls=%fused_computation.2.clone | custom fusion | bytes 2359312 | tf_op jit(solution)/shard_map/jit(_take)/gather | solution.py:48
  145.5 5.1 %broadcast_select_fusion = (bf16[4,128,3,384]{3,1,2,0:T(8,128)(2,1)}, bf16[4,128,3,384]{3,1,2,0:T(8,128)(2,1)}, bf16[4,128,3,384]{3,1,2,0:T(8,128)(2,1)}, bf16[4,128,3,384]{3,1,2,0:T(8,128)(2,1)}) fusion(bf16[4,128,3,384]{3,1,2,0:T(8,128)(2,1)S(1)} %gather_fusion.3, pred[4]{0:T(512)(128)(4,1)S(1)} %compare_and_fusion, ...), kind=kLoop, calls=%fused_computation.29 | loop fusion | flops 2359296 | bytes 9437188 | tf_op jit(solution)/shard_map/jit(_take)/select_n | solution.py:48
  150.6 19.5 %all_to_all.35 = bf16[4,128,3,384]{3,1,2,0:T(8,128)(2,1)S(1)} all-to-all(bf16[4,128,3,384]{3,1,2,0:T(8,128)(2,1)} %get-tuple-element.15), channel_id=1, replica_groups=mesh['expert'=4,'cuts'=2,'dp'=4] {'expert'}, dimensions={0} | all-to-all | bytes 2359296 | tf_op jit(solution)/shard_map/all_to_all | solution.py:139
  170.1 17.6 %all_to_all.36 = bf16[4,128,3,384]{3,1,2,0:T(8,128)(2,1)} all-to-all(bf16[4,128,3,384]{3,1,2,0:T(8,128)(2,1)S(1)} %copy-done.3), channel_id=1, replica_groups=mesh['expert'=4,'cuts'=2,'dp'=4] {'expert'}, dimensions={0} | all-to-all | bytes 2359296 | tf_op jit(solution)/shard_map/all_to_all | solution.py:59
  187.7 16.0 %all_to_all.37 = bf16[4,128,3,384]{3,1,2,0:T(8,128)(2,1)} all-to-all(bf16[4,128,3,384]{3,1,2,0:T(8,128)(2,1)S(1)} %copy-done.2), channel_id=1, replica_groups=mesh['expert'=4,'cuts'=2,'dp'=4] {'expert'}, dimensions={0} | all-to-all | bytes 2359296 | tf_op jit(solution)/shard_map/all_to_all | solution.py:58
  203.7 4.3 %all-to-all-start.3 = ((bf16[4,128,3,384]{3,1,2,0:T(8,128)(2,1)}), bf16[4,128,3,384]{3,1,2,0:T(8,128)(2,1)}, u32[]{:S(2)}, u32[]{:S(2)}) async-start(bf16[4,128,3,384]{3,1,2,0:T(8,128)(2,1)} %get-tuple-element.16), calls=%async_computation.4 | async-start | bytes 2359296 | tf_op jit(solution)/shard_map/all_to_all | solution.py:50
  208.2 2.2 convolution_convert_fusion.5
  210.5 8.6 %all-to-all-done.3 = bf16[4,128,3,384]{3,1,2,0:T(8,128)(2,1)} async-done(((bf16[4,128,3,384]{3,1,2,0:T(8,128)(2,1)}), bf16[4,128,3,384]{3,1,2,0:T(8,128)(2,1)}, u32[]{:S(2)}, u32[]{:S(2)}) %all-to-all-start.3) | async-done | bytes 1179680 | tf_op jit(solution)/shard_map/all_to_all | solution.py:50
  219.1 6.2 %fusion.9 = (bf16[1,4,128,3,384]{4,2,3,1,0:T(8,128)(2,1)}, f32[1,4,128,3,384]{4,2,3,1,0:T(8,128)}, bf16[1,4,128,3,384]{4,2,3,1,0:T(8,128)(2,1)}) fusion(bf16[4,128,3,384]{3,1,2,0:T(8,128)(2,1)S(1)} %all_to_all.35, bf16[4,128,3,384]{3,1,2,0:T(8,128)(2,1)} %all_to_all.36, bf16[4,128,3,384]{3,1,2,0:T(8,128)(2,1)} %all_to_all.37, ...), kind=kLoop, calls=%fused_computation.27 | loop fusion | flops 11206656 | bytes 9437184 | tf_op jit(solution)/shard_map/broadcast_in_dim | solution.py:147
  (38 shorter events, 14.0 us)
Async XLA Ops:
  8.0 46.1 %copy-start = (f32[1,512,3,384]{3,1,2,0:T(8,128)S(1)}, f32[1,512,3,384]{3,1,2,0:T(8,128)}, u32[]{:S(2)}) copy-start(f32[1,512,3,384]{3,1,2,0:T(8,128)} %param.18) | copy-start | bytes 7077892
  8.0 10.0 %copy-start.4 = (bf16[128,2048]{1,0:T(8,128)(2,1)S(1)}, bf16[128,2048]{1,0:T(8,128)(2,1)}, u32[]{:S(2)}) copy-start(bf16[128,2048]{1,0:T(8,128)(2,1)} %param.14) | copy-start | bytes 1572868
  12.8 14.6 %all-to-all-start.1 = ((bf16[4,40,2048]{2,1,0:T(8,128)(2,1)}), bf16[4,40,2048]{2,1,0:T(8,128)(2,1)S(1)}, u32[]{:S(2)}, u32[]{:S(2)}) async-start(bf16[4,40,2048]{2,1,0:T(8,128)(2,1)} %bitcast.45), calls=%async_computation.1 | async-start | bytes 1310720 | tf_op jit(solution)/shard_map/all_to_all | solution.py:77
  27.4 13.1 %all-to-all-start = ((bf16[4,40,2048]{2,1,0:T(8,128)(2,1)}), bf16[4,40,2048]{2,1,0:T(8,128)(2,1)}, u32[]{:S(2)}, u32[]{:S(2)}) async-start(bf16[4,40,2048]{2,1,0:T(8,128)(2,1)} %bitcast.44), calls=%async_computation | async-start | bytes 1310720 | tf_op jit(solution)/shard_map/all_to_all | solution.py:84
  31.6 101.7 %reduce-scatter.5.cloned.1.call-start = ((), (), s32[]{:S(2)}) async-start(), calls=%async_computation.10 | async-start | bytes 5898240 | tf_op jit(solution)/shard_map/reduce_scatter | solution.py:132
  34.1 1.7 copy-start.1
  40.5 1.8 copy-start.7
  44.0 1.1 copy-start.5
  44.0 1.1 copy-start.6
  59.9 90.7 %all-to-all-start.2 = ((bf16[4,40,2048]{2,1,0:T(8,128)(2,1)}), bf16[4,40,2048]{2,1,0:T(8,128)(2,1)}, u32[]{:S(2)}, u32[]{:S(2)}) async-start(bf16[4,40,2048]{2,1,0:T(8,128)(2,1)} %bitcast.46), calls=%async_computation.2 | async-start | bytes 1310720 | tf_op jit(solution)/shard_map/all_to_all | solution.py:110
  150.6 19.5 %copy-start.3 = (bf16[4,128,3,384]{3,1,2,0:T(8,128)(2,1)S(1)}, bf16[4,128,3,384]{3,1,2,0:T(8,128)(2,1)}, u32[]{:S(2)}) copy-start(bf16[4,128,3,384]{3,1,2,0:T(8,128)(2,1)} %get-tuple-element.13) | copy-start | bytes 3538948
  170.1 17.6 %copy-start.2 = (bf16[4,128,3,384]{3,1,2,0:T(8,128)(2,1)S(1)}, bf16[4,128,3,384]{3,1,2,0:T(8,128)(2,1)}, u32[]{:S(2)}) copy-start(bf16[4,128,3,384]{3,1,2,0:T(8,128)(2,1)} %get-tuple-element.14) | copy-start | bytes 3538948
  203.7 15.4 %all-to-all-start.3 = ((bf16[4,128,3,384]{3,1,2,0:T(8,128)(2,1)}), bf16[4,128,3,384]{3,1,2,0:T(8,128)(2,1)}, u32[]{:S(2)}, u32[]{:S(2)}) async-start(bf16[4,128,3,384]{3,1,2,0:T(8,128)(2,1)} %get-tuple-element.16), calls=%async_computation.4 | async-start | bytes 2359296 | tf_op jit(solution)/shard_map/all_to_all | solution.py:50
  208.0 17.3 %reduce-scatter.3.cloned.1.call-start = ((), (), s32[]{:S(2)}) async-start(), calls=%async_computation.9 | async-start | bytes 786432 | tf_op jit(solution)/shard_map/reduce_scatter | solution.py:123
Sparse Core Ops, SparseCore 0:
  47.7 85.5 reduce-scatter.4
Sparse Core Ops, SparseCore 1:
  211.3 8.9 reduce-scatter.2
where the time goes:
time: 234 us; the launch traced here: 233 us
  waiting for transfers between devices  90.1 us (39%)
  blocking collectives  53.1 us (23%)
  local copies, waits for them, and re-layouts  21.3 us (9%)
  other arithmetic  19.7 us (8%)
  starting transfers between devices  18 us (8%)
  between operations  15.6 us (7%)
  matrix products  14.9 us (6%)
    reduce_scatter x1, waiting for transfers between devices, local(): lax.psum_scatter(jnp.concatenate([paired, downed], axis=1).astype(jnp.bfl...  69.2 us
    all_to_all x1, blocking collectives, local(): lax.all_to_all(arrange(gradient).astype(jnp.bfloat16), 'expert', split_ax...  19.5 us
    all_to_all x1, blocking collectives, local(): lax.all_to_all(arrange(second_moment[0]), 'expert', split_axis=0, concat_...  17.6 us
    all_to_all x1, blocking collectives, local(): lax.all_to_all(arrange(first_moment[0]), 'expert', split_axis=0, concat_a...  16 us
    gather x4, local copies, waits for them, and re-layouts, arrange(): jnp.take(tensor.reshape(experts, slice_rows, 3, unit_count), send_order,...  9.74 us
    all_to_all x1, waiting for transfers between devices, local(): lax.all_to_all(arrange(master_weight[0]).astype(jnp.bfloat16), 'expert',...  8.59 us
    all_to_all x1, waiting for transfers between devices, local(): lax.all_to_all(send_in.reshape(experts, capacity, model_width), 'expert',...  8.25 us
    div x2, local copies, waits for them, and re-layouts, local(): gradient = summed.reshape(shard_rows, 3, unit_count) / dp_count  6.68 us
  transfers between devices with their start and end apart: 6, of which 4 were waited for; matrix products, arithmetic and copies ran while one was open for 18% of the time, Pallas kernels for 0%

commit v1 on v0

v1 whole, which is shorter than its diff:
```python
import functools

import jax
import jax.numpy as jnp
from jax import lax
from jax.experimental import pallas as pl
from jax.experimental.pallas import tpu as pltpu
from jax.sharding import PartitionSpec as P

beta_first = 0.9
beta_second = 0.95
learn_rate = 0.01
decay_rate = 0.1
epsilon = 1e-08

F32 = jnp.float32
BF16 = jnp.bfloat16
VMEM = pl.BlockSpec(memory_space=pltpu.VMEM)
MIB = 1 << 20


def adam_update(master, first_old, second_old, gradient):
    first_new = beta_first * first_old.astype(F32) + (1.0 - beta_first) * gradient
    second_new = beta_second * second_old.astype(F32) + (1.0 - beta_second) * gradient * gradient
    master_new = master - learn_rate * (
        first_new / (jnp.sqrt(second_new) + epsilon) + decay_rate * master
    )
    return (master_new, first_new, second_new)


def expert_grads(gate, lift, hidden_grad):
    sigmoid = jax.nn.sigmoid(gate)
    silu = gate * sigmoid
    hidden = (silu * lift).astype(BF16)
    lift_grad = (hidden_grad * silu).astype(BF16)
    gate_grad = (hidden_grad * lift * sigmoid * (1.0 + gate * (1.0 - sigmoid))).astype(BF16)
    return gate_grad, lift_grad, hidden


def slot_masks(ids, me, experts, capacity):
    rows = ids.shape[1]
    high = max(8, experts)
    match = lax.broadcasted_iota(jnp.int32, (high, rows), 0) == ids
    onehot = jnp.where(match, 1.0, 0.0)
    earlier = jnp.where(
        lax.broadcasted_iota(jnp.int32, (rows, rows), 0)
        < lax.broadcasted_iota(jnp.int32, (rows, rows), 1),
        1.0,
        0.0,
    )
    counts = jnp.dot(onehot.astype(BF16), earlier.astype(BF16), preferred_element_type=F32)
    within = jnp.sum(onehot * counts, axis=0, keepdims=True).astype(jnp.int32)
    slot = lax.broadcasted_iota(jnp.int32, (capacity, rows), 0)
    masks = [
        jnp.where(jnp.where(ids == (me ^ k), within, -1) == slot, 1.0, 0.0) for k in range(experts)
    ]
    return jnp.concatenate(masks, axis=0).astype(BF16)


def dispatch_kernel(experts, capacity, dp_count, ids_ref, in_ref, grad_ref, *out_refs):
    me = lax.axis_index("expert")
    core = lax.axis_index("cuts")
    half = out_refs[0].shape[2] // 2
    cores = in_ref.shape[1] // (dp_count * half)
    masks = slot_masks(ids_ref[...], me, experts, capacity)
    for q in range(dp_count):
        columns = pl.ds(pl.multiple_of((q * cores + core) * half, half), half)
        for x_ref, start in ((in_ref, 0), (grad_ref, half)):
            picked = jnp.dot(masks, x_ref[:, columns], preferred_element_type=F32)
            for k in range(experts):
                out_refs[k][q, :, start : start + half] = picked[
                    k * capacity : (k + 1) * capacity
                ].astype(BF16)


def collect_kernel(experts, dp_count, *refs):
    got, whole, parts = refs[:experts], refs[experts], refs[experts + 1 :]
    me = lax.axis_index("dp")
    for q in range(dp_count):
        joined = jnp.concatenate([got[k][q].astype(F32) for k in range(experts)], axis=0)
        whole[q] = joined.astype(BF16)
    for a in range(1, dp_count):
        parts[a - 1][...] = whole[lax.rem(me + a, dp_count)]


def expert_kernel(dp_count, mine_ref, other_ref, gate_up_ref, down_ref, out_ref):
    core = lax.axis_index("cuts")
    half = mine_ref.shape[2] // 2
    units = down_ref.shape[1]
    rows = mine_ref.shape[1]
    projected = jnp.zeros((rows, 2 * units), F32)
    hidden_grad = jnp.zeros((rows, units), F32)
    for x_ref, side in ((mine_ref, core), (other_ref, 1 - core)):
        for q in range(dp_count):
            depth = pl.ds(pl.multiple_of((2 * q + side) * half, half), half)
            projected += jnp.dot(x_ref[q, :, :half], gate_up_ref[depth, :], preferred_element_type=F32)
            hidden_grad += jnp.dot(x_ref[q, :, half:], down_ref[depth, :], preferred_element_type=F32)
    gate_grad, lift_grad, hidden = expert_grads(
        projected[:, :units], projected[:, units:], hidden_grad
    )
    out_ref[:, :units] = gate_grad
    out_ref[:, units : 2 * units] = lift_grad
    out_ref[:, 2 * units :] = hidden


def slot_grad_kernel(pair_ref, gate_up_ref, keep_ref, send_ref):
    core = lax.axis_index("cuts")
    width = keep_ref.shape[1]
    units = gate_up_ref.shape[1]
    pair = pair_ref[:, :units]
    for out_ref, side in ((keep_ref, core), (send_ref, 1 - core)):
        depth = pl.ds(pl.multiple_of(side * width, width), width)
        out_ref[...] = lax.dot_general(
            pair, gate_up_ref[depth, :], (((1,), (1,)), ((), ())), preferred_element_type=F32
        ).astype(BF16)


def split_kernel(capacity, keep_ref, got_ref, *out_refs):
    total = keep_ref[...].astype(F32) + got_ref[...].astype(F32)
    for k, out_ref in enumerate(out_refs):
        out_ref[...] = total[k * capacity : (k + 1) * capacity].astype(BF16)


def combine_kernel(experts, capacity, ids_ref, *refs):
    got, out_ref = refs[:experts], refs[experts]
    me = lax.axis_index("expert")
    masks = slot_masks(ids_ref[...], me, experts, capacity)
    joined = jnp.concatenate([got[k][...].astype(F32) for k in range(experts)], axis=0)
    out_ref[...] = lax.dot_general(
        masks, joined.astype(BF16), (((0,), (0,)), ((), ())), preferred_element_type=F32
    ).astype(BF16)


def arrange_kernel(experts, owner_ref, master_ref, first_ref, second_ref, *out_refs):
    me = lax.axis_index("expert")
    height = out_refs[0].shape[1]
    for k in range(experts):
        j = 0
        for i in range(experts):
            j = jnp.where(owner_ref[me, i] == (me ^ k), i, j)
        rows = pl.ds(pl.multiple_of(j * height, height), height)
        for m in range(3):
            out_refs[k][m] = master_ref[m, rows, :].astype(BF16)
            out_refs[k][3 + m] = first_ref[m, rows, :]
            out_refs[k][6 + m] = second_ref[m, rows, :]


def weight_kernel(experts, dp_count, owner_ref, *refs):
    mine, other = refs[:dp_count], refs[dp_count : 2 * dp_count]
    hidden = refs[2 * dp_count : 3 * dp_count]
    outs = refs[3 * dp_count : 3 * dp_count + experts]
    held = refs[3 * dp_count + experts]
    me = lax.axis_index("expert")
    core = lax.axis_index("cuts")
    part = lax.axis_index("dp")
    height = outs[0].shape[1]
    units = outs[0].shape[2]
    half = mine[1].shape[1] // 2
    per_half = half // height
    for source, side in ((mine, core), (other, 1 - core)):
        pair = jnp.zeros((half, 2 * units), F32)
        down = jnp.zeros((half, units), F32)
        for a in range(dp_count):
            rows = source[0][part] if a == 0 else source[a][...]
            pair += lax.dot_general(
                rows[:, :half], hidden[a][:, : 2 * units], (((0,), (0,)), ((), ())),
                preferred_element_type=F32,
            )
            down += lax.dot_general(
                rows[:, half:], hidden[a][:, 2 * units :], (((0,), (0,)), ((), ())),
                preferred_element_type=F32,
            )
        pair = pair * (1.0 / dp_count)
        down = down * (1.0 / dp_count)
        for i in range(per_half):
            rows = slice(i * height, (i + 1) * height)
            held[0] = pair[rows, :units].astype(BF16)
            held[1] = pair[rows, units:].astype(BF16)
            held[2] = down[rows].astype(BF16)
            k_of = owner_ref[me, side * per_half + i] ^ me
            for k in range(experts):

                @pl.when(k_of == k)
                def _():
                    outs[k][...] = held[...]


def adam_kernel(source_ref, state_master, state_first, state_second, grad_ref, *refs):
    out_master, out_first, out_second = refs[-3:]
    master, first, second = adam_update(
        state_master[0].astype(F32), state_first[0], state_second[0], grad_ref[0].astype(F32)
    )
    out_master[0, 0] = master
    out_first[0, 0] = first.astype(BF16)
    out_second[0, 0] = second.astype(BF16)


def call(kernel, out_shape, n_in, smem=(), scratch=(), limit=40, flops=0, moved=0):
    specs = [pl.BlockSpec(memory_space=pltpu.SMEM) if i in smem else VMEM for i in range(n_in)]
    return pl.pallas_call(
        kernel,
        out_shape=out_shape,
        in_specs=specs,
        out_specs=jax.tree.map(lambda _: VMEM, out_shape),
        scratch_shapes=list(scratch),
        compiler_params=pltpu.CompilerParams(vmem_limit_bytes=limit * MIB),
        cost_estimate=pl.CostEstimate(flops=flops, bytes_accessed=moved, transcendentals=0),
    )


def shape(*dims, dtype=BF16):
    return jax.ShapeDtypeStruct(dims, dtype)


def adam_step(state, grad, source, buffers, experts):
    parts, height, units = grad.shape
    block = lambda at: pl.BlockSpec((1, height, units), lambda m, s, at=at: (at + m, 0, 0))
    out_block = pl.BlockSpec((1, 1, height, units), lambda m, s: (s[0], m, 0, 0))
    out_shape = [shape(experts, parts, height, units, dtype=t) for t in (F32, BF16, BF16)]
    held = [pl.BlockSpec(memory_space=pl.ANY)] * len(buffers)
    return pl.pallas_call(
        adam_kernel,
        grid_spec=pltpu.PrefetchScalarGridSpec(
            num_scalar_prefetch=1,
            grid=(parts,),
            in_specs=[block(0), block(parts), block(2 * parts), block(0)] + held,
            out_specs=[out_block] * 3,
        ),
        out_shape=out_shape,
        input_output_aliases={5 + i: i for i in range(len(buffers))},
        compiler_params=pltpu.CompilerParams(vmem_limit_bytes=16 * MIB),
        cost_estimate=pl.CostEstimate(
            flops=20 * parts * height * units, bytes_accessed=16 * parts * height * units,
            transcendentals=2 * parts * height * units,
        ),
    )(source, state, state, state, grad, *buffers)


def exchange(tensor, axis, k, count):
    return lax.ppermute(tensor, axis, [(i, i ^ k) for i in range(count)])


def rotate(tensor, axis, a, count):
    return lax.ppermute(tensor, axis, [(i, (i + a) % count) for i in range(count)])


def after(values, *others):
    return lax.optimization_barrier((values, others))[0]


def aligned_local(
    activations,
    out_grad,
    expert_ids,
    gate_up_weight,
    down_weight,
    master_weight,
    first_moment,
    second_moment,
    new_owner,
):
    experts = lax.axis_size("expert")
    dp_count = lax.axis_size("dp")
    cores = lax.axis_size("cuts")
    row_count, model_width = activations.shape
    capacity = row_count // experts + max(1, row_count // (4 * experts))
    slots = experts * capacity
    shard_rows = model_width // dp_count
    half = shard_rows // cores
    height = shard_rows // experts
    units = master_weight.shape[3]
    me = lax.axis_index("expert")
    ids = expert_ids.reshape(1, row_count)
    gate_up = gate_up_weight[0].reshape(model_width, 2 * units)
    down = down_weight[0]

    sent = call(
        functools.partial(dispatch_kernel, experts, capacity, dp_count),
        [shape(dp_count, capacity, 2 * half)] * experts,
        3,
        flops=2 * slots * row_count * model_width,
        moved=4 * row_count * model_width + 4 * slots * model_width,
    )(ids, activations, out_grad)
    got = [sent[0]] + [exchange(sent[k], "expert", k, experts) for k in range(1, experts)]

    states = call(
        functools.partial(arrange_kernel, experts),
        [shape(9, height, units)] * experts,
        4,
        smem=(0,),
        moved=14 * shard_rows * 3 * units,
    )(
        new_owner,
        master_weight[0].transpose(1, 0, 2),
        first_moment[0].transpose(1, 0, 2),
        second_moment[0].transpose(1, 0, 2),
    )

    mine, *parts = call(
        functools.partial(collect_kernel, experts, dp_count),
        [shape(dp_count, slots, 2 * half)] + [shape(slots, 2 * half)] * (dp_count - 1),
        experts,
        moved=12 * slots * model_width,
    )(*got)
    other = exchange(mine, "cuts", 1, cores)
    part_mine = [mine] + [rotate(parts[a - 1], "dp", a, dp_count) for a in range(1, dp_count)]
    states_sent = after(list(states[1:]), *got[1:])
    moved_states = [states[0]] + [
        exchange(states_sent[k - 1], "expert", k, experts) for k in range(1, experts)
    ]

    hidden = call(
        functools.partial(expert_kernel, dp_count),
        shape(slots, 3 * units),
        4,
        flops=6 * slots * model_width * units,
        moved=6 * model_width * units + 8 * slots * model_width,
    )(mine, other, gate_up, down)
    hiddens = [hidden] + [rotate(hidden, "dp", a, dp_count) for a in range(1, dp_count)]
    part_other = [other] + [exchange(part_mine[a], "cuts", 1, cores) for a in range(1, dp_count)]

    keep, give = call(
        slot_grad_kernel,
        [shape(slots, model_width // cores)] * 2,
        2,
        flops=4 * slots * model_width * units,
        moved=4 * model_width * units + 4 * slots * model_width,
    )(hidden, gate_up)
    taken = exchange(give, "cuts", 1, cores)
    back = call(
        functools.partial(split_kernel, capacity),
        [shape(capacity, model_width // cores)] * experts,
        2,
        moved=6 * slots * model_width // cores,
    )(keep, taken)
    returned = [back[0]] + [exchange(back[k], "expert", k, experts) for k in range(1, experts)]
    input_grad = call(
        functools.partial(combine_kernel, experts, capacity),
        shape(row_count, model_width // cores),
        1 + experts,
        flops=2 * slots * row_count * model_width // cores,
        moved=4 * slots * model_width // cores,
    )(ids, *returned)

    grads = call(
        functools.partial(weight_kernel, experts, dp_count),
        [shape(3, height, units)] * experts,
        1 + 3 * dp_count,
        smem=(0,),
        scratch=[pltpu.VMEM((3, height, units), BF16)],
        flops=6 * slots * dp_count * shard_rows * units,
        moved=4 * slots * dp_count * (shard_rows + units),
    )(new_owner, *part_mine, *part_other, *hiddens)
    moved_grads = [grads[0]] + [exchange(grads[k], "expert", k, experts) for k in range(1, experts)]

    buffers = ()
    for k in range(experts):
        source = (me ^ k).astype(jnp.int32).reshape(1)
        buffers = adam_step(moved_states[k], moved_grads[k], source, buffers, experts)
    outs = [b.transpose(0, 2, 1, 3)[None] for b in buffers]
    return (input_grad, *outs)


def plain_local(
    activations,
    out_grad,
    expert_ids,
    gate_up_weight,
    down_weight,
    master_weight,
    first_moment,
    second_moment,
    new_owner,
):
    experts = lax.axis_size("expert")
    dp_count = lax.axis_size("dp")
    row_count = activations.shape[0]
    model_width = activations.shape[1]
    capacity = row_count // experts + max(1, row_count // (4 * experts))
    shard_rows = model_width // dp_count
    slice_rows = shard_rows // experts
    unit_count = master_weight.shape[3]
    expert_index = lax.axis_index("expert")
    owners = lax.dynamic_slice_in_dim(new_owner, expert_index, 1, 0)[0]
    send_order = jnp.argsort(owners)
    scatter = functools.partial(
        lax.all_to_all, axis_name="expert", split_axis=0, concat_axis=0, tiled=True
    )

    def arrange(tensor):
        return jnp.take(tensor.reshape(experts, slice_rows, 3, unit_count), send_order, axis=0)

    early_master = scatter(arrange(master_weight[0]).astype(BF16)).astype(F32)
    early_first = scatter(arrange(first_moment[0]))
    early_second = scatter(arrange(second_moment[0]))
    row_expert = expert_ids[:, 0]
    onehot = (row_expert[:, None] == jnp.arange(experts, dtype=jnp.int32)[None, :]).astype(
        jnp.int32
    )
    within = jnp.sum(jnp.cumsum(onehot, axis=0) * onehot, axis=1) - 1
    target = row_expert * capacity + within
    dispatch = (
        jnp.arange(experts * capacity, dtype=jnp.int32)[:, None] == target[None, :]
    ).astype(BF16)
    rows = jnp.concatenate([activations, out_grad], axis=1)
    sent = jnp.dot(dispatch, rows, preferred_element_type=F32).astype(BF16)
    got = scatter(sent.reshape(experts, capacity, 2 * model_width))
    got = got.reshape(experts * capacity, 2 * model_width)
    slots_in, slots_grad = got[:, :model_width], got[:, model_width:]
    gate_up = gate_up_weight[0].reshape(model_width, -1)
    projected = jnp.dot(slots_in, gate_up, preferred_element_type=F32)
    hidden_grad = jnp.dot(slots_grad, down_weight[0], preferred_element_type=F32)
    gate_grad, lift_grad, hidden = expert_grads(
        projected[:, :unit_count], projected[:, unit_count:], hidden_grad
    )
    pair_grad = jnp.concatenate([gate_grad, lift_grad], axis=1)
    slot_grad = lax.dot_general(
        pair_grad, gate_up, (((1,), (1,)), ((), ())), preferred_element_type=F32
    )
    returned = scatter(slot_grad.astype(BF16).reshape(experts, capacity, model_width))
    row_grad = lax.dot_general(
        dispatch,
        returned.reshape(experts * capacity, model_width),
        (((0,), (0,)), ((), ())),
        preferred_element_type=F32,
    )
    input_grad = lax.psum_scatter(row_grad.astype(BF16), "cuts", scatter_dimension=1, tiled=True)
    paired = lax.dot_general(
        slots_in, pair_grad, (((0,), (0,)), ((), ())), preferred_element_type=F32
    )
    downed = lax.dot_general(
        slots_grad, hidden, (((0,), (0,)), ((), ())), preferred_element_type=F32
    )
    summed = lax.psum_scatter(
        jnp.concatenate([paired, downed], axis=1).astype(BF16),
        "dp",
        scatter_dimension=0,
        tiled=True,
    ).astype(F32)
    gradient = summed.reshape(shard_rows, 3, unit_count) / dp_count
    moved_gradient = scatter(arrange(gradient).astype(BF16)).astype(F32)
    moved_master, first_new, second_new = adam_update(
        early_master, early_first, early_second, moved_gradient
    )
    return (
        input_grad,
        moved_master[None],
        first_new.astype(BF16)[None],
        second_new.astype(BF16)[None],
    )


def local(*args):
    experts = lax.axis_size("expert")
    dp_count = lax.axis_size("dp")
    cores = lax.axis_size("cuts")
    row_count, model_width = args[0].shape
    capacity = row_count // experts + max(1, row_count // (4 * experts))
    height = model_width // (dp_count * experts)
    whole_tiles = (
        experts & (experts - 1) == 0
        and cores == 2
        and capacity % 8 == 0
        and (experts * capacity) % 16 == 0
        and row_count % 128 == 0
        and height % 128 == 0
        and (model_width // (dp_count * cores)) % height == 0
        and args[5].shape[3] % 128 == 0
    )
    return (aligned_local if whole_tiles else plain_local)(*args)


def solution(mesh):
    in_specs = (
        P(("expert", "dp"), None),
        P(("expert", "dp"), None),
        P(("expert", "dp"), None),
        P("expert", None, None, "cuts"),
        P("expert", None, "cuts"),
        P("expert", "dp", None, "cuts"),
        P("expert", "dp", None, "cuts"),
        P("expert", "dp", None, "cuts"),
        P(),
    )
    out_specs = (
        P(("expert", "dp"), "cuts"),
        P("expert", None, "dp", None, "cuts"),
        P("expert", None, "dp", None, "cuts"),
        P("expert", None, "dp", None, "cuts"),
    )
    return jax.shard_map(local, mesh=mesh, in_specs=in_specs, out_specs=out_specs, check_vma=False)
```

time: 234 us -> 107 us (0.46)
  blocking collectives: 53.1 us -> 0 us
  waiting for transfers between devices: 90.1 us -> 46.9 us
  Pallas kernels: 0 us -> 20.5 us
  other arithmetic: 19.7 us -> 0 us
  matrix products: 14.9 us -> 0 us
  between operations: 15.6 us -> 0.8 us
  local copies, waits for them, and re-layouts: 21.3 us -> 10 us
  starting transfers between devices: 18 us -> 28.4 us
    reduce_scatter x2 -> x0, waiting for transfers between devices: 69.2 us -> none  [the longest x1 69.2 us: local(): lax.psum_scatter(jnp.concatenate([paired, downed], axis=1).astype(jnp.bfl...]
    all_to_all x3 -> x0, blocking collectives: 53.1 us -> none  [the longest x1 19.5 us: local(): lax.all_to_all(arrange(gradient).astype(jnp.bfloat16), 'expert', split_ax...]
    ppermute x0 -> x23, waiting for transfers between devices: none -> 46.9 us  [the longest x6 35.6 us: rotate(): lax.ppermute(tensor, axis, [(i, (i + a) % count) for i in range(count)])]
    ppermute x0 -> x23, starting transfers between devices: none -> 28.4 us  [the longest x17 16.3 us: exchange(): return lax.ppermute(tensor, axis, [(i, i ^ k) for i in range(count)])]
    all_to_all x4 -> x0, waiting for transfers between devices: 20.9 us -> none  [the longest x1 8.59 us: local(): lax.all_to_all(arrange(master_weight[0]).astype(jnp.bfloat16), 'expert',...]
    pallas_call x0 -> x12, Pallas kernels: none -> 20.5 us  [the longest x4 10.7 us: adam_step(): pl.pallas_call(adam_kernel, grid_spec=pltpu.PrefetchScalarGridSpec(num_sc...]
    all_to_all x4 -> x0, starting transfers between devices: 17.8 us -> none  [the longest x1 5.16 us: local(): lax.all_to_all(send_in.reshape(experts, capacity, model_width), 'expert',...]
    dot_general x8 -> x0, matrix products: 14.9 us -> none  [the longest x1 4.08 us: local(): lax.dot_general(pair_grad, gate_up, (((1,), (1,)), ((), ())), preferred_e...]
  transfers between devices with their start and end apart: 6 -> 23, of which waited for: 4 -> 9; matrix products, arithmetic and copies ran while one was open for 18% -> 1% of each run, Pallas kernels for 0% -> 16%
where the time goes in v1:
time: 107 us
  waiting for transfers between devices  46.9 us (44%)
  starting transfers between devices  28.4 us (27%)
  Pallas kernels  20.5 us (19%)
  local copies, waits for them, and re-layouts  10 us (9%)
    ppermute x6, waiting for transfers between devices, rotate(): lax.ppermute(tensor, axis, [(i, (i + a) % count) for i in range(count)])  35.6 us
    ppermute x17, starting transfers between devices, exchange(): return lax.ppermute(tensor, axis, [(i, i ^ k) for i in range(count)])  16.3 us
    ppermute x6, starting transfers between devices, rotate(): lax.ppermute(tensor, axis, [(i, (i + a) % count) for i in range(count)])  12.1 us
    ppermute x17, waiting for transfers between devices, exchange(): return lax.ppermute(tensor, axis, [(i, i ^ k) for i in range(count)])  11.3 us
    pallas_call x4, Pallas kernels, adam_step(): pl.pallas_call(adam_kernel, grid_spec=pltpu.PrefetchScalarGridSpec(num_sc...  10.7 us
    unnamed x41, local copies, waits for them, and re-layouts  10 us
    pallas_call x1, Pallas kernels, aligned_local(): call(functools.partial(weight_kernel, experts, dp_count), [shape(3, heigh...  3.7 us
    pallas_call x1, Pallas kernels, aligned_local(): call(functools.partial(arrange_kernel, experts), [shape(9, height, units)...  2.17 us
  transfers between devices with their start and end apart: 23, of which 9 were waited for; matrix products, arithmetic and copies ran while one was open for 1% of the time, Pallas kernels for 16%

profile of v1, /device:TPU:0, one launch (start us, length us, event | category | flops | bytes accessed | tf_op | source)
XLA Modules:
  0.0 106.7 jit_solution(7088158026189282257)
XLA Ops:
  3.9 3.0 %collective-permute-start = (bf16[4,40,512]{2,1,0:T(8,128)(2,1)S(1)}, bf16[4,40,512]{2,1,0:T(8,128)(2,1)S(1)}, u32[]{:S(2)}, u32[]{:S(2)}) collective-permute-start(bf16[4,40,512]{2,1,0:T(8,128)(2,1)S(1)} %get-tuple-element.42), channel_id=1, source_target_pairs={{0,8},{8,0},{16,24},{24,16},{1,9},{9,1},{17,25},{25,17},{2,10},{10... | collective-permute-start | bytes 491528 | tf_op jit(solution)/shard_map/ppermute | solution.py:240
  6.9 1.5 %collective-permute-start.1 = (bf16[4,40,512]{2,1,0:T(8,128)(2,1)S(1)}, bf16[4,40,512]{2,1,0:T(8,128)(2,1)S(1)}, u32[]{:S(2)}, u32[]{:S(2)}) collective-permute-start(bf16[4,40,512]{2,1,0:T(8,128)(2,1)S(1)} %get-tuple-element.43), channel_id=1, source_target_pairs={{0,16},{8,24},{16,0},{24,8},{1,17},{9,25},{17,1},{25,9},{2,18},{10... | collective-permute-start | bytes 491528 | tf_op jit(solution)/shard_map/ppermute | solution.py:240
  8.5 3.5 %collective-permute-done.refs_1_ = bf16[4,40,512]{2,1,0:T(8,128)(2,1)S(1)} collective-permute-done((bf16[4,40,512]{2,1,0:T(8,128)(2,1)S(1)}, bf16[4,40,512]{2,1,0:T(8,128)(2,1)S(1)}, u32[]{:S(2)}, u32[]{:S(2)}) %collective-permute-start) | collective-permute-done | bytes 163872 | tf_op jit(solution)/shard_map/ppermute | solution.py:240
  12.0 4.1 %collective-permute-done.1.refs_2_ = bf16[4,40,512]{2,1,0:T(8,128)(2,1)S(1)} collective-permute-done((bf16[4,40,512]{2,1,0:T(8,128)(2,1)S(1)}, bf16[4,40,512]{2,1,0:T(8,128)(2,1)S(1)}, u32[]{:S(2)}, u32[]{:S(2)}) %collective-permute-start.1) | collective-permute-done | bytes 163872 | tf_op jit(solution)/shard_map/ppermute | solution.py:240
  16.3 1.7 %copy-done = f32[1,512,3,384]{3,1,2,0:T(8,128)S(1)} copy-done((f32[1,512,3,384]{3,1,2,0:T(8,128)S(1)}, f32[1,512,3,384]{3,1,2,0:T(8,128)}, u32[]{:S(2)}) %copy-start) | copy-done | bytes 2359320
  18.0 1.3 %copy-done.3 = bf16[1,512,3,384]{3,1,2,0:T(8,128)(2,1)S(1)} copy-done((bf16[1,512,3,384]{3,1,2,0:T(8,128)(2,1)S(1)}, bf16[1,512,3,384]{3,1,2,0:T(8,128)(2,1)}, u32[]{:S(2)}) %copy-start.3) | copy-done | bytes 1179672
  19.2 2.2 %shard_map.126 = (bf16[9,128,384]{2,1,0:T(8,128)(2,1)S(1)}, bf16[9,128,384]{2,1,0:T(8,128)(2,1)S(1)}, bf16[9,128,384]{2,1,0:T(8,128)(2,1)}, bf16[9,128,384]{2,1,0:T(8,128)(2,1)}) custom-call(s32[4,4]{1,0:T(4,128)S(1)} %copy-done.16, f32[3,512,384]{2,1,0:T(8,128)S(1)} %bitcast.29, bf16[3,512,384]{2,1,0:T(8,128)(2,1)S(1)} %bitcast.31, ...), custom_call_target="tpu_custom_call" | custom-call | bytes 8257536 | tf_op jit(solution)/shard_map/pallas_call | solution.py:286
  22.6 1.6 %collective-permute-start.9 = (bf16[160,512]{1,0:T(8,128)(2,1)S(1)}, bf16[160,512]{1,0:T(8,128)(2,1)S(1)}, u32[]{:S(2)}, u32[]{:S(2)}) collective-permute-start(bf16[160,512]{1,0:T(8,128)(2,1)S(1)} %get-tuple-element.56), channel_id=1, source_target_pairs={{0,1},{1,2},{2,3},{3,0},{4,5},{5,6},{6,7},{7,4},{8,9},{9,10},{10,1... | collective-permute-start | bytes 491528 | tf_op jit(solution)/shard_map/ppermute | solution.py:244
  24.2 2.6 %collective-permute-start.10 = (bf16[160,512]{1,0:T(8,128)(2,1)S(1)}, bf16[160,512]{1,0:T(8,128)(2,1)S(1)}, u32[]{:S(2)}, u32[]{:S(2)}) collective-permute-start(bf16[160,512]{1,0:T(8,128)(2,1)S(1)} %get-tuple-element.57), channel_id=1, source_target_pairs={{0,2},{1,3},{2,0},{3,1},{4,6},{5,7},{6,4},{7,5},{8,10},{9,11},{10,... | collective-permute-start | bytes 491528 | tf_op jit(solution)/shard_map/ppermute | solution.py:244
  27.5 1.4 %collective-permute-start.11 = (bf16[160,512]{1,0:T(8,128)(2,1)S(1)}, bf16[160,512]{1,0:T(8,128)(2,1)S(1)}, u32[]{:S(2)}, u32[]{:S(2)}) collective-permute-start(bf16[160,512]{1,0:T(8,128)(2,1)S(1)} %get-tuple-element.58), channel_id=1, source_target_pairs={{0,3},{1,0},{2,1},{3,2},{4,7},{5,4},{6,5},{7,6},{8,11},{9,8},{10,9... | collective-permute-start | bytes 491528 | tf_op jit(solution)/shard_map/ppermute | solution.py:244
  31.8 6.2 %collective-permute-done.10.refs_2_ = bf16[160,512]{1,0:T(8,128)(2,1)S(1)} collective-permute-done((bf16[160,512]{1,0:T(8,128)(2,1)S(1)}, bf16[160,512]{1,0:T(8,128)(2,1)S(1)}, u32[]{:S(2)}, u32[]{:S(2)}) %collective-permute-start.10) | collective-permute-done | bytes 163872 | tf_op jit(solution)/shard_map/ppermute | solution.py:244
  39.3 1.8 %collective-permute-start.8 = (bf16[9,128,384]{2,1,0:T(8,128)(2,1)}, bf16[9,128,384]{2,1,0:T(8,128)(2,1)S(1)}, u32[]{:S(2)}, u32[]{:S(2)}) collective-permute-start(bf16[9,128,384]{2,1,0:T(8,128)(2,1)} %get-tuple-element.55), channel_id=1, source_target_pairs={{0,24},{8,16},{16,8},{24,0},{1,25},{9,17},{17,9},{25,1},{2,26},{10... | collective-permute-start | bytes 2654216 | tf_op jit(solution)/shard_map/ppermute | solution.py:240
  41.1 5.0 %collective-permute-start.17 = (bf16[160,1152]{1,0:T(8,128)(2,1)S(1)}, bf16[160,1152]{1,0:T(8,128)(2,1)S(1)}, u32[]{:S(2)}, u32[]{:S(2)}) collective-permute-start(bf16[160,1152]{1,0:T(8,128)(2,1)S(1)} %shard_map.122.pair_ref.refs_8_), channel_id=1, source_target_pairs={{0,3},{1,0},{2,1},{3,2},{4,7},{5,4},{6,5},{7,6},{8,11},{9,8},{10,9... | collective-permute-start | bytes 1105928 | tf_op jit(solution)/shard_map/ppermute | solution.py:244
  47.7 7.4 %collective-permute-done.17.refs_11_ = bf16[160,1152]{1,0:T(8,128)(2,1)S(1)} collective-permute-done((bf16[160,1152]{1,0:T(8,128)(2,1)S(1)}, bf16[160,1152]{1,0:T(8,128)(2,1)S(1)}, u32[]{:S(2)}, u32[]{:S(2)}) %collective-permute-start.17) | collective-permute-done | bytes 368672 | tf_op jit(solution)/shard_map/ppermute | solution.py:244
  56.1 21.6 %collective-permute-done.16.refs_10_ = bf16[160,1152]{1,0:T(8,128)(2,1)S(1)} collective-permute-done((bf16[160,1152]{1,0:T(8,128)(2,1)S(1)}, bf16[160,1152]{1,0:T(8,128)(2,1)S(1)}, u32[]{:S(2)}, u32[]{:S(2)}) %collective-permute-start.16) | collective-permute-done | bytes 368672 | tf_op jit(solution)/shard_map/ppermute | solution.py:244
  77.7 1.5 %collective-permute-start.6 = (bf16[40,1024]{1,0:T(8,128)(2,1)S(1)}, bf16[40,1024]{1,0:T(8,128)(2,1)S(1)}, u32[]{:S(2)}, u32[]{:S(2)}) collective-permute-start(bf16[40,1024]{1,0:T(8,128)(2,1)S(1)} %get-tuple-element.50), channel_id=1, source_target_pairs={{0,16},{8,24},{16,0},{24,8},{1,17},{9,25},{17,1},{25,9},{2,18},{10... | collective-permute-start | bytes 245768 | tf_op jit(solution)/shard_map/ppermute | solution.py:240
  80.4 3.7 %shard_map.127 = (bf16[3,128,384]{2,1,0:T(8,128)(2,1)S(1)}, bf16[3,128,384]{2,1,0:T(8,128)(2,1)}, bf16[3,128,384]{2,1,0:T(8,128)(2,1)}, bf16[3,128,384]{2,1,0:T(8,128)(2,1)}) custom-call(s32[4,4]{1,0:T(4,128)S(1)} %copy-done.16, bf16[4,160,512]{2,1,0:T(8,128)(2,1)S(1)} %get-tuple-element.45.mine_ref.refs_0_, ...), custom_call_target="tpu_custom_call" | custom-call | flops 754974720 | bytes 2293760 | tf_op jit(solution)/shard_map/pallas_call | solution.py:345
  87.0 1.5 %collective-permute-start.20 = (bf16[3,128,384]{2,1,0:T(8,128)(2,1)}, bf16[3,128,384]{2,1,0:T(8,128)(2,1)}, u32[]{:S(2)}, u32[]{:S(2)}) collective-permute-start(bf16[3,128,384]{2,1,0:T(8,128)(2,1)} %get-tuple-element.61), channel_id=1, source_target_pairs={{0,16},{8,24},{16,0},{24,8},{1,17},{9,25},{17,1},{25,9},{2,18},{10... | collective-permute-start | bytes 884744 | tf_op jit(solution)/shard_map/ppermute | solution.py:240
  91.3 1.8 %shard_map.128 = (f32[4,3,128,384]{3,2,1,0:T(8,128)}, bf16[4,3,128,384]{3,2,1,0:T(8,128)(2,1)}, bf16[4,3,128,384]{3,2,1,0:T(8,128)(2,1)}) custom-call(s32[1]{0:T(128)} %bitcast.11.source_ref, bf16[9,128,384]{2,1,0:T(8,128)(2,1)S(1)} %get-tuple-element.64.state_master.state_first.state_second, ...), custom_call_target="tpu_custom_call" | custom-call | flops 2949120 | bytes 2359296 | tf_op jit(solution)/shard_map/pallas_call | solution.py:221
  94.2 1.6 %collective-permute-done.22.grad_ref = bf16[3,128,384]{2,1,0:T(8,128)(2,1)} collective-permute-done((bf16[3,128,384]{2,1,0:T(8,128)(2,1)}, bf16[3,128,384]{2,1,0:T(8,128)(2,1)}, u32[]{:S(2)}, u32[]{:S(2)}) %collective-permute-start.22) | collective-permute-done | bytes 294944 | tf_op jit(solution)/shard_map/ppermute | solution.py:240
  95.8 3.0 %shard_map.129 = (f32[4,3,128,384]{3,2,1,0:T(8,128)}, bf16[4,3,128,384]{3,2,1,0:T(8,128)(2,1)}, bf16[4,3,128,384]{3,2,1,0:T(8,128)(2,1)}) custom-call(s32[1]{0:T(128)} %bitcast.10.source_ref, bf16[9,128,384]{2,1,0:T(8,128)(2,1)S(1)} %collective-permute-done.21.state_master.state_first.state_second, ...), custom_call_target="tpu_custom_call", output_to_operand_aliasing={{0}: (5, {}), {1}: (6, {}), {2}: (7, {})} | custom-call | flops 2949120 | bytes 2359296 | tf_op jit(solution)/shard_map/pallas_call | solution.py:221
  98.7 2.0 %collective-permute-done.20.grad_ref = bf16[3,128,384]{2,1,0:T(8,128)(2,1)} collective-permute-done((bf16[3,128,384]{2,1,0:T(8,128)(2,1)}, bf16[3,128,384]{2,1,0:T(8,128)(2,1)}, u32[]{:S(2)}, u32[]{:S(2)}) %collective-permute-start.20) | collective-permute-done | bytes 294944 | tf_op jit(solution)/shard_map/ppermute | solution.py:240
  100.7 3.0 %shard_map.130 = (f32[4,3,128,384]{3,2,1,0:T(8,128)}, bf16[4,3,128,384]{3,2,1,0:T(8,128)(2,1)}, bf16[4,3,128,384]{3,2,1,0:T(8,128)(2,1)}) custom-call(s32[1]{0:T(128)} %bitcast.9.source_ref, bf16[9,128,384]{2,1,0:T(8,128)(2,1)S(1)} %collective-permute-done.19.state_master.state_first.state_second, ...), custom_call_target="tpu_custom_call", output_to_operand_aliasing={{0}: (5, {}), {1}: (6, {}), {2}: (7, {})} | custom-call | flops 2949120 | bytes 2359296 | tf_op jit(solution)/shard_map/pallas_call | solution.py:221
  103.7 3.0 %shard_map.131 = (f32[4,3,128,384]{3,2,1,0:T(8,128)}, bf16[4,3,128,384]{3,2,1,0:T(8,128)(2,1)}, bf16[4,3,128,384]{3,2,1,0:T(8,128)(2,1)}) custom-call(s32[1]{0:T(128)} %bitcast.2.source_ref, bf16[9,128,384]{2,1,0:T(8,128)(2,1)S(1)} %collective-permute-done.8.state_master.state_first.state_second, ...), custom_call_target="tpu_custom_call", output_to_operand_aliasing={{0}: (5, {}), {1}: (6, {}), {2}: (7, {})} | custom-call | flops 2949120 | bytes 2359296 | tf_op jit(solution)/shard_map/pallas_call | solution.py:221
  (75 shorter events, 20.0 us)
Async XLA Ops:
  3.9 8.0 %collective-permute-start = (bf16[4,40,512]{2,1,0:T(8,128)(2,1)S(1)}, bf16[4,40,512]{2,1,0:T(8,128)(2,1)S(1)}, u32[]{:S(2)}, u32[]{:S(2)}) collective-permute-start(bf16[4,40,512]{2,1,0:T(8,128)(2,1)S(1)} %get-tuple-element.42), channel_id=1, source_target_pairs={{0,8},{8,0},{16,24},{24,16},{1,9},{9,1},{17,25},{25,17},{2,10},{10... | collective-permute-start | bytes 491528 | tf_op jit(solution)/shard_map/ppermute | solution.py:240
  6.9 9.2 %collective-permute-start.1 = (bf16[4,40,512]{2,1,0:T(8,128)(2,1)S(1)}, bf16[4,40,512]{2,1,0:T(8,128)(2,1)S(1)}, u32[]{:S(2)}, u32[]{:S(2)}) collective-permute-start(bf16[4,40,512]{2,1,0:T(8,128)(2,1)S(1)} %get-tuple-element.43), channel_id=1, source_target_pairs={{0,16},{8,24},{16,0},{24,8},{1,17},{9,25},{17,1},{25,9},{2,18},{10... | collective-permute-start | bytes 491528 | tf_op jit(solution)/shard_map/ppermute | solution.py:240
  8.5 7.7 %collective-permute-start.2 = (bf16[4,40,512]{2,1,0:T(8,128)(2,1)S(1)}, bf16[4,40,512]{2,1,0:T(8,128)(2,1)S(1)}, u32[]{:S(2)}, u32[]{:S(2)}) collective-permute-start(bf16[4,40,512]{2,1,0:T(8,128)(2,1)S(1)} %get-tuple-element.44), channel_id=1, source_target_pairs={{0,24},{8,16},{16,8},{24,0},{1,25},{9,17},{17,9},{25,1},{2,26},{10... | collective-permute-start | bytes 491528 | tf_op jit(solution)/shard_map/ppermute | solution.py:240
  16.2 12.7 %collective-permute-start.3 = (bf16[4,160,512]{2,1,0:T(8,128)(2,1)S(1)}, bf16[4,160,512]{2,1,0:T(8,128)(2,1)S(1)}, u32[]{:S(2)}, u32[]{:S(2)}) collective-permute-start(bf16[4,160,512]{2,1,0:T(8,128)(2,1)S(1)} %get-tuple-element.45.mine_ref.refs_0_), channel_id=1, source_target_pairs={{0,4},{4,0},{1,5},{5,1},{2,6},{6,2},{3,7},{7,3},{8,12},{12,8},{9,1... | collective-permute-start | bytes 1966088 | tf_op jit(solution)/shard_map/ppermute | solution.py:240
  21.4 24.7 %collective-permute-start.21 = (bf16[9,128,384]{2,1,0:T(8,128)(2,1)S(1)}, bf16[9,128,384]{2,1,0:T(8,128)(2,1)S(1)}, u32[]{:S(2)}, u32[]{:S(2)}) collective-permute-start(bf16[9,128,384]{2,1,0:T(8,128)(2,1)S(1)} %get-tuple-element.62), channel_id=1, source_target_pairs={{0,8},{8,0},{16,24},{24,16},{1,9},{9,1},{17,25},{25,17},{2,10},{10... | collective-permute-start | bytes 2654216 | tf_op jit(solution)/shard_map/ppermute | solution.py:240
  22.6 8.9 %collective-permute-start.9 = (bf16[160,512]{1,0:T(8,128)(2,1)S(1)}, bf16[160,512]{1,0:T(8,128)(2,1)S(1)}, u32[]{:S(2)}, u32[]{:S(2)}) collective-permute-start(bf16[160,512]{1,0:T(8,128)(2,1)S(1)} %get-tuple-element.56), channel_id=1, source_target_pairs={{0,1},{1,2},{2,3},{3,0},{4,5},{5,6},{6,7},{7,4},{8,9},{9,10},{10,1... | collective-permute-start | bytes 491528 | tf_op jit(solution)/shard_map/ppermute | solution.py:244
  24.2 13.7 %collective-permute-start.10 = (bf16[160,512]{1,0:T(8,128)(2,1)S(1)}, bf16[160,512]{1,0:T(8,128)(2,1)S(1)}, u32[]{:S(2)}, u32[]{:S(2)}) collective-permute-start(bf16[160,512]{1,0:T(8,128)(2,1)S(1)} %get-tuple-element.57), channel_id=1, source_target_pairs={{0,2},{1,3},{2,0},{3,1},{4,6},{5,7},{6,4},{7,5},{8,10},{9,11},{10,... | collective-permute-start | bytes 491528 | tf_op jit(solution)/shard_map/ppermute | solution.py:244
  27.5 10.4 %collective-permute-start.11 = (bf16[160,512]{1,0:T(8,128)(2,1)S(1)}, bf16[160,512]{1,0:T(8,128)(2,1)S(1)}, u32[]{:S(2)}, u32[]{:S(2)}) collective-permute-start(bf16[160,512]{1,0:T(8,128)(2,1)S(1)} %get-tuple-element.58), channel_id=1, source_target_pairs={{0,3},{1,0},{2,1},{3,2},{4,7},{5,4},{6,5},{7,6},{8,11},{9,8},{10,9... | collective-permute-start | bytes 491528 | tf_op jit(solution)/shard_map/ppermute | solution.py:244
  31.2 15.3 %collective-permute-start.4 = (bf16[160,1024]{1,0:T(8,128)(2,1)S(1)}, bf16[160,1024]{1,0:T(8,128)(2,1)S(1)}, u32[]{:S(2)}, u32[]{:S(2)}) collective-permute-start(bf16[160,1024]{1,0:T(8,128)(2,1)S(1)} %get-tuple-element.47), channel_id=1, source_target_pairs={{0,4},{4,0},{1,5},{5,1},{2,6},{6,2},{3,7},{7,3},{8,12},{12,8},{9,1... | collective-permute-start | bytes 983048 | tf_op jit(solution)/shard_map/ppermute | solution.py:240
  31.6 6.9 %collective-permute-start.12 = (bf16[160,512]{1,0:T(8,128)(2,1)S(1)}, bf16[160,512]{1,0:T(8,128)(2,1)S(1)}, u32[]{:S(2)}, u32[]{:S(2)}) collective-permute-start(bf16[160,512]{1,0:T(8,128)(2,1)S(1)} %collective-permute-done.9.refs_1_), channel_id=1, source_target_pairs={{0,4},{4,0},{1,5},{5,1},{2,6},{6,2},{3,7},{7,3},{8,12},{12,8},{9,1... | collective-permute-start | bytes 491528 | tf_op jit(solution)/shard_map/ppermute | solution.py:240
  37.9 1.4 %collective-permute-start.13 = (bf16[160,512]{1,0:T(8,128)(2,1)S(1)}, bf16[160,512]{1,0:T(8,128)(2,1)S(1)}, u32[]{:S(2)}, u32[]{:S(2)}) collective-permute-start(bf16[160,512]{1,0:T(8,128)(2,1)S(1)} %collective-permute-done.10.refs_2_), channel_id=1, source_target_pairs={{0,4},{4,0},{1,5},{5,1},{2,6},{6,2},{3,7},{7,3},{8,12},{12,8},{9,1... | collective-permute-start | bytes 491528 | tf_op jit(solution)/shard_map/ppermute | solution.py:240
  37.9 3.1 %collective-permute-start.14 = (bf16[160,512]{1,0:T(8,128)(2,1)S(1)}, bf16[160,512]{1,0:T(8,128)(2,1)S(1)}, u32[]{:S(2)}, u32[]{:S(2)}) collective-permute-start(bf16[160,512]{1,0:T(8,128)(2,1)S(1)} %collective-permute-done.11.refs_3_), channel_id=1, source_target_pairs={{0,4},{4,0},{1,5},{5,1},{2,6},{6,2},{3,7},{7,3},{8,12},{12,8},{9,1... | collective-permute-start | bytes 491528 | tf_op jit(solution)/shard_map/ppermute | solution.py:240
  38.4 60.3 %collective-permute-start.19 = (bf16[9,128,384]{2,1,0:T(8,128)(2,1)}, bf16[9,128,384]{2,1,0:T(8,128)(2,1)S(1)}, u32[]{:S(2)}, u32[]{:S(2)}) collective-permute-start(bf16[9,128,384]{2,1,0:T(8,128)(2,1)} %get-tuple-element.60), channel_id=1, source_target_pairs={{0,16},{8,24},{16,0},{24,8},{1,17},{9,25},{17,1},{25,9},{2,18},{10... | collective-permute-start | bytes 2654216 | tf_op jit(solution)/shard_map/ppermute | solution.py:240
  39.3 64.4 %collective-permute-start.8 = (bf16[9,128,384]{2,1,0:T(8,128)(2,1)}, bf16[9,128,384]{2,1,0:T(8,128)(2,1)S(1)}, u32[]{:S(2)}, u32[]{:S(2)}) collective-permute-start(bf16[9,128,384]{2,1,0:T(8,128)(2,1)} %get-tuple-element.55), channel_id=1, source_target_pairs={{0,24},{8,16},{16,8},{24,0},{1,25},{9,17},{17,9},{25,1},{2,26},{10... | collective-permute-start | bytes 2654216 | tf_op jit(solution)/shard_map/ppermute | solution.py:240
  41.1 14.1 %collective-permute-start.17 = (bf16[160,1152]{1,0:T(8,128)(2,1)S(1)}, bf16[160,1152]{1,0:T(8,128)(2,1)S(1)}, u32[]{:S(2)}, u32[]{:S(2)}) collective-permute-start(bf16[160,1152]{1,0:T(8,128)(2,1)S(1)} %shard_map.122.pair_ref.refs_8_), channel_id=1, source_target_pairs={{0,3},{1,0},{2,1},{3,2},{4,7},{5,4},{6,5},{7,6},{8,11},{9,8},{10,9... | collective-permute-start | bytes 1105928 | tf_op jit(solution)/shard_map/ppermute | solution.py:244
  46.1 31.6 %collective-permute-start.16 = (bf16[160,1152]{1,0:T(8,128)(2,1)S(1)}, bf16[160,1152]{1,0:T(8,128)(2,1)S(1)}, u32[]{:S(2)}, u32[]{:S(2)}) collective-permute-start(bf16[160,1152]{1,0:T(8,128)(2,1)S(1)} %shard_map.122.pair_ref.refs_8_), channel_id=1, source_target_pairs={{0,2},{1,3},{2,0},{3,1},{4,6},{5,7},{6,4},{7,5},{8,10},{9,11},{10,... | collective-permute-start | bytes 1105928 | tf_op jit(solution)/shard_map/ppermute | solution.py:244
  46.4 32.8 %collective-permute-start.15 = (bf16[160,1152]{1,0:T(8,128)(2,1)S(1)}, bf16[160,1152]{1,0:T(8,128)(2,1)S(1)}, u32[]{:S(2)}, u32[]{:S(2)}) collective-permute-start(bf16[160,1152]{1,0:T(8,128)(2,1)S(1)} %shard_map.122.pair_ref.refs_8_), channel_id=1, source_target_pairs={{0,1},{1,2},{2,3},{3,0},{4,5},{5,6},{6,7},{7,4},{8,9},{9,10},{10,1... | collective-permute-start | bytes 1105928 | tf_op jit(solution)/shard_map/ppermute | solution.py:244
  47.7 36.5 %copy-start.8 = (bf16[40,1024]{1,0:T(8,128)(2,1)}, bf16[40,1024]{1,0:T(8,128)(2,1)S(1)}, u32[]{:S(2)}) copy-start(bf16[40,1024]{1,0:T(8,128)(2,1)S(1)} %get-tuple-element.48.refs_0_) | copy-start | bytes 245764
  55.1 29.7 %collective-permute-start.5 = (bf16[40,1024]{1,0:T(8,128)(2,1)S(1)}, bf16[40,1024]{1,0:T(8,128)(2,1)S(1)}, u32[]{:S(2)}, u32[]{:S(2)}) collective-permute-start(bf16[40,1024]{1,0:T(8,128)(2,1)S(1)} %get-tuple-element.49), channel_id=1, source_target_pairs={{0,8},{8,0},{16,24},{24,16},{1,9},{9,1},{17,25},{25,17},{2,10},{10... | collective-permute-start | bytes 245768 | tf_op jit(solution)/shard_map/ppermute | solution.py:240
  77.7 8.6 %collective-permute-start.6 = (bf16[40,1024]{1,0:T(8,128)(2,1)S(1)}, bf16[40,1024]{1,0:T(8,128)(2,1)S(1)}, u32[]{:S(2)}, u32[]{:S(2)}) collective-permute-start(bf16[40,1024]{1,0:T(8,128)(2,1)S(1)} %get-tuple-element.50), channel_id=1, source_target_pairs={{0,16},{8,24},{16,0},{24,8},{1,17},{9,25},{17,1},{25,9},{2,18},{10... | collective-permute-start | bytes 245768 | tf_op jit(solution)/shard_map/ppermute | solution.py:240
  79.3 9.2 %collective-permute-start.7 = (bf16[40,1024]{1,0:T(8,128)(2,1)S(1)}, bf16[40,1024]{1,0:T(8,128)(2,1)S(1)}, u32[]{:S(2)}, u32[]{:S(2)}) collective-permute-start(bf16[40,1024]{1,0:T(8,128)(2,1)S(1)} %get-tuple-element.51), channel_id=1, source_target_pairs={{0,24},{8,16},{16,8},{24,0},{1,25},{9,17},{17,9},{25,1},{2,26},{10... | collective-permute-start | bytes 245768 | tf_op jit(solution)/shard_map/ppermute | solution.py:240
  85.5 10.3 %collective-permute-start.22 = (bf16[3,128,384]{2,1,0:T(8,128)(2,1)}, bf16[3,128,384]{2,1,0:T(8,128)(2,1)}, u32[]{:S(2)}, u32[]{:S(2)}) collective-permute-start(bf16[3,128,384]{2,1,0:T(8,128)(2,1)} %get-tuple-element.63), channel_id=1, source_target_pairs={{0,8},{8,0},{16,24},{24,16},{1,9},{9,1},{17,25},{25,17},{2,10},{10... | collective-permute-start | bytes 884744 | tf_op jit(solution)/shard_map/ppermute | solution.py:240
  87.0 13.8 %collective-permute-start.20 = (bf16[3,128,384]{2,1,0:T(8,128)(2,1)}, bf16[3,128,384]{2,1,0:T(8,128)(2,1)}, u32[]{:S(2)}, u32[]{:S(2)}) collective-permute-start(bf16[3,128,384]{2,1,0:T(8,128)(2,1)} %get-tuple-element.61), channel_id=1, source_target_pairs={{0,16},{8,24},{16,0},{24,8},{1,17},{9,25},{17,1},{25,9},{2,18},{10... | collective-permute-start | bytes 884744 | tf_op jit(solution)/shard_map/ppermute | solution.py:240
  89.1 14.6 %collective-permute-start.18 = (bf16[3,128,384]{2,1,0:T(8,128)(2,1)}, bf16[3,128,384]{2,1,0:T(8,128)(2,1)}, u32[]{:S(2)}, u32[]{:S(2)}) collective-permute-start(bf16[3,128,384]{2,1,0:T(8,128)(2,1)} %get-tuple-element.59), channel_id=1, source_target_pairs={{0,24},{8,16},{16,8},{24,0},{1,25},{9,17},{17,9},{25,1},{2,26},{10... | collective-permute-start | bytes 884744 | tf_op jit(solution)/shard_map/ppermute | solution.py:240
  (19 other events, 56.6 us)

commit v2 on v1

--- a/solution.py
+++ b/solution.py
@@ -16,6 +16,8 @@
 F32 = jnp.float32
 BF16 = jnp.bfloat16
 VMEM = pl.BlockSpec(memory_space=pltpu.VMEM)
+SMEM = pl.BlockSpec(memory_space=pltpu.SMEM)
+HBM = pl.BlockSpec(memory_space=pltpu.HBM)
 MIB = 1 << 20
 
 
@@ -57,30 +59,42 @@
     return jnp.concatenate(masks, axis=0).astype(BF16)
 
 
-def dispatch_kernel(experts, capacity, dp_count, ids_ref, in_ref, grad_ref, *out_refs):
+def dispatch_kernel(experts, capacity, dp_count, ids_any, in_any, grad_any, *refs):
+    outs, (ids_ref, held, sems) = refs[:experts], refs[experts:]
     me = lax.axis_index("expert")
     core = lax.axis_index("cuts")
-    half = out_refs[0].shape[2] // 2
-    cores = in_ref.shape[1] // (dp_count * half)
+    half = held.shape[3]
+    cores = in_any.shape[1] // (dp_count * half)
+    first = pltpu.make_async_copy(ids_any, ids_ref, sems.at[2 * dp_count])
+    first.start()
+    copies = []
+    for x, x_any in enumerate((in_any, grad_any)):
+        for q in range(dp_count):
+            columns = pl.ds(pl.multiple_of((q * cores + core) * half, half), half)
+            copies.append(
+                pltpu.make_async_copy(x_any.at[:, columns], held.at[x, q], sems.at[x * dp_count + q])
+            )
+            copies[-1].start()
+    first.wait()
     masks = slot_masks(ids_ref[...], me, experts, capacity)
-    for q in range(dp_count):
-        columns = pl.ds(pl.multiple_of((q * cores + core) * half, half), half)
-        for x_ref, start in ((in_ref, 0), (grad_ref, half)):
-            picked = jnp.dot(masks, x_ref[:, columns], preferred_element_type=F32)
+    for x in range(2):
+        for q in range(dp_count):
+            copies[x * dp_count + q].wait()
+            picked = jnp.dot(masks, held[x, q], preferred_element_type=F32)
             for k in range(experts):
-                out_refs[k][q, :, start : start + half] = picked[
+                outs[k][q, :, x * half : (x + 1) * half] = picked[
                     k * capacity : (k + 1) * capacity
                 ].astype(BF16)
 
 
 def collect_kernel(experts, dp_count, *refs):
     got, whole, parts = refs[:experts], refs[experts], refs[experts + 1 :]
-    me = lax.axis_index("dp")
+    part = lax.axis_index("dp")
     for q in range(dp_count):
         joined = jnp.concatenate([got[k][q].astype(F32) for k in range(experts)], axis=0)
         whole[q] = joined.astype(BF16)
-    for a in range(1, dp_count):
-        parts[a - 1][...] = whole[lax.rem(me + a, dp_count)]
+    for k in range(1, dp_count):
+        parts[k - 1][...] = whole[part ^ k]
 
 
 def expert_kernel(dp_count, mine_ref, other_ref, gate_up_ref, down_ref, out_ref):
@@ -121,9 +135,12 @@
         out_ref[...] = total[k * capacity : (k + 1) * capacity].astype(BF16)
 
 
-def combine_kernel(experts, capacity, ids_ref, *refs):
-    got, out_ref = refs[:experts], refs[experts]
+def combine_kernel(experts, capacity, ids_any, *refs):
+    got, (out_ref, ids_ref, sem) = refs[:experts], refs[experts:]
     me = lax.axis_index("expert")
+    copy = pltpu.make_async_copy(ids_any, ids_ref, sem)
+    copy.start()
+    copy.wait()
     masks = slot_masks(ids_ref[...], me, experts, capacity)
     joined = jnp.concatenate([got[k][...].astype(F32) for k in range(experts)], axis=0)
     out_ref[...] = lax.dot_general(
@@ -131,52 +148,70 @@
     ).astype(BF16)
 
 
-def arrange_kernel(experts, owner_ref, master_ref, first_ref, second_ref, *out_refs):
+def slice_for(owner_ref, me, target, experts):
+    j = 0
+    for i in range(experts):
+        j = jnp.where(owner_ref[me, i] == target, i, j)
+    return j
+
+
+def arrange_kernel(experts, groups, owner_ref, master_any, first_any, second_any, *refs):
+    outs, (held, sems) = refs[: len(groups)], refs[len(groups) :]
     me = lax.axis_index("expert")
-    height = out_refs[0].shape[1]
-    for k in range(experts):
-        j = 0
-        for i in range(experts):
-            j = jnp.where(owner_ref[me, i] == (me ^ k), i, j)
+    height = held.shape[2]
+    stored = (master_any, first_any, second_any)
+    masters, others = [], []
+    for g, (k, parts) in enumerate(groups):
+        j = slice_for(owner_ref, me, me ^ k, experts)
         rows = pl.ds(pl.multiple_of(j * height, height), height)
+        for n, i in enumerate(parts):
+            target = held.at[k] if i == 0 else outs[g].at[pl.ds(3 * n, 3)]
+            copy = pltpu.make_async_copy(stored[i].at[:, rows, :], target, sems.at[k, i])
+            copy.start()
+            if i == 0:
+                masters.append((copy, k, g, n))
+            else:
+                others.append(copy)
+    for copy, k, g, n in masters:
+        copy.wait()
         for m in range(3):
-            out_refs[k][m] = master_ref[m, rows, :].astype(BF16)
-            out_refs[k][3 + m] = first_ref[m, rows, :]
-            out_refs[k][6 + m] = second_ref[m, rows, :]
+            outs[g][3 * n + m] = held[k, m].astype(BF16)
+    for copy in others:
+        copy.wait()
 
 
 def weight_kernel(experts, dp_count, owner_ref, *refs):
     mine, other = refs[:dp_count], refs[dp_count : 2 * dp_count]
     hidden = refs[2 * dp_count : 3 * dp_count]
     outs = refs[3 * dp_count : 3 * dp_count + experts]
-    held = refs[3 * dp_count + experts]
+    rows_ref, hidden_ref, held = refs[3 * dp_count + experts :]
     me = lax.axis_index("expert")
     core = lax.axis_index("cuts")
     part = lax.axis_index("dp")
     height = outs[0].shape[1]
     units = outs[0].shape[2]
-    half = mine[1].shape[1] // 2
+    slots = hidden[0].shape[0]
+    half = mine[0].shape[2] // 2
     per_half = half // height
+    for k in range(dp_count):
+        hidden_ref[k * slots : (k + 1) * slots] = hidden[k][...]
     for source, side in ((mine, core), (other, 1 - core)):
-        pair = jnp.zeros((half, 2 * units), F32)
-        down = jnp.zeros((half, units), F32)
-        for a in range(dp_count):
-            rows = source[0][part] if a == 0 else source[a][...]
-            pair += lax.dot_general(
-                rows[:, :half], hidden[a][:, : 2 * units], (((0,), (0,)), ((), ())),
+        rows_ref[:slots] = source[0][part]
+        for a in range(1, dp_count):
+            rows_ref[a * slots : (a + 1) * slots] = source[a][...]
+        sums = [
+            lax.dot_general(
+                rows_ref[:, at : at + half], hidden_ref[:, low:high], (((0,), (0,)), ((), ())),
                 preferred_element_type=F32,
             )
-            down += lax.dot_general(
-                rows[:, half:], hidden[a][:, 2 * units :], (((0,), (0,)), ((), ())),
-                preferred_element_type=F32,
+            * (1.0 / dp_count)
+            for at, low, high in (
+                (0, 0, units), (0, units, 2 * units), (half, 2 * units, 3 * units),
             )
-        pair = pair * (1.0 / dp_count)
-        down = down * (1.0 / dp_count)
+        ]
         for i in range(per_half):
-            rows = slice(i * height, (i + 1) * height)
-            held[0] = pair[rows, :units].astype(BF16)
-            held[1] = pair[rows, units:].astype(BF16)
-            held[2] = down[rows].astype(BF16)
+            for m in range(3):
+                held[m] = sums[m][i * height : (i + 1) * height].astype(BF16)
             k_of = owner_ref[me, side * per_half + i] ^ me
             for k in range(experts):
 
@@ -185,18 +220,28 @@
                     outs[k][...] = held[...]
 
 
-def adam_kernel(source_ref, state_master, state_first, state_second, grad_ref, *refs):
-    out_master, out_first, out_second = refs[-3:]
-    master, first, second = adam_update(
-        state_master[0].astype(F32), state_first[0], state_second[0], grad_ref[0].astype(F32)
-    )
-    out_master[0, 0] = master
-    out_first[0, 0] = first.astype(BF16)
-    out_second[0, 0] = second.astype(BF16)
-
-
-def call(kernel, out_shape, n_in, smem=(), scratch=(), limit=40, flops=0, moved=0):
-    specs = [pl.BlockSpec(memory_space=pltpu.SMEM) if i in smem else VMEM for i in range(n_in)]
+def adam_kernel(k, places, grad_ref, *refs):
+    outs, held, sems = refs[-7:-4], refs[-4:-1], refs[-1]
+    block = lax.axis_index("expert") ^ k
+    copies = []
+    for m in range(3):
+        master, first, second = [refs[ref][3 * n + m] for ref, n in places]
+        values = adam_update(master.astype(F32), first, second, grad_ref[m].astype(F32))
+        for i in range(3):
+            held[i][m] = values[i].astype(held[i].dtype)
+            copies.append(
+                pltpu.make_async_copy(held[i].at[m], outs[i].at[block, m], sems.at[m, i])
+            )
+            copies[-1].start()
+    for copy in copies:
+        copy.wait()
+
+
+def call(kernel, out_shape, n_in, smem=(), held=(), scratch=(), limit=16, flops=0, moved=0):
+    specs = [
+        SMEM if i in smem else HBM if i in held else VMEM
+        for i in range(n_in)
+    ]
     return pl.pallas_call(
         kernel,
         out_shape=out_shape,
@@ -212,36 +257,28 @@
     return jax.ShapeDtypeStruct(dims, dtype)
 
 
-def adam_step(state, grad, source, buffers, experts):
+def adam_step(states, places, grad, k, buffers, experts):
     parts, height, units = grad.shape
-    block = lambda at: pl.BlockSpec((1, height, units), lambda m, s, at=at: (at + m, 0, 0))
-    out_block = pl.BlockSpec((1, 1, height, units), lambda m, s: (s[0], m, 0, 0))
-    out_shape = [shape(experts, parts, height, units, dtype=t) for t in (F32, BF16, BF16)]
-    held = [pl.BlockSpec(memory_space=pl.ANY)] * len(buffers)
+    types = (F32, BF16, BF16)
     return pl.pallas_call(
-        adam_kernel,
-        grid_spec=pltpu.PrefetchScalarGridSpec(
-            num_scalar_prefetch=1,
-            grid=(parts,),
-            in_specs=[block(0), block(parts), block(2 * parts), block(0)] + held,
-            out_specs=[out_block] * 3,
-        ),
-        out_shape=out_shape,
-        input_output_aliases={5 + i: i for i in range(len(buffers))},
+        functools.partial(adam_kernel, k, places),
+        out_shape=[shape(experts, parts, height, units, dtype=t) for t in types],
+        in_specs=[VMEM] * (1 + len(states)) + [HBM] * len(buffers),
+        out_specs=[HBM] * 3,
+        scratch_shapes=[pltpu.VMEM((parts, height, units), t) for t in types]
+        + [pltpu.SemaphoreType.DMA((parts, 3))],
+        input_output_aliases={1 + len(states) + i: i for i in range(len(buffers))},
         compiler_params=pltpu.CompilerParams(vmem_limit_bytes=16 * MIB),
         cost_estimate=pl.CostEstimate(
-            flops=20 * parts * height * units, bytes_accessed=16 * parts * height * units,
+            flops=20 * parts * height * units,
+            bytes_accessed=16 * parts * height * units,
             transcendentals=2 * parts * height * units,
         ),
-    )(source, state, state, state, grad, *buffers)
+    )(grad, *states, *buffers)
 
 
 def exchange(tensor, axis, k, count):
     return lax.ppermute(tensor, axis, [(i, i ^ k) for i in range(count)])
-
-
-def rotate(tensor, axis, a, count):
-    return lax.ppermute(tensor, axis, [(i, (i + a) % count) for i in range(count)])
 
 
 def after(values, *others):
@@ -269,7 +306,6 @@
     half = shard_rows // cores
     height = shard_rows // experts
     units = master_weight.shape[3]
-    me = lax.axis_index("expert")
     ids = expert_ids.reshape(1, row_count)
     gate_up = gate_up_weight[0].reshape(model_width, 2 * units)
     down = down_weight[0]
@@ -278,23 +314,40 @@
         functools.partial(dispatch_kernel, experts, capacity, dp_count),
         [shape(dp_count, capacity, 2 * half)] * experts,
         3,
+        held=(0, 1, 2),
+        scratch=[
+            pltpu.VMEM((1, row_count), jnp.int32),
+            pltpu.VMEM((2, dp_count, row_count, half), BF16),
+            pltpu.SemaphoreType.DMA((2 * dp_count + 1,)),
+        ],
         flops=2 * slots * row_count * model_width,
-        moved=4 * row_count * model_width + 4 * slots * model_width,
+        moved=2 * row_count * model_width + 4 * slots * model_width,
     )(ids, activations, out_grad)
     got = [sent[0]] + [exchange(sent[k], "expert", k, experts) for k in range(1, experts)]
 
+    near = [k for k in range(1, experts) if k.bit_count() == 1]
+    far = [k for k in range(1, experts) if k.bit_count() > 1]
+    groups = [(k, (0, 1, 2)) for k in range(experts)]
+    stored = [t[0].transpose(1, 0, 2) for t in (master_weight, first_moment, second_moment)]
     states = call(
-        functools.partial(arrange_kernel, experts),
-        [shape(9, height, units)] * experts,
+        functools.partial(arrange_kernel, experts, groups),
+        [shape(3 * len(parts), height, units) for _, parts in groups],
         4,
         smem=(0,),
+        held=(1, 2, 3),
+        scratch=[
+            pltpu.VMEM((experts, 3, height, units), F32),
+            pltpu.SemaphoreType.DMA((experts, 3)),
+        ],
         moved=14 * shard_rows * 3 * units,
-    )(
-        new_owner,
-        master_weight[0].transpose(1, 0, 2),
-        first_moment[0].transpose(1, 0, 2),
-        second_moment[0].transpose(1, 0, 2),
-    )
+    )(new_owner, *stored)
+    got, states = lax.optimization_barrier((got, states))
+    states = dict(zip(groups, states))
+
+    def send_states(parts, ks, *others):
+        for k in ks:
+            states[k, parts] = exchange(after(states[k, parts], *others), "expert", k, experts)
+        return [states[k, parts] for k in ks]
 
     mine, *parts = call(
         functools.partial(collect_kernel, experts, dp_count),
@@ -303,11 +356,8 @@
         moved=12 * slots * model_width,
     )(*got)
     other = exchange(mine, "cuts", 1, cores)
-    part_mine = [mine] + [rotate(parts[a - 1], "dp", a, dp_count) for a in range(1, dp_count)]
-    states_sent = after(list(states[1:]), *got[1:])
-    moved_states = [states[0]] + [
-        exchange(states_sent[k - 1], "expert", k, experts) for k in range(1, experts)
-    ]
+    rows = {1: exchange(parts[0], "dp", 1, dp_count)}
+    sent_states = send_states((0, 1, 2), near)
 
     hidden = call(
         functools.partial(expert_kernel, dp_count),
@@ -316,8 +366,28 @@
         flops=6 * slots * model_width * units,
         moved=6 * model_width * units + 8 * slots * model_width,
     )(mine, other, gate_up, down)
-    hiddens = [hidden] + [rotate(hidden, "dp", a, dp_count) for a in range(1, dp_count)]
-    part_other = [other] + [exchange(part_mine[a], "cuts", 1, cores) for a in range(1, dp_count)]
+
+    hiddens = {0: hidden}
+    for bits in range(1, dp_count.bit_length()):
+        level = [k for k in range(dp_count - 1, 0, -1) if k.bit_count() == bits]
+        for k in level:
+            low = k & -k
+            block = hiddens[k ^ low]
+            if bits > 1:
+                block = after(block, tied)
+            elif k == 1:
+                block = after(block, rows[1])
+            hiddens[k] = exchange(block, "dp", low, dp_count)
+        if bits == 1:
+            send_states((0, 1, 2), far, hidden, sent_states)
+        else:
+            for k in range(2, dp_count):
+                if k not in rows:
+                    rows[k] = exchange(after(parts[k - 1], tied), "dp", k, dp_count)
+        tied = [hiddens[k] for k in level]
+    hiddens = [hiddens[k] for k in range(dp_count)]
+    rows_mine = [mine] + [rows[k] for k in range(1, dp_count)]
+    rows_other = [other] + [exchange(rows[k], "cuts", 1, cores) for k in range(1, dp_count)]
 
     keep, give = call(
         slot_grad_kernel,
@@ -338,6 +408,8 @@
         functools.partial(combine_kernel, experts, capacity),
         shape(row_count, model_width // cores),
         1 + experts,
+        held=(0,),
+        scratch=[pltpu.VMEM((1, row_count), jnp.int32), pltpu.SemaphoreType.DMA(())],
         flops=2 * slots * row_count * model_width // cores,
         moved=4 * slots * model_width // cores,
     )(ids, *returned)
@@ -347,16 +419,29 @@
         [shape(3, height, units)] * experts,
         1 + 3 * dp_count,
         smem=(0,),
-        scratch=[pltpu.VMEM((3, height, units), BF16)],
+        scratch=[
+            pltpu.VMEM((slots * dp_count, 2 * half), BF16),
+            pltpu.VMEM((slots * dp_count, 3 * units), BF16),
+            pltpu.VMEM((3, height, units), BF16),
+        ],
         flops=6 * slots * dp_count * shard_rows * units,
         moved=4 * slots * dp_count * (shard_rows + units),
-    )(new_owner, *part_mine, *part_other, *hiddens)
-    moved_grads = [grads[0]] + [exchange(grads[k], "expert", k, experts) for k in range(1, experts)]
+    )(new_owner, *rows_mine, *rows_other, *hiddens)
+    moved_grads = {0: grads[0]}
+    for k in near + far:
+        grad = after(grads[k], returned) if k in far else grads[k]
+        moved_grads[k] = exchange(grad, "expert", k, experts)
 
     buffers = ()
     for k in range(experts):
-        source = (me ^ k).astype(jnp.int32).reshape(1)
-        buffers = adam_step(moved_states[k], moved_grads[k], source, buffers, experts)
+        held = [group for group in groups if group[0] == k]
+        places = [
+            next((n, group[1].index(i)) for n, group in enumerate(held) if i in group[1])
+            for i in range(3)
+        ]
+        buffers = adam_step(
+            [states[group] for group in held], places, moved_grads[k], k, buffers, experts
+        )
     outs = [b.transpose(0, 2, 1, 3)[None] for b in buffers]
     return (input_grad, *outs)
 
@@ -459,6 +544,7 @@
     height = model_width // (dp_count * experts)
     whole_tiles = (
         experts & (experts - 1) == 0
+        and dp_count & (dp_count - 1) == 0
         and cores == 2
         and capacity % 8 == 0
         and (experts * capacity) % 16 == 0

time: 107 us -> 87.8 us (0.82)
  waiting for transfers between devices: 46.9 us -> 37.7 us
  Pallas kernels: 20.5 us -> 14.1 us
  starting transfers between devices: 28.4 us -> 25.8 us
    ppermute x6 -> x0, waiting for transfers between devices: 35.6 us -> none  [rotate(): lax.ppermute(tensor, axis, [(i, (i + a) % count) for i in range(count)])]
    ppermute x17 -> x23, waiting for transfers between devices: 11.3 us -> 37.7 us  [exchange(): return lax.ppermute(tensor, axis, [(i, i ^ k) for i in range(count)])]
    ppermute x6 -> x0, starting transfers between devices: 12.1 us -> none  [rotate(): lax.ppermute(tensor, axis, [(i, (i + a) % count) for i in range(count)])]
    ppermute x17 -> x23, starting transfers between devices: 16.3 us -> 25.8 us  [exchange(): return lax.ppermute(tensor, axis, [(i, i ^ k) for i in range(count)])]
    pallas_call x5, Pallas kernels: 12.9 us -> 6.59 us  [the longest x4 5.4 us: adam_step(): pl.pallas_call(functools.partial(adam_kernel, k, places), out_shape=[shap...]
    pallas_call x1, Pallas kernels: 3.7 us -> 2.33 us  [aligned_local(): call(functools.partial(weight_kernel, experts, dp_count), [shape(3, heigh...]
    pallas_call x1, Pallas kernels: 0.45 us -> 1.71 us  [aligned_local(): call(functools.partial(dispatch_kernel, experts, capacity, dp_count), [sh...]
    unnamed x41 -> x23, local copies, waits for them, and re-layouts: 10 us -> 9.02 us
  transfers between devices with their start and end apart: 23 -> 23, of which waited for: 9 -> 9; matrix products, arithmetic and copies ran while one was open for 1% -> 1% of each run, Pallas kernels for 16% -> 13%
where the time goes in v2:
time: 87.8 us; the launch traced here: 87.4 us
  waiting for transfers between devices  37.7 us (43%)
  starting transfers between devices  25.8 us (29%)
  Pallas kernels  14.1 us (16%)
  local copies, waits for them, and re-layouts  9.02 us (10%)
    ppermute x23, waiting for transfers between devices, exchange(): return lax.ppermute(tensor, axis, [(i, i ^ k) for i in range(count)])  37.7 us
    ppermute x23, starting transfers between devices, exchange(): return lax.ppermute(tensor, axis, [(i, i ^ k) for i in range(count)])  25.8 us
    unnamed x23, local copies, waits for them, and re-layouts  9.02 us
    pallas_call x4, Pallas kernels, adam_step(): pl.pallas_call(functools.partial(adam_kernel, k, places), out_shape=[shap...  5.4 us
    pallas_call x1, Pallas kernels, aligned_local(): call(functools.partial(weight_kernel, experts, dp_count), [shape(3, heigh...  2.33 us
  transfers between devices with their start and end apart: 23, of which 9 were waited for; matrix products, arithmetic and copies ran while one was open for 1% of the time, Pallas kernels for 13%

profile of v2, /device:TPU:0, one launch (start us, length us, event | category | flops | bytes accessed | tf_op | source)
XLA Modules:
  0.0 87.4 jit_solution(8039843897915305688)
XLA Ops:
  3.4 1.7 %shard_map.120 = (bf16[4,40,512]{2,1,0:T(8,128)(2,1)S(1)}, bf16[4,40,512]{2,1,0:T(8,128)(2,1)S(1)}, bf16[4,40,512]{2,1,0:T(8,128)(2,1)S(1)}, bf16[4,40,512]{2,1,0:T(8,128)(2,1)S(1)}) custom-call(s32[1,128]{1,0:T(1,128)S(1)} %bitcast.29, bf16[128,2048]{1,0:T(8,128)(2,1)S(1)} %copy-done.4, bf16[128,2048]{1,0:T(8,128)(2,1)S(1)} %copy-done.5), custom_call_target="tpu_custom_call" | custom-call | flops 83886080 | bytes 1835008 | tf_op jit(solution)/shard_map/pallas_call | solution.py:313
  5.1 3.0 %collective-permute-start = (bf16[4,40,512]{2,1,0:T(8,128)(2,1)S(1)}, bf16[4,40,512]{2,1,0:T(8,128)(2,1)S(1)}, u32[]{:S(2)}, u32[]{:S(2)}) collective-permute-start(bf16[4,40,512]{2,1,0:T(8,128)(2,1)S(1)} %get-tuple-element.53), channel_id=1, source_target_pairs={{0,8},{8,0},{16,24},{24,16},{1,9},{9,1},{17,25},{25,17},{2,10},{10... | collective-permute-start | bytes 491528 | tf_op jit(solution)/shard_map/ppermute | solution.py:281
  8.1 1.5 %collective-permute-start.1 = (bf16[4,40,512]{2,1,0:T(8,128)(2,1)S(1)}, bf16[4,40,512]{2,1,0:T(8,128)(2,1)S(1)}, u32[]{:S(2)}, u32[]{:S(2)}) collective-permute-start(bf16[4,40,512]{2,1,0:T(8,128)(2,1)S(1)} %get-tuple-element.54), channel_id=1, source_target_pairs={{0,16},{8,24},{16,0},{24,8},{1,17},{9,25},{17,1},{25,9},{2,18},{10... | collective-permute-start | bytes 491528 | tf_op jit(solution)/shard_map/ppermute | solution.py:281
  9.6 1.7 %copy-done = f32[1,512,3,384]{3,1,2,0:T(8,128)S(1)} copy-done((f32[1,512,3,384]{3,1,2,0:T(8,128)S(1)}, f32[1,512,3,384]{3,1,2,0:T(8,128)}, u32[]{:S(2)}) %copy-start) | copy-done | bytes 2359320
  15.7 1.5 %collective-permute-done.1.refs_2_ = bf16[4,40,512]{2,1,0:T(8,128)(2,1)S(1)} collective-permute-done((bf16[4,40,512]{2,1,0:T(8,128)(2,1)S(1)}, bf16[4,40,512]{2,1,0:T(8,128)(2,1)S(1)}, u32[]{:S(2)}, u32[]{:S(2)}) %collective-permute-start.1) | collective-permute-done | bytes 163872 | tf_op jit(solution)/shard_map/ppermute | solution.py:281
  19.5 1.6 %collective-permute-start.8 = (bf16[160,512]{1,0:T(8,128)(2,1)S(1)}, bf16[160,512]{1,0:T(8,128)(2,1)S(1)}, u32[]{:S(2)}, u32[]{:S(2)}) collective-permute-start(bf16[160,512]{1,0:T(8,128)(2,1)S(1)} %get-tuple-element.71), channel_id=1, source_target_pairs={{0,1},{1,0},{2,3},{3,2},{4,5},{5,4},{6,7},{7,6},{8,9},{9,8},{10,11... | collective-permute-start | bytes 491528 | tf_op jit(solution)/shard_map/ppermute | solution.py:281
  23.6 1.9 %collective-permute-done.8.refs_1_ = bf16[160,512]{1,0:T(8,128)(2,1)S(1)} collective-permute-done((bf16[160,512]{1,0:T(8,128)(2,1)S(1)}, bf16[160,512]{1,0:T(8,128)(2,1)S(1)}, u32[]{:S(2)}, u32[]{:S(2)}) %collective-permute-start.8) | collective-permute-done | bytes 163872 | tf_op jit(solution)/shard_map/ppermute | solution.py:281
  25.5 1.6 %collective-permute-start.10 = (bf16[160,1152]{1,0:T(8,128)(2,1)S(1)}, bf16[160,1152]{1,0:T(8,128)(2,1)S(1)}, u32[]{:S(2)}, u32[]{:S(2)}) collective-permute-start(bf16[160,1152]{1,0:T(8,128)(2,1)S(1)} %shard_map.123.pair_ref.refs_8_), channel_id=1, source_target_pairs={{0,1},{1,0},{2,3},{3,2},{4,5},{5,4},{6,7},{7,6},{8,9},{9,8},{10,11... | collective-permute-start | bytes 1105928 | tf_op jit(solution)/shard_map/ppermute | solution.py:281
  27.1 2.6 %collective-permute-start.9 = (bf16[160,1152]{1,0:T(8,128)(2,1)S(1)}, bf16[160,1152]{1,0:T(8,128)(2,1)S(1)}, u32[]{:S(2)}, u32[]{:S(2)}) collective-permute-start(bf16[160,1152]{1,0:T(8,128)(2,1)S(1)} %shard_map.123.pair_ref.refs_8_), channel_id=1, source_target_pairs={{0,2},{1,3},{2,0},{3,1},{4,6},{5,7},{6,4},{7,5},{8,10},{9,11},{10,... | collective-permute-start | bytes 1105928 | tf_op jit(solution)/shard_map/ppermute | solution.py:281
  29.7 9.8 %collective-permute-done.18.refs_0_ = bf16[9,128,384]{2,1,0:T(8,128)(2,1)S(1)} collective-permute-done((bf16[9,128,384]{2,1,0:T(8,128)(2,1)S(1)}, bf16[9,128,384]{2,1,0:T(8,128)(2,1)S(1)}, u32[]{:S(2)}, u32[]{:S(2)}) %collective-permute-start.18) | collective-permute-done | bytes 884768 | tf_op jit(solution)/shard_map/ppermute | solution.py:281
  40.4 1.8 %collective-permute-start.20 = (bf16[9,128,384]{2,1,0:T(8,128)(2,1)S(1)}, bf16[9,128,384]{2,1,0:T(8,128)(2,1)S(1)}, u32[]{:S(2)}, u32[]{:S(2)}) collective-permute-start(bf16[9,128,384]{2,1,0:T(8,128)(2,1)S(1)} %get-tuple-element.83), channel_id=1, source_target_pairs={{0,24},{8,16},{16,8},{24,0},{1,25},{9,17},{17,9},{25,1},{2,26},{10... | collective-permute-start | bytes 2654216 | tf_op jit(solution)/shard_map/ppermute | solution.py:281
  43.5 1.7 %collective-permute-done.9.refs_10_ = bf16[160,1152]{1,0:T(8,128)(2,1)S(1)} collective-permute-done((bf16[160,1152]{1,0:T(8,128)(2,1)S(1)}, bf16[160,1152]{1,0:T(8,128)(2,1)S(1)}, u32[]{:S(2)}, u32[]{:S(2)}) %collective-permute-start.9) | collective-permute-done | bytes 368672 | tf_op jit(solution)/shard_map/ppermute | solution.py:281
  45.6 2.6 %collective-permute-start.11 = (bf16[160,512]{1,0:T(8,128)(2,1)S(1)}, bf16[160,512]{1,0:T(8,128)(2,1)S(1)}, u32[]{:S(2)}, u32[]{:S(2)}) collective-permute-start(bf16[160,512]{1,0:T(8,128)(2,1)S(1)} %get-tuple-element.74), channel_id=1, source_target_pairs={{0,2},{1,3},{2,0},{3,1},{4,6},{5,7},{6,4},{7,5},{8,10},{9,11},{10,... | collective-permute-start | bytes 491528 | tf_op jit(solution)/shard_map/ppermute | solution.py:281
  48.2 1.3 %collective-permute-start.12 = (bf16[160,512]{1,0:T(8,128)(2,1)S(1)}, bf16[160,512]{1,0:T(8,128)(2,1)S(1)}, u32[]{:S(2)}, u32[]{:S(2)}) collective-permute-start(bf16[160,512]{1,0:T(8,128)(2,1)S(1)} %get-tuple-element.76), channel_id=1, source_target_pairs={{0,3},{1,2},{2,1},{3,0},{4,7},{5,6},{6,5},{7,4},{8,11},{9,10},{10,... | collective-permute-start | bytes 491528 | tf_op jit(solution)/shard_map/ppermute | solution.py:281
  49.6 8.6 %collective-permute-done.11.refs_2_ = bf16[160,512]{1,0:T(8,128)(2,1)S(1)} collective-permute-done((bf16[160,512]{1,0:T(8,128)(2,1)S(1)}, bf16[160,512]{1,0:T(8,128)(2,1)S(1)}, u32[]{:S(2)}, u32[]{:S(2)}) %collective-permute-start.11) | collective-permute-done | bytes 163872 | tf_op jit(solution)/shard_map/ppermute | solution.py:281
  58.2 5.3 %collective-permute-done.12.refs_3_ = bf16[160,512]{1,0:T(8,128)(2,1)S(1)} collective-permute-done((bf16[160,512]{1,0:T(8,128)(2,1)S(1)}, bf16[160,512]{1,0:T(8,128)(2,1)S(1)}, u32[]{:S(2)}, u32[]{:S(2)}) %collective-permute-start.12) | collective-permute-done | bytes 163872 | tf_op jit(solution)/shard_map/ppermute | solution.py:281
  65.4 1.7 %collective-permute-start.7 = (bf16[40,1024]{1,0:T(8,128)(2,1)S(1)}, bf16[40,1024]{1,0:T(8,128)(2,1)S(1)}, u32[]{:S(2)}, u32[]{:S(2)}) collective-permute-start(bf16[40,1024]{1,0:T(8,128)(2,1)S(1)} %get-tuple-element.70), channel_id=1, source_target_pairs={{0,24},{8,16},{16,8},{24,0},{1,25},{9,17},{17,9},{25,1},{2,26},{10... | collective-permute-start | bytes 245768 | tf_op jit(solution)/shard_map/ppermute | solution.py:281
  67.2 2.3 %shard_map.127 = (bf16[3,128,384]{2,1,0:T(8,128)(2,1)S(1)}, bf16[3,128,384]{2,1,0:T(8,128)(2,1)S(1)}, bf16[3,128,384]{2,1,0:T(8,128)(2,1)S(1)}, bf16[3,128,384]{2,1,0:T(8,128)(2,1)S(1)}) custom-call(s32[4,4]{1,0:T(4,128)S(1)} %copy-done.7, bf16[4,160,512]{2,1,0:T(8,128)(2,1)S(1)} %get-tuple-element.64.mine_ref.refs_0_, ...), custom_call_target="tpu_custom_call" | custom-call | flops 754974720 | bytes 2293760 | tf_op jit(solution)/shard_map/pallas_call | solution.py:417
  71.3 1.7 %collective-permute-start.17 = (bf16[3,128,384]{2,1,0:T(8,128)(2,1)S(1)}, bf16[3,128,384]{2,1,0:T(8,128)(2,1)S(1)}, u32[]{:S(2)}, u32[]{:S(2)}) collective-permute-start(bf16[3,128,384]{2,1,0:T(8,128)(2,1)S(1)} %get-tuple-element.79), channel_id=1, source_target_pairs={{0,24},{8,16},{16,8},{24,0},{1,25},{9,17},{17,9},{25,1},{2,26},{10... | collective-permute-start | bytes 884744 | tf_op jit(solution)/shard_map/ppermute | solution.py:281
  74.2 1.4 %shard_map.128 = (f32[4,3,128,384]{3,2,1,0:T(8,128)}, bf16[4,3,128,384]{3,2,1,0:T(8,128)(2,1)}, bf16[4,3,128,384]{3,2,1,0:T(8,128)(2,1)}) custom-call(bf16[3,128,384]{2,1,0:T(8,128)(2,1)S(1)} %get-tuple-element.86.grad_ref, bf16[9,128,384]{2,1,0:T(8,128)(2,1)S(1)} %get-tuple-element.87.refs_0_), custom_call_target="tpu_custom_call" | custom-call | flops 2949120 | bytes 2359296 | tf_op jit(solution)/shard_map/pallas_call | solution.py:263
  75.6 3.9 %collective-permute-done.22.grad_ref = bf16[3,128,384]{2,1,0:T(8,128)(2,1)S(1)} collective-permute-done((bf16[3,128,384]{2,1,0:T(8,128)(2,1)S(1)}, bf16[3,128,384]{2,1,0:T(8,128)(2,1)S(1)}, u32[]{:S(2)}, u32[]{:S(2)}) %collective-permute-start.22) | collective-permute-done | bytes 294944 | tf_op jit(solution)/shard_map/ppermute | solution.py:281
  79.5 1.3 %shard_map.129 = (f32[4,3,128,384]{3,2,1,0:T(8,128)}, bf16[4,3,128,384]{3,2,1,0:T(8,128)(2,1)}, bf16[4,3,128,384]{3,2,1,0:T(8,128)(2,1)}) custom-call(bf16[3,128,384]{2,1,0:T(8,128)(2,1)S(1)} %collective-permute-done.22.grad_ref, ...), custom_call_target="tpu_custom_call", output_to_operand_aliasing={{0}: (2, {}), {1}: (3, {}), {2}: (4, {})} | custom-call | flops 2949120 | bytes 2359296 | tf_op jit(solution)/shard_map/pallas_call | solution.py:263
  80.8 3.9 %collective-permute-done.21.grad_ref = bf16[3,128,384]{2,1,0:T(8,128)(2,1)S(1)} collective-permute-done((bf16[3,128,384]{2,1,0:T(8,128)(2,1)S(1)}, bf16[3,128,384]{2,1,0:T(8,128)(2,1)S(1)}, u32[]{:S(2)}, u32[]{:S(2)}) %collective-permute-start.21) | collective-permute-done | bytes 294944 | tf_op jit(solution)/shard_map/ppermute | solution.py:281
  86.1 1.4 %shard_map.131 = (f32[4,3,128,384]{3,2,1,0:T(8,128)}, bf16[4,3,128,384]{3,2,1,0:T(8,128)(2,1)}, bf16[4,3,128,384]{3,2,1,0:T(8,128)(2,1)}) custom-call(bf16[3,128,384]{2,1,0:T(8,128)(2,1)S(1)} %collective-permute-done.17.grad_ref, ...), custom_call_target="tpu_custom_call", output_to_operand_aliasing={{0}: (2, {}), {1}: (3, {}), {2}: (4, {})} | custom-call | flops 2949120 | bytes 2359296 | tf_op jit(solution)/shard_map/pallas_call | solution.py:263
  (57 shorter events, 20.8 us)
Async XLA Ops:
  5.1 10.6 %collective-permute-start = (bf16[4,40,512]{2,1,0:T(8,128)(2,1)S(1)}, bf16[4,40,512]{2,1,0:T(8,128)(2,1)S(1)}, u32[]{:S(2)}, u32[]{:S(2)}) collective-permute-start(bf16[4,40,512]{2,1,0:T(8,128)(2,1)S(1)} %get-tuple-element.53), channel_id=1, source_target_pairs={{0,8},{8,0},{16,24},{24,16},{1,9},{9,1},{17,25},{25,17},{2,10},{10... | collective-permute-start | bytes 491528 | tf_op jit(solution)/shard_map/ppermute | solution.py:281
  8.1 9.2 %collective-permute-start.1 = (bf16[4,40,512]{2,1,0:T(8,128)(2,1)S(1)}, bf16[4,40,512]{2,1,0:T(8,128)(2,1)S(1)}, u32[]{:S(2)}, u32[]{:S(2)}) collective-permute-start(bf16[4,40,512]{2,1,0:T(8,128)(2,1)S(1)} %get-tuple-element.54), channel_id=1, source_target_pairs={{0,16},{8,24},{16,0},{24,8},{1,17},{9,25},{17,1},{25,9},{2,18},{10... | collective-permute-start | bytes 491528 | tf_op jit(solution)/shard_map/ppermute | solution.py:281
  9.6 7.7 %collective-permute-start.2 = (bf16[4,40,512]{2,1,0:T(8,128)(2,1)S(1)}, bf16[4,40,512]{2,1,0:T(8,128)(2,1)S(1)}, u32[]{:S(2)}, u32[]{:S(2)}) collective-permute-start(bf16[4,40,512]{2,1,0:T(8,128)(2,1)S(1)} %get-tuple-element.55), channel_id=1, source_target_pairs={{0,24},{8,16},{16,8},{24,0},{1,25},{9,17},{17,9},{25,1},{2,26},{10... | collective-permute-start | bytes 491528 | tf_op jit(solution)/shard_map/ppermute | solution.py:281
  17.3 4.4 %collective-permute-start.3 = (bf16[4,160,512]{2,1,0:T(8,128)(2,1)S(1)}, bf16[4,160,512]{2,1,0:T(8,128)(2,1)S(1)}, u32[]{:S(2)}, u32[]{:S(2)}) collective-permute-start(bf16[4,160,512]{2,1,0:T(8,128)(2,1)S(1)} %get-tuple-element.64.mine_ref.refs_0_), channel_id=1, source_target_pairs={{0,4},{4,0},{1,5},{5,1},{2,6},{6,2},{3,7},{7,3},{8,12},{12,8},{9,1... | collective-permute-start | bytes 1966088 | tf_op jit(solution)/shard_map/ppermute | solution.py:281
  17.4 22.1 %collective-permute-start.18 = (bf16[9,128,384]{2,1,0:T(8,128)(2,1)S(1)}, bf16[9,128,384]{2,1,0:T(8,128)(2,1)S(1)}, u32[]{:S(2)}, u32[]{:S(2)}) collective-permute-start(bf16[9,128,384]{2,1,0:T(8,128)(2,1)S(1)} %get-tuple-element.81), channel_id=1, source_target_pairs={{0,8},{8,0},{16,24},{24,16},{1,9},{9,1},{17,25},{25,17},{2,10},{10... | collective-permute-start | bytes 2654216 | tf_op jit(solution)/shard_map/ppermute | solution.py:281
  18.7 21.7 %collective-permute-start.19 = (bf16[9,128,384]{2,1,0:T(8,128)(2,1)S(1)}, bf16[9,128,384]{2,1,0:T(8,128)(2,1)S(1)}, u32[]{:S(2)}, u32[]{:S(2)}) collective-permute-start(bf16[9,128,384]{2,1,0:T(8,128)(2,1)S(1)} %get-tuple-element.82), channel_id=1, source_target_pairs={{0,16},{8,24},{16,0},{24,8},{1,17},{9,25},{17,1},{25,9},{2,18},{10... | collective-permute-start | bytes 2654216 | tf_op jit(solution)/shard_map/ppermute | solution.py:281
  19.5 6.0 %collective-permute-start.8 = (bf16[160,512]{1,0:T(8,128)(2,1)S(1)}, bf16[160,512]{1,0:T(8,128)(2,1)S(1)}, u32[]{:S(2)}, u32[]{:S(2)}) collective-permute-start(bf16[160,512]{1,0:T(8,128)(2,1)S(1)} %get-tuple-element.71), channel_id=1, source_target_pairs={{0,1},{1,0},{2,3},{3,2},{4,5},{5,4},{6,7},{7,6},{8,9},{9,8},{10,11... | collective-permute-start | bytes 491528 | tf_op jit(solution)/shard_map/ppermute | solution.py:281
  23.6 43.6 %copy-start.7 = (s32[4,4]{1,0:T(4,128)S(1)}, s32[4,4]{1,0:T(4,128)}, u32[]{:S(2)}) copy-start(s32[4,4]{1,0:T(4,128)} %owner_ref.3) | copy-start | bytes 196
  25.5 17.9 %collective-permute-start.10 = (bf16[160,1152]{1,0:T(8,128)(2,1)S(1)}, bf16[160,1152]{1,0:T(8,128)(2,1)S(1)}, u32[]{:S(2)}, u32[]{:S(2)}) collective-permute-start(bf16[160,1152]{1,0:T(8,128)(2,1)S(1)} %shard_map.123.pair_ref.refs_8_), channel_id=1, source_target_pairs={{0,1},{1,0},{2,3},{3,2},{4,5},{5,4},{6,7},{7,6},{8,9},{9,8},{10,11... | collective-permute-start | bytes 1105928 | tf_op jit(solution)/shard_map/ppermute | solution.py:281
  27.1 18.1 %collective-permute-start.9 = (bf16[160,1152]{1,0:T(8,128)(2,1)S(1)}, bf16[160,1152]{1,0:T(8,128)(2,1)S(1)}, u32[]{:S(2)}, u32[]{:S(2)}) collective-permute-start(bf16[160,1152]{1,0:T(8,128)(2,1)S(1)} %shard_map.123.pair_ref.refs_8_), channel_id=1, source_target_pairs={{0,2},{1,3},{2,0},{3,1},{4,6},{5,7},{6,4},{7,5},{8,10},{9,11},{10,... | collective-permute-start | bytes 1105928 | tf_op jit(solution)/shard_map/ppermute | solution.py:281
  40.4 45.6 %collective-permute-start.20 = (bf16[9,128,384]{2,1,0:T(8,128)(2,1)S(1)}, bf16[9,128,384]{2,1,0:T(8,128)(2,1)S(1)}, u32[]{:S(2)}, u32[]{:S(2)}) collective-permute-start(bf16[9,128,384]{2,1,0:T(8,128)(2,1)S(1)} %get-tuple-element.83), channel_id=1, source_target_pairs={{0,24},{8,16},{16,8},{24,0},{1,25},{9,17},{17,9},{25,1},{2,26},{10... | collective-permute-start | bytes 2654216 | tf_op jit(solution)/shard_map/ppermute | solution.py:281
  43.4 6.2 %collective-permute-start.4 = (bf16[160,1024]{1,0:T(8,128)(2,1)S(1)}, bf16[160,1024]{1,0:T(8,128)(2,1)S(1)}, u32[]{:S(2)}, u32[]{:S(2)}) collective-permute-start(bf16[160,1024]{1,0:T(8,128)(2,1)S(1)} %get-tuple-element.66), channel_id=1, source_target_pairs={{0,4},{4,0},{1,5},{5,1},{2,6},{6,2},{3,7},{7,3},{8,12},{12,8},{9,1... | collective-permute-start | bytes 983048 | tf_op jit(solution)/shard_map/ppermute | solution.py:281
  45.2 22.0 %collective-permute-start.16 = (bf16[160,1152]{1,0:T(8,128)(2,1)S(1)}, bf16[160,1152]{1,0:T(8,128)(2,1)S(1)}, u32[]{:S(2)}, u32[]{:S(2)}) collective-permute-start(bf16[160,1152]{1,0:T(8,128)(2,1)S(1)} %collective-permute-done.9.refs_10_), channel_id=1, source_target_pairs={{0,1},{1,0},{2,3},{3,2},{4,5},{5,4},{6,7},{7,6},{8,9},{9,8},{10,11... | collective-permute-start | bytes 1105928 | tf_op jit(solution)/shard_map/ppermute | solution.py:281
  45.6 12.6 %collective-permute-start.11 = (bf16[160,512]{1,0:T(8,128)(2,1)S(1)}, bf16[160,512]{1,0:T(8,128)(2,1)S(1)}, u32[]{:S(2)}, u32[]{:S(2)}) collective-permute-start(bf16[160,512]{1,0:T(8,128)(2,1)S(1)} %get-tuple-element.74), channel_id=1, source_target_pairs={{0,2},{1,3},{2,0},{3,1},{4,6},{5,7},{6,4},{7,5},{8,10},{9,11},{10,... | collective-permute-start | bytes 491528 | tf_op jit(solution)/shard_map/ppermute | solution.py:281
  48.2 15.3 %collective-permute-start.12 = (bf16[160,512]{1,0:T(8,128)(2,1)S(1)}, bf16[160,512]{1,0:T(8,128)(2,1)S(1)}, u32[]{:S(2)}, u32[]{:S(2)}) collective-permute-start(bf16[160,512]{1,0:T(8,128)(2,1)S(1)} %get-tuple-element.76), channel_id=1, source_target_pairs={{0,3},{1,2},{2,1},{3,0},{4,7},{5,6},{6,5},{7,4},{8,11},{9,10},{10,... | collective-permute-start | bytes 491528 | tf_op jit(solution)/shard_map/ppermute | solution.py:281
  49.6 14.0 %collective-permute-start.13 = (bf16[160,512]{1,0:T(8,128)(2,1)S(1)}, bf16[160,512]{1,0:T(8,128)(2,1)S(1)}, u32[]{:S(2)}, u32[]{:S(2)}) collective-permute-start(bf16[160,512]{1,0:T(8,128)(2,1)S(1)} %collective-permute-done.8.refs_1_), channel_id=1, source_target_pairs={{0,4},{4,0},{1,5},{5,1},{2,6},{6,2},{3,7},{7,3},{8,12},{12,8},{9,1... | collective-permute-start | bytes 491528 | tf_op jit(solution)/shard_map/ppermute | solution.py:281
  58.2 6.0 %collective-permute-start.14 = (bf16[160,512]{1,0:T(8,128)(2,1)S(1)}, bf16[160,512]{1,0:T(8,128)(2,1)S(1)}, u32[]{:S(2)}, u32[]{:S(2)}) collective-permute-start(bf16[160,512]{1,0:T(8,128)(2,1)S(1)} %collective-permute-done.11.refs_2_), channel_id=1, source_target_pairs={{0,4},{4,0},{1,5},{5,1},{2,6},{6,2},{3,7},{7,3},{8,12},{12,8},{9,1... | collective-permute-start | bytes 491528 | tf_op jit(solution)/shard_map/ppermute | solution.py:281
  63.5 1.9 %collective-permute-start.15 = (bf16[160,512]{1,0:T(8,128)(2,1)S(1)}, bf16[160,512]{1,0:T(8,128)(2,1)S(1)}, u32[]{:S(2)}, u32[]{:S(2)}) collective-permute-start(bf16[160,512]{1,0:T(8,128)(2,1)S(1)} %collective-permute-done.12.refs_3_), channel_id=1, source_target_pairs={{0,4},{4,0},{1,5},{5,1},{2,6},{6,2},{3,7},{7,3},{8,12},{12,8},{9,1... | collective-permute-start | bytes 491528 | tf_op jit(solution)/shard_map/ppermute | solution.py:281
  63.6 6.5 %collective-permute-start.5 = (bf16[40,1024]{1,0:T(8,128)(2,1)S(1)}, bf16[40,1024]{1,0:T(8,128)(2,1)S(1)}, u32[]{:S(2)}, u32[]{:S(2)}) collective-permute-start(bf16[40,1024]{1,0:T(8,128)(2,1)S(1)} %get-tuple-element.68), channel_id=1, source_target_pairs={{0,8},{8,0},{16,24},{24,16},{1,9},{9,1},{17,25},{25,17},{2,10},{10... | collective-permute-start | bytes 245768 | tf_op jit(solution)/shard_map/ppermute | solution.py:281
  64.2 7.2 %collective-permute-start.6 = (bf16[40,1024]{1,0:T(8,128)(2,1)S(1)}, bf16[40,1024]{1,0:T(8,128)(2,1)S(1)}, u32[]{:S(2)}, u32[]{:S(2)}) collective-permute-start(bf16[40,1024]{1,0:T(8,128)(2,1)S(1)} %get-tuple-element.69), channel_id=1, source_target_pairs={{0,16},{8,24},{16,0},{24,8},{1,17},{9,25},{17,1},{25,9},{2,18},{10... | collective-permute-start | bytes 245768 | tf_op jit(solution)/shard_map/ppermute | solution.py:281
  65.4 5.9 %collective-permute-start.7 = (bf16[40,1024]{1,0:T(8,128)(2,1)S(1)}, bf16[40,1024]{1,0:T(8,128)(2,1)S(1)}, u32[]{:S(2)}, u32[]{:S(2)}) collective-permute-start(bf16[40,1024]{1,0:T(8,128)(2,1)S(1)} %get-tuple-element.70), channel_id=1, source_target_pairs={{0,24},{8,16},{16,8},{24,0},{1,25},{9,17},{17,9},{25,1},{2,26},{10... | collective-permute-start | bytes 245768 | tf_op jit(solution)/shard_map/ppermute | solution.py:281
  69.5 10.0 %collective-permute-start.22 = (bf16[3,128,384]{2,1,0:T(8,128)(2,1)S(1)}, bf16[3,128,384]{2,1,0:T(8,128)(2,1)S(1)}, u32[]{:S(2)}, u32[]{:S(2)}) collective-permute-start(bf16[3,128,384]{2,1,0:T(8,128)(2,1)S(1)} %get-tuple-element.85), channel_id=1, source_target_pairs={{0,8},{8,0},{16,24},{24,16},{1,9},{9,1},{17,25},{25,17},{2,10},{10... | collective-permute-start | bytes 884744 | tf_op jit(solution)/shard_map/ppermute | solution.py:281
  70.1 14.6 %collective-permute-start.21 = (bf16[3,128,384]{2,1,0:T(8,128)(2,1)S(1)}, bf16[3,128,384]{2,1,0:T(8,128)(2,1)S(1)}, u32[]{:S(2)}, u32[]{:S(2)}) collective-permute-start(bf16[3,128,384]{2,1,0:T(8,128)(2,1)S(1)} %get-tuple-element.84), channel_id=1, source_target_pairs={{0,16},{8,24},{16,0},{24,8},{1,17},{9,25},{17,1},{25,9},{2,18},{10... | collective-permute-start | bytes 884744 | tf_op jit(solution)/shard_map/ppermute | solution.py:281
  71.3 14.7 %collective-permute-start.17 = (bf16[3,128,384]{2,1,0:T(8,128)(2,1)S(1)}, bf16[3,128,384]{2,1,0:T(8,128)(2,1)S(1)}, u32[]{:S(2)}, u32[]{:S(2)}) collective-permute-start(bf16[3,128,384]{2,1,0:T(8,128)(2,1)S(1)} %get-tuple-element.79), channel_id=1, source_target_pairs={{0,24},{8,16},{16,8},{24,0},{1,25},{9,17},{17,9},{25,1},{2,26},{10... | collective-permute-start | bytes 884744 | tf_op jit(solution)/shard_map/ppermute | solution.py:281
  (10 other events, 23.3 us)

commit v3 on v2

--- a/solution.py
+++ b/solution.py
@@ -19,6 +19,8 @@
 SMEM = pl.BlockSpec(memory_space=pltpu.SMEM)
 HBM = pl.BlockSpec(memory_space=pltpu.HBM)
 MIB = 1 << 20
+DISPATCH_LIMIT = 60
+PASS_FLOPS = 4 * 10**9
 
 
 def adam_update(master, first_old, second_old, gradient):
@@ -60,27 +62,27 @@
 
 
 def dispatch_kernel(experts, capacity, dp_count, ids_any, in_any, grad_any, *refs):
-    outs, (ids_ref, held, sems) = refs[:experts], refs[experts:]
+    outs, (masks_ref, ids_ref, held, sems) = refs[:experts], refs[experts:]
     me = lax.axis_index("expert")
     core = lax.axis_index("cuts")
-    half = held.shape[3]
+    half = outs[0].shape[2] // 2
     cores = in_any.shape[1] // (dp_count * half)
-    first = pltpu.make_async_copy(ids_any, ids_ref, sems.at[2 * dp_count])
+    first = pltpu.make_async_copy(ids_any, ids_ref, sems.at[2])
     first.start()
-    copies = []
-    for x, x_any in enumerate((in_any, grad_any)):
+    copies = [
+        pltpu.make_async_copy(x_any, held.at[x], sems.at[x])
+        for x, x_any in enumerate((in_any, grad_any))
+    ]
+    for copy in copies:
+        copy.start()
+    first.wait()
+    masks = slot_masks(ids_ref[...], me, experts, capacity)
+    masks_ref[...] = masks
+    for x in range(2):
+        copies[x].wait()
         for q in range(dp_count):
             columns = pl.ds(pl.multiple_of((q * cores + core) * half, half), half)
-            copies.append(
-                pltpu.make_async_copy(x_any.at[:, columns], held.at[x, q], sems.at[x * dp_count + q])
-            )
-            copies[-1].start()
-    first.wait()
-    masks = slot_masks(ids_ref[...], me, experts, capacity)
-    for x in range(2):
-        for q in range(dp_count):
-            copies[x * dp_count + q].wait()
-            picked = jnp.dot(masks, held[x, q], preferred_element_type=F32)
+            picked = jnp.dot(masks, held[x, :, columns], preferred_element_type=F32)
             for k in range(experts):
                 outs[k][q, :, x * half : (x + 1) * half] = picked[
                     k * capacity : (k + 1) * capacity
@@ -117,6 +119,10 @@
     out_ref[:, 2 * units :] = hidden
 
 
+def pass_kernel(got_ref, out_ref):
+    out_ref[...] = got_ref[...]
+
+
 def slot_grad_kernel(pair_ref, gate_up_ref, keep_ref, send_ref):
     core = lax.axis_index("cuts")
     width = keep_ref.shape[1]
@@ -129,22 +135,39 @@
         ).astype(BF16)
 
 
-def split_kernel(capacity, keep_ref, got_ref, *out_refs):
+def split_kernel(experts, capacity, carriers, keep_ref, got_ref, *refs):
+    outs = refs[len(carriers) :]
     total = keep_ref[...].astype(F32) + got_ref[...].astype(F32)
-    for k, out_ref in enumerate(out_refs):
-        out_ref[...] = total[k * capacity : (k + 1) * capacity].astype(BF16)
-
-
-def combine_kernel(experts, capacity, ids_any, *refs):
-    got, (out_ref, ids_ref, sem) = refs[:experts], refs[experts:]
-    me = lax.axis_index("expert")
-    copy = pltpu.make_async_copy(ids_any, ids_ref, sem)
-    copy.start()
-    copy.wait()
-    masks = slot_masks(ids_ref[...], me, experts, capacity)
-    joined = jnp.concatenate([got[k][...].astype(F32) for k in range(experts)], axis=0)
+    outs[0][...] = total[:capacity].astype(BF16)
+    height, units = outs[1].shape[1:]
+    for k in range(1, experts):
+        piece = total[k * capacity : (k + 1) * capacity]
+        blank = -piece.shape[1] % units
+        if blank:
+            piece = jnp.concatenate([piece, jnp.zeros((capacity, blank), F32)], axis=1)
+        strips = [piece[:, at : at + units] for at in range(0, piece.shape[1], units)]
+        spare = height - len(strips) * capacity
+        if spare:
+            strips.append(jnp.zeros((spare, units), F32))
+        outs[k][outs[k].shape[0] - 1] = jnp.concatenate(strips, axis=0).astype(BF16)
+
+
+def combine_kernel(capacity, masks_ref, *refs):
+    got, out_ref = refs[:-1], refs[-1]
+    width = out_ref.shape[1]
+    pieces = []
+    for ref in got:
+        if len(ref.shape) == 2:
+            pieces.append(ref[...].astype(F32))
+            continue
+        block = ref[ref.shape[0] - 1].astype(F32)
+        strips = [
+            block[n * capacity : (n + 1) * capacity] for n in range(-(-width // block.shape[1]))
+        ]
+        pieces.append(jnp.concatenate(strips, axis=1)[:, :width])
     out_ref[...] = lax.dot_general(
-        masks, joined.astype(BF16), (((0,), (0,)), ((), ())), preferred_element_type=F32
+        masks_ref[...], jnp.concatenate(pieces, axis=0).astype(BF16), (((0,), (0,)), ((), ())),
+        preferred_element_type=F32,
     ).astype(BF16)
 
 
@@ -161,7 +184,7 @@
     height = held.shape[2]
     stored = (master_any, first_any, second_any)
     masters, others = [], []
-    for g, (k, parts) in enumerate(groups):
+    for g, (k, parts, _) in enumerate(groups):
         j = slice_for(owner_ref, me, me ^ k, experts)
         rows = pl.ds(pl.multiple_of(j * height, height), height)
         for n, i in enumerate(parts):
@@ -180,11 +203,12 @@
         copy.wait()
 
 
-def weight_kernel(experts, dp_count, owner_ref, *refs):
+def weight_kernel(experts, dp_count, with_piece, owner_ref, *refs):
     mine, other = refs[:dp_count], refs[dp_count : 2 * dp_count]
     hidden = refs[2 * dp_count : 3 * dp_count]
-    outs = refs[3 * dp_count : 3 * dp_count + experts]
-    rows_ref, hidden_ref, held = refs[3 * dp_count + experts :]
+    packed = refs[3 * dp_count : 3 * dp_count + len(with_piece)]
+    outs = refs[3 * dp_count + len(with_piece) : -3]
+    rows_ref, hidden_ref, held = refs[-3:]
     me = lax.axis_index("expert")
     core = lax.axis_index("cuts")
     part = lax.axis_index("dp")
@@ -193,6 +217,8 @@
     slots = hidden[0].shape[0]
     half = mine[0].shape[2] // 2
     per_half = half // height
+    for k, piece in zip(with_piece, packed):
+        outs[k][3] = piece[0]
     for k in range(dp_count):
         hidden_ref[k * slots : (k + 1) * slots] = hidden[k][...]
     for source, side in ((mine, core), (other, 1 - core)):
@@ -217,7 +243,7 @@
 
                 @pl.when(k_of == k)
                 def _():
-                    outs[k][...] = held[...]
+                    outs[k][:3] = held[...]
 
 
 def adam_kernel(k, places, grad_ref, *refs):
@@ -258,7 +284,8 @@
 
 
 def adam_step(states, places, grad, k, buffers, experts):
-    parts, height, units = grad.shape
+    parts = 3
+    height, units = grad.shape[1:]
     types = (F32, BF16, BF16)
     return pl.pallas_call(
         functools.partial(adam_kernel, k, places),
@@ -310,16 +337,17 @@
     gate_up = gate_up_weight[0].reshape(model_width, 2 * units)
     down = down_weight[0]
 
-    sent = call(
+    *sent, masks = call(
         functools.partial(dispatch_kernel, experts, capacity, dp_count),
-        [shape(dp_count, capacity, 2 * half)] * experts,
+        [shape(dp_count, capacity, 2 * half)] * experts + [shape(slots, row_count)],
         3,
         held=(0, 1, 2),
         scratch=[
             pltpu.VMEM((1, row_count), jnp.int32),
-            pltpu.VMEM((2, dp_count, row_count, half), BF16),
-            pltpu.SemaphoreType.DMA((2 * dp_count + 1,)),
+            pltpu.VMEM((2, row_count, model_width), BF16),
+            pltpu.SemaphoreType.DMA((3,)),
         ],
+        limit=DISPATCH_LIMIT,
         flops=2 * slots * row_count * model_width,
         moved=2 * row_count * model_width + 4 * slots * model_width,
     )(ids, activations, out_grad)
@@ -327,11 +355,13 @@
 
     near = [k for k in range(1, experts) if k.bit_count() == 1]
     far = [k for k in range(1, experts) if k.bit_count() > 1]
-    groups = [(k, (0, 1, 2)) for k in range(experts)]
+    early = [(k, (0, 1, 2), 0) for k in near]
+    carriers = [(k, (0, 1, 2), 1) for k in far]
+    groups = [(0, (0, 1, 2), 0)] + early + carriers
     stored = [t[0].transpose(1, 0, 2) for t in (master_weight, first_moment, second_moment)]
     states = call(
         functools.partial(arrange_kernel, experts, groups),
-        [shape(3 * len(parts), height, units) for _, parts in groups],
+        [shape(3 * len(parts) + more, height, units) for _, parts, more in groups],
         4,
         smem=(0,),
         held=(1, 2, 3),
@@ -341,13 +371,15 @@
         ],
         moved=14 * shard_rows * 3 * units,
     )(new_owner, *stored)
-    got, states = lax.optimization_barrier((got, states))
+    got, states, gate_up = lax.optimization_barrier((got, states, gate_up))
     states = dict(zip(groups, states))
 
-    def send_states(parts, ks, *others):
-        for k in ks:
-            states[k, parts] = exchange(after(states[k, parts], *others), "expert", k, experts)
-        return [states[k, parts] for k in ks]
+    def send_states(some, *others):
+        for group in some:
+            states[group] = exchange(after(states[group], *others), "expert", group[0], experts)
+        return [states[group] for group in some]
+
+    sent_states = send_states(early)
 
     mine, *parts = call(
         functools.partial(collect_kernel, experts, dp_count),
@@ -356,8 +388,8 @@
         moved=12 * slots * model_width,
     )(*got)
     other = exchange(mine, "cuts", 1, cores)
+
     rows = {1: exchange(parts[0], "dp", 1, dp_count)}
-    sent_states = send_states((0, 1, 2), near)
 
     hidden = call(
         functools.partial(expert_kernel, dp_count),
@@ -367,57 +399,48 @@
         moved=6 * model_width * units + 8 * slots * model_width,
     )(mine, other, gate_up, down)
 
-    hiddens = {0: hidden}
-    for bits in range(1, dp_count.bit_length()):
-        level = [k for k in range(dp_count - 1, 0, -1) if k.bit_count() == bits]
-        for k in level:
-            low = k & -k
-            block = hiddens[k ^ low]
-            if bits > 1:
-                block = after(block, tied)
-            elif k == 1:
-                block = after(block, rows[1])
-            hiddens[k] = exchange(block, "dp", low, dp_count)
-        if bits == 1:
-            send_states((0, 1, 2), far, hidden, sent_states)
-        else:
-            for k in range(2, dp_count):
-                if k not in rows:
-                    rows[k] = exchange(after(parts[k - 1], tied), "dp", k, dp_count)
-        tied = [hiddens[k] for k in level]
-    hiddens = [hiddens[k] for k in range(dp_count)]
-    rows_mine = [mine] + [rows[k] for k in range(1, dp_count)]
-    rows_other = [other] + [exchange(rows[k], "cuts", 1, cores) for k in range(1, dp_count)]
-
     keep, give = call(
         slot_grad_kernel,
         [shape(slots, model_width // cores)] * 2,
         2,
         flops=4 * slots * model_width * units,
         moved=4 * model_width * units + 4 * slots * model_width,
-    )(hidden, gate_up)
+    )(after(hidden, rows[1]), gate_up)
     taken = exchange(give, "cuts", 1, cores)
-    back = call(
-        functools.partial(split_kernel, capacity),
-        [shape(capacity, model_width // cores)] * experts,
-        2,
-        moved=6 * slots * model_width // cores,
-    )(keep, taken)
-    returned = [back[0]] + [exchange(back[k], "expert", k, experts) for k in range(1, experts)]
-    input_grad = call(
-        functools.partial(combine_kernel, experts, capacity),
-        shape(row_count, model_width // cores),
-        1 + experts,
-        held=(0,),
-        scratch=[pltpu.VMEM((1, row_count), jnp.int32), pltpu.SemaphoreType.DMA(())],
-        flops=2 * slots * row_count * model_width // cores,
-        moved=4 * slots * model_width // cores,
-    )(ids, *returned)
+    summed = [shape(capacity, model_width // cores)] + [shape(1, height, units)] * (experts - 1)
+    for group in carriers:
+        summed[group[0]] = shape(*states[group].shape)
+    summed = pl.pallas_call(
+        functools.partial(split_kernel, experts, capacity, far),
+        out_shape=summed,
+        in_specs=[VMEM] * (2 + len(far)),
+        out_specs=[VMEM] * experts,
+        input_output_aliases={2 + i: k for i, k in enumerate(far)},
+        compiler_params=pltpu.CompilerParams(vmem_limit_bytes=16 * MIB),
+        cost_estimate=pl.CostEstimate(
+            flops=slots * model_width, bytes_accessed=6 * slots * model_width, transcendentals=0
+        ),
+    )(keep, taken, *[states[group] for group in carriers])
+    for group in carriers:
+        states[group] = summed[group[0]]
+    send_states(carriers, sent_states)
+
+    hiddens = {0: hidden, 2: exchange(hidden, "dp", 2, dp_count)}
+    hiddens[1] = exchange(hidden, "dp", 1, dp_count)
+    passed = call(pass_kernel, shape(*hidden.shape), 1, flops=PASS_FLOPS)(
+        after(hiddens[2], hiddens[1], rows[1])
+    )
+    hiddens[3] = exchange(passed, "dp", 1, dp_count)
+    for k in range(2, dp_count):
+        rows[k] = exchange(parts[k - 1], "dp", k, dp_count)
+    hiddens = [hiddens[k] for k in range(dp_count)]
+    rows_mine = [mine] + [rows[k] for k in range(1, dp_count)]
+    rows_other = [other] + [exchange(rows[k], "cuts", 1, cores) for k in range(1, dp_count)]
 
     grads = call(
-        functools.partial(weight_kernel, experts, dp_count),
-        [shape(3, height, units)] * experts,
-        1 + 3 * dp_count,
+        functools.partial(weight_kernel, experts, dp_count, near),
+        [shape(3 + (k in near), height, units) for k in range(experts)],
+        1 + 3 * dp_count + len(near),
         smem=(0,),
         scratch=[
             pltpu.VMEM((slots * dp_count, 2 * half), BF16),
@@ -426,11 +449,20 @@
         ],
         flops=6 * slots * dp_count * shard_rows * units,
         moved=4 * slots * dp_count * (shard_rows + units),
-    )(new_owner, *rows_mine, *rows_other, *hiddens)
+    )(new_owner, *rows_mine, *rows_other, *hiddens, *[summed[k] for k in near])
     moved_grads = {0: grads[0]}
     for k in near + far:
-        grad = after(grads[k], returned) if k in far else grads[k]
-        moved_grads[k] = exchange(grad, "expert", k, experts)
+        moved_grads[k] = exchange(grads[k], "expert", k, experts)
+
+    returned = {**moved_grads, 0: summed[0]}
+    returned.update({group[0]: states[group] for group in carriers})
+    input_grad = call(
+        functools.partial(combine_kernel, capacity),
+        shape(row_count, model_width // cores),
+        1 + experts,
+        flops=2 * slots * row_count * model_width // cores,
+        moved=4 * slots * model_width // cores,
+    )(masks, *[returned[k] for k in range(experts)])
 
     buffers = ()
     for k in range(experts):
@@ -552,6 +584,7 @@
         and height % 128 == 0
         and (model_width // (dp_count * cores)) % height == 0
         and args[5].shape[3] % 128 == 0
+        and -(-(model_width // cores) // args[5].shape[3]) * capacity <= height
     )
     return (aligned_local if whole_tiles else plain_local)(*args)
 

time: 87.8 us -> 83.2 us (0.948)
  local copies, waits for them, and re-layouts: 9.02 us -> 3.28 us
  waiting for transfers between devices: 37.7 us -> 42.8 us
  starting transfers between devices: 25.8 us -> 21.5 us
    unnamed x23 -> x15, local copies, waits for them, and re-layouts: 9.02 us -> 3.28 us
    ppermute x23 -> x20, waiting for transfers between devices: 37.7 us -> 42.8 us  [exchange(): return lax.ppermute(tensor, axis, [(i, i ^ k) for i in range(count)])]
    ppermute x23 -> x20, starting transfers between devices: 25.8 us -> 21.5 us  [exchange(): return lax.ppermute(tensor, axis, [(i, i ^ k) for i in range(count)])]
    pallas_call x3 -> x4, Pallas kernels: 3.53 us -> 3.44 us  [the longest x1 2.36 us: aligned_local(): call(functools.partial(weight_kernel, experts, dp_count, near), [shape(3...]
  transfers between devices with their start and end apart: 23 -> 20, of which waited for: 9 -> 10; matrix products, arithmetic and copies ran while one was open for 1% -> 3% of each run, Pallas kernels for 13% -> 13%
where the time goes in v3:
time: 83.2 us; the launch traced here: 83.1 us
  waiting for transfers between devices  42.8 us (51%)
  starting transfers between devices  21.5 us (26%)
  Pallas kernels  14.7 us (18%)
  local copies, waits for them, and re-layouts  3.28 us (4%)
    ppermute x20, waiting for transfers between devices, exchange(): return lax.ppermute(tensor, axis, [(i, i ^ k) for i in range(count)])  42.8 us
    ppermute x20, starting transfers between devices, exchange(): return lax.ppermute(tensor, axis, [(i, i ^ k) for i in range(count)])  21.5 us
    pallas_call x4, Pallas kernels, adam_step(): pl.pallas_call(functools.partial(adam_kernel, k, places), out_shape=[shap...  5.39 us
    unnamed x15, local copies, waits for them, and re-layouts  3.28 us
    pallas_call x1, Pallas kernels, aligned_local(): call(functools.partial(weight_kernel, experts, dp_count, near), [shape(3...  2.36 us
    pallas_call x1, Pallas kernels, aligned_local(): call(functools.partial(dispatch_kernel, experts, capacity, dp_count), [sh...  2.36 us
  transfers between devices with their start and end apart: 20, of which 10 were waited for; matrix products, arithmetic and copies ran while one was open for 3% of the time, Pallas kernels for 13%

profile of v3, /device:TPU:0, one launch (start us, length us, event | category | flops | bytes accessed | tf_op | source)
XLA Modules:
  0.0 83.1 jit_solution(7480909691722885007)
XLA Ops:
  0.6 2.4 %shard_map.120 = (bf16[4,40,512]{2,1,0:T(8,128)(2,1)}, bf16[4,40,512]{2,1,0:T(8,128)(2,1)}, bf16[4,40,512]{2,1,0:T(8,128)(2,1)}, bf16[4,40,512]{2,1,0:T(8,128)(2,1)}, bf16[160,128]{1,0:T(8,128)(2,1)}) custom-call(s32[1,128]{1,0:T(1,128)} %bitcast.33, bf16[128,2048]{1,0:T(8,128)(2,1)} %in_any.1, bf16[128,2048]{1,0:T(8,128)(2,1)} %grad_any.1), custom_call_target="tpu_custom_call" | custom-call | flops 83886080 | bytes 1835008 | tf_op jit(solution)/shard_map/pallas_call | solution.py:340
  3.0 3.0 %collective-permute-start = (bf16[4,40,512]{2,1,0:T(8,128)(2,1)}, bf16[4,40,512]{2,1,0:T(8,128)(2,1)S(1)}, u32[]{:S(2)}, u32[]{:S(2)}) collective-permute-start(bf16[4,40,512]{2,1,0:T(8,128)(2,1)} %get-tuple-element.53), channel_id=1, source_target_pairs={{0,8},{8,0},{16,24},{24,16},{1,9},{9,1},{17,25},{25,17},{2,10},{10... | collective-permute-start | bytes 491528 | tf_op jit(solution)/shard_map/ppermute | solution.py:308
  6.0 1.5 %collective-permute-start.1 = (bf16[4,40,512]{2,1,0:T(8,128)(2,1)}, bf16[4,40,512]{2,1,0:T(8,128)(2,1)S(1)}, u32[]{:S(2)}, u32[]{:S(2)}) collective-permute-start(bf16[4,40,512]{2,1,0:T(8,128)(2,1)} %get-tuple-element.54), channel_id=1, source_target_pairs={{0,16},{8,24},{16,0},{24,8},{1,17},{9,25},{17,1},{25,9},{2,18},{10... | collective-permute-start | bytes 491528 | tf_op jit(solution)/shard_map/ppermute | solution.py:308
  7.6 2.7 %copy.23 = bf16[256,8,2,384]{3,1,2,0:T(8,128)(2,1)S(1)} copy(bf16[256,8,2,384]{3,2,1,0:T(2,128)(2,1)} %bitcast.32) | data formatting | bytes 6291456
  10.8 1.2 %shard_map.121 = (bf16[9,128,384]{2,1,0:T(8,128)(2,1)S(1)}, bf16[9,128,384]{2,1,0:T(8,128)(2,1)S(1)}, bf16[9,128,384]{2,1,0:T(8,128)(2,1)S(1)}, bf16[10,128,384]{2,1,0:T(8,128)(2,1)S(1)}) custom-call(s32[4,4]{1,0:T(4,128)S(1)} %copy-done.6, f32[3,512,384]{2,1,0:T(8,128)S(1)} %bitcast.25, bf16[3,512,384]{2,1,0:T(8,128)(2,1)S(1)} %bitcast.27, ...), custom_call_target="tpu_custom_call" | custom-call | bytes 8257536 | tf_op jit(solution)/shard_map/pallas_call | solution.py:362
  12.1 3.3 %collective-permute-done.1.refs_2_ = bf16[4,40,512]{2,1,0:T(8,128)(2,1)S(1)} collective-permute-done((bf16[4,40,512]{2,1,0:T(8,128)(2,1)}, bf16[4,40,512]{2,1,0:T(8,128)(2,1)S(1)}, u32[]{:S(2)}, u32[]{:S(2)}) %collective-permute-start.1) | collective-permute-done | bytes 163872 | tf_op jit(solution)/shard_map/ppermute | solution.py:308
  15.6 1.3 %collective-permute-start.16 = (bf16[9,128,384]{2,1,0:T(8,128)(2,1)S(1)}, bf16[9,128,384]{2,1,0:T(8,128)(2,1)S(1)}, u32[]{:S(2)}, u32[]{:S(2)}) collective-permute-start(bf16[9,128,384]{2,1,0:T(8,128)(2,1)S(1)} %get-tuple-element.80), channel_id=1, source_target_pairs={{0,8},{8,0},{16,24},{24,16},{1,9},{9,1},{17,25},{25,17},{2,10},{10... | collective-permute-start | bytes 2654216 | tf_op jit(solution)/shard_map/ppermute | solution.py:308
  17.7 1.6 %collective-permute-start.4 = (bf16[160,512]{1,0:T(8,128)(2,1)S(1)}, bf16[160,512]{1,0:T(8,128)(2,1)S(1)}, u32[]{:S(2)}, u32[]{:S(2)}) collective-permute-start(bf16[160,512]{1,0:T(8,128)(2,1)S(1)} %get-tuple-element.66), channel_id=1, source_target_pairs={{0,1},{1,0},{2,3},{3,2},{4,5},{5,4},{6,7},{7,6},{8,9},{9,8},{10,11... | collective-permute-start | bytes 491528 | tf_op jit(solution)/shard_map/ppermute | solution.py:308
  20.9 2.6 %collective-permute-start.12 = (bf16[160,1152]{1,0:T(8,128)(2,1)S(1)}, bf16[160,1152]{1,0:T(8,128)(2,1)S(1)}, u32[]{:S(2)}, u32[]{:S(2)}) collective-permute-start(bf16[160,1152]{1,0:T(8,128)(2,1)S(1)} %shard_map.123.pair_ref.refs_8_), channel_id=1, source_target_pairs={{0,2},{1,3},{2,0},{3,1},{4,6},{5,7},{6,4},{7,5},{8,10},{9,11},{10,... | collective-permute-start | bytes 1105928 | tf_op jit(solution)/shard_map/ppermute | solution.py:308
  23.4 9.1 %collective-permute-done.4.refs_1_ = bf16[160,512]{1,0:T(8,128)(2,1)S(1)} collective-permute-done((bf16[160,512]{1,0:T(8,128)(2,1)S(1)}, bf16[160,512]{1,0:T(8,128)(2,1)S(1)}, u32[]{:S(2)}, u32[]{:S(2)}) %collective-permute-start.4) | collective-permute-done | bytes 163872 | tf_op jit(solution)/shard_map/ppermute | solution.py:308
  33.8 1.6 %collective-permute-done.5.got_ref = bf16[160,1024]{1,0:T(8,128)(2,1)S(1)} collective-permute-done((bf16[160,1024]{1,0:T(8,128)(2,1)S(1)}, bf16[160,1024]{1,0:T(8,128)(2,1)S(1)}, u32[]{:S(2)}, u32[]{:S(2)}) %collective-permute-start.5) | collective-permute-done | bytes 327712 | tf_op jit(solution)/shard_map/ppermute | solution.py:308
  35.5 2.1 %collective-permute-done.16.refs_0_ = bf16[9,128,384]{2,1,0:T(8,128)(2,1)S(1)} collective-permute-done((bf16[9,128,384]{2,1,0:T(8,128)(2,1)S(1)}, bf16[9,128,384]{2,1,0:T(8,128)(2,1)S(1)}, u32[]{:S(2)}, u32[]{:S(2)}) %collective-permute-start.16) | collective-permute-done | bytes 884768 | tf_op jit(solution)/shard_map/ppermute | solution.py:308
  38.6 1.8 %collective-permute-start.18 = (bf16[10,128,384]{2,1,0:T(8,128)(2,1)S(1)}, bf16[10,128,384]{2,1,0:T(8,128)(2,1)S(1)}, u32[]{:S(2)}, u32[]{:S(2)}) collective-permute-start(bf16[10,128,384]{2,1,0:T(8,128)(2,1)S(1)} %get-tuple-element.82), channel_id=1, source_target_pairs={{0,24},{8,16},{16,8},{24,0},{1,25},{9,17},{17,9},{25,1},{2,26},{10... | collective-permute-start | bytes 2949128 | tf_op jit(solution)/shard_map/ppermute | solution.py:308
  40.4 1.8 %collective-permute-start.13 = (bf16[160,1152]{1,0:T(8,128)(2,1)S(1)}, bf16[160,1152]{1,0:T(8,128)(2,1)S(1)}, u32[]{:S(2)}, u32[]{:S(2)}) collective-permute-start(bf16[160,1152]{1,0:T(8,128)(2,1)S(1)} %shard_map.126), channel_id=1, source_target_pairs={{0,1},{1,0},{2,3},{3,2},{4,5},{5,4},{6,7},{7,6},{8,9},{9,8},{10,11... | collective-permute-start | bytes 1105928 | tf_op jit(solution)/shard_map/ppermute | solution.py:308
  42.1 2.3 %collective-permute-start.7 = (bf16[160,512]{1,0:T(8,128)(2,1)S(1)}, bf16[160,512]{1,0:T(8,128)(2,1)S(1)}, u32[]{:S(2)}, u32[]{:S(2)}) collective-permute-start(bf16[160,512]{1,0:T(8,128)(2,1)S(1)} %get-tuple-element.73), channel_id=1, source_target_pairs={{0,3},{1,2},{2,1},{3,0},{4,7},{5,6},{6,5},{7,4},{8,11},{9,10},{10,... | collective-permute-start | bytes 491528 | tf_op jit(solution)/shard_map/ppermute | solution.py:308
  44.6 12.7 %collective-permute-done.7.refs_3_ = bf16[160,512]{1,0:T(8,128)(2,1)S(1)} collective-permute-done((bf16[160,512]{1,0:T(8,128)(2,1)S(1)}, bf16[160,512]{1,0:T(8,128)(2,1)S(1)}, u32[]{:S(2)}, u32[]{:S(2)}) %collective-permute-start.7) | collective-permute-done | bytes 163872 | tf_op jit(solution)/shard_map/ppermute | solution.py:308
  58.9 2.4 %shard_map.127 = (bf16[3,128,384]{2,1,0:T(8,128)(2,1)S(1)}, bf16[4,128,384]{2,1,0:T(8,128)(2,1)S(1)}, bf16[4,128,384]{2,1,0:T(8,128)(2,1)S(1)}, bf16[3,128,384]{2,1,0:T(8,128)(2,1)S(1)}) custom-call(s32[4,4]{1,0:T(4,128)S(1)} %copy-done.6, bf16[4,160,512]{2,1,0:T(8,128)(2,1)S(1)} %get-tuple-element.64.mine_ref.refs_0_, ...), custom_call_target="tpu_custom_call" | custom-call | flops 754974720 | bytes 2293760 | tf_op jit(solution)/shard_map/pallas_call | solution.py:440
  63.1 1.7 %collective-permute-start.19 = (bf16[3,128,384]{2,1,0:T(8,128)(2,1)S(1)}, bf16[3,128,384]{2,1,0:T(8,128)(2,1)S(1)}, u32[]{:S(2)}, u32[]{:S(2)}) collective-permute-start(bf16[3,128,384]{2,1,0:T(8,128)(2,1)S(1)} %get-tuple-element.83), channel_id=1, source_target_pairs={{0,24},{8,16},{16,8},{24,0},{1,25},{9,17},{17,9},{25,1},{2,26},{10... | collective-permute-start | bytes 884744 | tf_op jit(solution)/shard_map/ppermute | solution.py:308
  64.8 1.3 %shard_map.129 = (f32[4,3,128,384]{3,2,1,0:T(8,128)}, bf16[4,3,128,384]{3,2,1,0:T(8,128)(2,1)}, bf16[4,3,128,384]{3,2,1,0:T(8,128)(2,1)}) custom-call(bf16[3,128,384]{2,1,0:T(8,128)(2,1)S(1)} %get-tuple-element.84.grad_ref, bf16[9,128,384]{2,1,0:T(8,128)(2,1)S(1)} %get-tuple-element.85.refs_0_), custom_call_target="tpu_custom_call" | custom-call | flops 2949120 | bytes 2359296 | tf_op jit(solution)/shard_map/pallas_call | solution.py:290
  66.2 7.1 %collective-permute-done.14.refs_1_.grad_ref = bf16[4,128,384]{2,1,0:T(8,128)(2,1)S(1)} collective-permute-done((bf16[4,128,384]{2,1,0:T(8,128)(2,1)S(1)}, bf16[4,128,384]{2,1,0:T(8,128)(2,1)S(1)}, u32[]{:S(2)}, u32[]{:S(2)}) %collective-permute-start.14) | collective-permute-done | bytes 393248 | tf_op jit(solution)/shard_map/ppermute | solution.py:308
  73.3 1.3 %shard_map.130 = (f32[4,3,128,384]{3,2,1,0:T(8,128)}, bf16[4,3,128,384]{3,2,1,0:T(8,128)(2,1)}, bf16[4,3,128,384]{3,2,1,0:T(8,128)(2,1)}) custom-call(bf16[4,128,384]{2,1,0:T(8,128)(2,1)S(1)} %collective-permute-done.14.refs_1_.grad_ref, ...), custom_call_target="tpu_custom_call", output_to_operand_aliasing={{0}: (2, {}), {1}: (3, {}), {2}: (4, {})} | custom-call | flops 2949120 | bytes 2359296 | tf_op jit(solution)/shard_map/pallas_call | solution.py:290
  74.6 4.8 %collective-permute-done.15.refs_2_.grad_ref = bf16[4,128,384]{2,1,0:T(8,128)(2,1)S(1)} collective-permute-done((bf16[4,128,384]{2,1,0:T(8,128)(2,1)S(1)}, bf16[4,128,384]{2,1,0:T(8,128)(2,1)S(1)}, u32[]{:S(2)}, u32[]{:S(2)}) %collective-permute-start.15) | collective-permute-done | bytes 393248 | tf_op jit(solution)/shard_map/ppermute | solution.py:308
  79.4 1.3 %shard_map.131 = (f32[4,3,128,384]{3,2,1,0:T(8,128)}, bf16[4,3,128,384]{3,2,1,0:T(8,128)(2,1)}, bf16[4,3,128,384]{3,2,1,0:T(8,128)(2,1)}) custom-call(bf16[4,128,384]{2,1,0:T(8,128)(2,1)S(1)} %collective-permute-done.15.refs_2_.grad_ref, ...), custom_call_target="tpu_custom_call", output_to_operand_aliasing={{0}: (2, {}), {1}: (3, {}), {2}: (4, {})} | custom-call | flops 2949120 | bytes 2359296 | tf_op jit(solution)/shard_map/pallas_call | solution.py:290
  81.7 1.3 %shard_map.132 = (f32[4,3,128,384]{3,2,1,0:T(8,128)}, bf16[4,3,128,384]{3,2,1,0:T(8,128)(2,1)}, bf16[4,3,128,384]{3,2,1,0:T(8,128)(2,1)}) custom-call(bf16[3,128,384]{2,1,0:T(8,128)(2,1)S(1)} %collective-permute-done.19.grad_ref, ...), custom_call_target="tpu_custom_call", output_to_operand_aliasing={{0}: (2, {}), {1}: (3, {}), {2}: (4, {})} | custom-call | flops 2949120 | bytes 2359296 | tf_op jit(solution)/shard_map/pallas_call | solution.py:290
  (44 shorter events, 10.0 us)
Async XLA Ops:
  3.0 9.0 %collective-permute-start = (bf16[4,40,512]{2,1,0:T(8,128)(2,1)}, bf16[4,40,512]{2,1,0:T(8,128)(2,1)S(1)}, u32[]{:S(2)}, u32[]{:S(2)}) collective-permute-start(bf16[4,40,512]{2,1,0:T(8,128)(2,1)} %get-tuple-element.53), channel_id=1, source_target_pairs={{0,8},{8,0},{16,24},{24,16},{1,9},{9,1},{17,25},{25,17},{2,10},{10... | collective-permute-start | bytes 491528 | tf_op jit(solution)/shard_map/ppermute | solution.py:308
  6.0 9.4 %collective-permute-start.1 = (bf16[4,40,512]{2,1,0:T(8,128)(2,1)}, bf16[4,40,512]{2,1,0:T(8,128)(2,1)S(1)}, u32[]{:S(2)}, u32[]{:S(2)}) collective-permute-start(bf16[4,40,512]{2,1,0:T(8,128)(2,1)} %get-tuple-element.54), channel_id=1, source_target_pairs={{0,16},{8,24},{16,0},{24,8},{1,17},{9,25},{17,1},{25,9},{2,18},{10... | collective-permute-start | bytes 491528 | tf_op jit(solution)/shard_map/ppermute | solution.py:308
  7.5 7.9 %collective-permute-start.2 = (bf16[4,40,512]{2,1,0:T(8,128)(2,1)}, bf16[4,40,512]{2,1,0:T(8,128)(2,1)S(1)}, u32[]{:S(2)}, u32[]{:S(2)}) collective-permute-start(bf16[4,40,512]{2,1,0:T(8,128)(2,1)} %get-tuple-element.55), channel_id=1, source_target_pairs={{0,24},{8,16},{16,8},{24,0},{1,25},{9,17},{17,9},{25,1},{2,26},{10... | collective-permute-start | bytes 491528 | tf_op jit(solution)/shard_map/ppermute | solution.py:308
  7.6 3.3 %copy-start.3 = (bf16[1,512,3,384]{3,1,2,0:T(8,128)(2,1)S(1)}, bf16[1,512,3,384]{3,1,2,0:T(8,128)(2,1)}, u32[]{:S(2)}) copy-start(bf16[1,512,3,384]{3,1,2,0:T(8,128)(2,1)} %param.16) | copy-start | bytes 3538948
  7.6 3.3 %copy-start.6 = (s32[4,4]{1,0:T(4,128)S(1)}, s32[4,4]{1,0:T(4,128)}, u32[]{:S(2)}) copy-start(s32[4,4]{1,0:T(4,128)} %owner_ref.3) | copy-start | bytes 196
  10.8 4.6 %copy-start.4 = (bf16[4,40,512]{2,1,0:T(8,128)(2,1)S(1)}, bf16[4,40,512]{2,1,0:T(8,128)(2,1)}, u32[]{:S(2)}) copy-start(bf16[4,40,512]{2,1,0:T(8,128)(2,1)} %get-tuple-element.60.refs_0_) | copy-start | bytes 491524
  10.8 8.4 %copy-start.1 = (bf16[1,2048,384]{2,1,0:T(8,128)(2,1)S(1)}, bf16[1,2048,384]{2,1,0:T(8,128)(2,1)}, u32[]{:S(2)}) copy-start(bf16[1,2048,384]{2,1,0:T(8,128)(2,1)} %param.13) | copy-start | bytes 4718596
  15.5 3.8 %collective-permute-start.3 = (bf16[4,160,512]{2,1,0:T(8,128)(2,1)S(1)}, bf16[4,160,512]{2,1,0:T(8,128)(2,1)S(1)}, u32[]{:S(2)}, u32[]{:S(2)}) collective-permute-start(bf16[4,160,512]{2,1,0:T(8,128)(2,1)S(1)} %get-tuple-element.64.mine_ref.refs_0_), channel_id=1, source_target_pairs={{0,4},{4,0},{1,5},{5,1},{2,6},{6,2},{3,7},{7,3},{8,12},{12,8},{9,1... | collective-permute-start | bytes 1966088 | tf_op jit(solution)/shard_map/ppermute | solution.py:308
  15.6 22.1 %collective-permute-start.16 = (bf16[9,128,384]{2,1,0:T(8,128)(2,1)S(1)}, bf16[9,128,384]{2,1,0:T(8,128)(2,1)S(1)}, u32[]{:S(2)}, u32[]{:S(2)}) collective-permute-start(bf16[9,128,384]{2,1,0:T(8,128)(2,1)S(1)} %get-tuple-element.80), channel_id=1, source_target_pairs={{0,8},{8,0},{16,24},{24,16},{1,9},{9,1},{17,25},{25,17},{2,10},{10... | collective-permute-start | bytes 2654216 | tf_op jit(solution)/shard_map/ppermute | solution.py:308
  16.9 21.7 %collective-permute-start.17 = (bf16[9,128,384]{2,1,0:T(8,128)(2,1)S(1)}, bf16[9,128,384]{2,1,0:T(8,128)(2,1)S(1)}, u32[]{:S(2)}, u32[]{:S(2)}) collective-permute-start(bf16[9,128,384]{2,1,0:T(8,128)(2,1)S(1)} %get-tuple-element.81), channel_id=1, source_target_pairs={{0,16},{8,24},{16,0},{24,8},{1,17},{9,25},{17,1},{25,9},{2,18},{10... | collective-permute-start | bytes 2654216 | tf_op jit(solution)/shard_map/ppermute | solution.py:308
  17.7 14.9 %collective-permute-start.4 = (bf16[160,512]{1,0:T(8,128)(2,1)S(1)}, bf16[160,512]{1,0:T(8,128)(2,1)S(1)}, u32[]{:S(2)}, u32[]{:S(2)}) collective-permute-start(bf16[160,512]{1,0:T(8,128)(2,1)S(1)} %get-tuple-element.66), channel_id=1, source_target_pairs={{0,1},{1,0},{2,3},{3,2},{4,5},{5,4},{6,7},{7,6},{8,9},{9,8},{10,11... | collective-permute-start | bytes 491528 | tf_op jit(solution)/shard_map/ppermute | solution.py:308
  20.3 20.0 %collective-permute-start.11 = (bf16[160,1152]{1,0:T(8,128)(2,1)S(1)}, bf16[160,1152]{1,0:T(8,128)(2,1)S(1)}, u32[]{:S(2)}, u32[]{:S(2)}) collective-permute-start(bf16[160,1152]{1,0:T(8,128)(2,1)S(1)} %shard_map.123.pair_ref.refs_8_), channel_id=1, source_target_pairs={{0,1},{1,0},{2,3},{3,2},{4,5},{5,4},{6,7},{7,6},{8,9},{9,8},{10,11... | collective-permute-start | bytes 1105928 | tf_op jit(solution)/shard_map/ppermute | solution.py:308
  20.9 19.5 %collective-permute-start.12 = (bf16[160,1152]{1,0:T(8,128)(2,1)S(1)}, bf16[160,1152]{1,0:T(8,128)(2,1)S(1)}, u32[]{:S(2)}, u32[]{:S(2)}) collective-permute-start(bf16[160,1152]{1,0:T(8,128)(2,1)S(1)} %shard_map.123.pair_ref.refs_8_), channel_id=1, source_target_pairs={{0,2},{1,3},{2,0},{3,1},{4,6},{5,7},{6,4},{7,5},{8,10},{9,11},{10,... | collective-permute-start | bytes 1105928 | tf_op jit(solution)/shard_map/ppermute | solution.py:308
  33.8 1.7 %collective-permute-start.5 = (bf16[160,1024]{1,0:T(8,128)(2,1)S(1)}, bf16[160,1024]{1,0:T(8,128)(2,1)S(1)}, u32[]{:S(2)}, u32[]{:S(2)}) collective-permute-start(bf16[160,1024]{1,0:T(8,128)(2,1)S(1)} %get-tuple-element.69), channel_id=1, source_target_pairs={{0,4},{4,0},{1,5},{5,1},{2,6},{6,2},{3,7},{7,3},{8,12},{12,8},{9,1... | collective-permute-start | bytes 983048 | tf_op jit(solution)/shard_map/ppermute | solution.py:308
  38.6 42.2 %collective-permute-start.18 = (bf16[10,128,384]{2,1,0:T(8,128)(2,1)S(1)}, bf16[10,128,384]{2,1,0:T(8,128)(2,1)S(1)}, u32[]{:S(2)}, u32[]{:S(2)}) collective-permute-start(bf16[10,128,384]{2,1,0:T(8,128)(2,1)S(1)} %get-tuple-element.82), channel_id=1, source_target_pairs={{0,24},{8,16},{16,8},{24,0},{1,25},{9,17},{17,9},{25,1},{2,26},{10... | collective-permute-start | bytes 2949128 | tf_op jit(solution)/shard_map/ppermute | solution.py:308
  40.4 18.5 %collective-permute-start.13 = (bf16[160,1152]{1,0:T(8,128)(2,1)S(1)}, bf16[160,1152]{1,0:T(8,128)(2,1)S(1)}, u32[]{:S(2)}, u32[]{:S(2)}) collective-permute-start(bf16[160,1152]{1,0:T(8,128)(2,1)S(1)} %shard_map.126), channel_id=1, source_target_pairs={{0,1},{1,0},{2,3},{3,2},{4,5},{5,4},{6,7},{7,6},{8,9},{9,8},{10,11... | collective-permute-start | bytes 1105928 | tf_op jit(solution)/shard_map/ppermute | solution.py:308
  42.1 15.1 %collective-permute-start.7 = (bf16[160,512]{1,0:T(8,128)(2,1)S(1)}, bf16[160,512]{1,0:T(8,128)(2,1)S(1)}, u32[]{:S(2)}, u32[]{:S(2)}) collective-permute-start(bf16[160,512]{1,0:T(8,128)(2,1)S(1)} %get-tuple-element.73), channel_id=1, source_target_pairs={{0,3},{1,2},{2,1},{3,0},{4,7},{5,6},{6,5},{7,4},{8,11},{9,10},{10,... | collective-permute-start | bytes 491528 | tf_op jit(solution)/shard_map/ppermute | solution.py:308
  44.5 12.8 %collective-permute-start.6 = (bf16[160,512]{1,0:T(8,128)(2,1)S(1)}, bf16[160,512]{1,0:T(8,128)(2,1)S(1)}, u32[]{:S(2)}, u32[]{:S(2)}) collective-permute-start(bf16[160,512]{1,0:T(8,128)(2,1)S(1)} %get-tuple-element.72), channel_id=1, source_target_pairs={{0,2},{1,3},{2,0},{3,1},{4,6},{5,7},{6,4},{7,5},{8,10},{9,11},{10,... | collective-permute-start | bytes 491528 | tf_op jit(solution)/shard_map/ppermute | solution.py:308
  44.6 14.1 %collective-permute-start.8 = (bf16[160,512]{1,0:T(8,128)(2,1)S(1)}, bf16[160,512]{1,0:T(8,128)(2,1)S(1)}, u32[]{:S(2)}, u32[]{:S(2)}) collective-permute-start(bf16[160,512]{1,0:T(8,128)(2,1)S(1)} %collective-permute-done.4.refs_1_), channel_id=1, source_target_pairs={{0,4},{4,0},{1,5},{5,1},{2,6},{6,2},{3,7},{7,3},{8,12},{12,8},{9,1... | collective-permute-start | bytes 491528 | tf_op jit(solution)/shard_map/ppermute | solution.py:308
  57.3 1.4 %collective-permute-start.10 = (bf16[160,512]{1,0:T(8,128)(2,1)S(1)}, bf16[160,512]{1,0:T(8,128)(2,1)S(1)}, u32[]{:S(2)}, u32[]{:S(2)}) collective-permute-start(bf16[160,512]{1,0:T(8,128)(2,1)S(1)} %collective-permute-done.7.refs_3_), channel_id=1, source_target_pairs={{0,4},{4,0},{1,5},{5,1},{2,6},{6,2},{3,7},{7,3},{8,12},{12,8},{9,1... | collective-permute-start | bytes 491528 | tf_op jit(solution)/shard_map/ppermute | solution.py:308
  57.3 1.6 %collective-permute-start.9 = (bf16[160,512]{1,0:T(8,128)(2,1)S(1)}, bf16[160,512]{1,0:T(8,128)(2,1)S(1)}, u32[]{:S(2)}, u32[]{:S(2)}) collective-permute-start(bf16[160,512]{1,0:T(8,128)(2,1)S(1)} %collective-permute-done.6.refs_2_), channel_id=1, source_target_pairs={{0,4},{4,0},{1,5},{5,1},{2,6},{6,2},{3,7},{7,3},{8,12},{12,8},{9,1... | collective-permute-start | bytes 491528 | tf_op jit(solution)/shard_map/ppermute | solution.py:308
  61.3 12.0 %collective-permute-start.14 = (bf16[4,128,384]{2,1,0:T(8,128)(2,1)S(1)}, bf16[4,128,384]{2,1,0:T(8,128)(2,1)S(1)}, u32[]{:S(2)}, u32[]{:S(2)}) collective-permute-start(bf16[4,128,384]{2,1,0:T(8,128)(2,1)S(1)} %get-tuple-element.77), channel_id=1, source_target_pairs={{0,8},{8,0},{16,24},{24,16},{1,9},{9,1},{17,25},{25,17},{2,10},{10... | collective-permute-start | bytes 1179656 | tf_op jit(solution)/shard_map/ppermute | solution.py:308
  62.1 17.3 %collective-permute-start.15 = (bf16[4,128,384]{2,1,0:T(8,128)(2,1)S(1)}, bf16[4,128,384]{2,1,0:T(8,128)(2,1)S(1)}, u32[]{:S(2)}, u32[]{:S(2)}) collective-permute-start(bf16[4,128,384]{2,1,0:T(8,128)(2,1)S(1)} %get-tuple-element.78), channel_id=1, source_target_pairs={{0,16},{8,24},{16,0},{24,8},{1,17},{9,25},{17,1},{25,9},{2,18},{10... | collective-permute-start | bytes 1179656 | tf_op jit(solution)/shard_map/ppermute | solution.py:308
  63.1 18.6 %collective-permute-start.19 = (bf16[3,128,384]{2,1,0:T(8,128)(2,1)S(1)}, bf16[3,128,384]{2,1,0:T(8,128)(2,1)S(1)}, u32[]{:S(2)}, u32[]{:S(2)}) collective-permute-start(bf16[3,128,384]{2,1,0:T(8,128)(2,1)S(1)} %get-tuple-element.83), channel_id=1, source_target_pairs={{0,24},{8,16},{16,8},{24,0},{1,25},{9,17},{17,9},{25,1},{2,26},{10... | collective-permute-start | bytes 884744 | tf_op jit(solution)/shard_map/ppermute | solution.py:308
  (3 other events, 7.0 us)

commit v4 on v3

--- a/solution.py
+++ b/solution.py
@@ -20,7 +20,7 @@
 HBM = pl.BlockSpec(memory_space=pltpu.HBM)
 MIB = 1 << 20
 DISPATCH_LIMIT = 60
-PASS_FLOPS = 4 * 10**9
+PASS_FLOPS = 2 * 10**9
 
 
 def adam_update(master, first_old, second_old, gradient):
@@ -203,62 +203,59 @@
         copy.wait()
 
 
-def weight_kernel(experts, dp_count, with_piece, owner_ref, *refs):
+def weight_kernel(experts, dp_count, ks, with_piece, owner_ref, *refs):
     mine, other = refs[:dp_count], refs[dp_count : 2 * dp_count]
     hidden = refs[2 * dp_count : 3 * dp_count]
     packed = refs[3 * dp_count : 3 * dp_count + len(with_piece)]
-    outs = refs[3 * dp_count + len(with_piece) : -3]
-    rows_ref, hidden_ref, held = refs[-3:]
+    outs = refs[3 * dp_count + len(with_piece) : -2]
+    rows_ref, hidden_ref = refs[-2:]
     me = lax.axis_index("expert")
     core = lax.axis_index("cuts")
     part = lax.axis_index("dp")
-    height = outs[0].shape[1]
-    units = outs[0].shape[2]
+    height, units = outs[0].shape[1:]
     slots = hidden[0].shape[0]
     half = mine[0].shape[2] // 2
     per_half = half // height
-    for k, piece in zip(with_piece, packed):
-        outs[k][3] = piece[0]
-    for k in range(dp_count):
-        hidden_ref[k * slots : (k + 1) * slots] = hidden[k][...]
-    for source, side in ((mine, core), (other, 1 - core)):
-        rows_ref[:slots] = source[0][part]
-        for a in range(1, dp_count):
-            rows_ref[a * slots : (a + 1) * slots] = source[a][...]
-        sums = [
-            lax.dot_general(
-                rows_ref[:, at : at + half], hidden_ref[:, low:high], (((0,), (0,)), ((), ())),
+    for n in range(dp_count):
+        place = slice(n * slots, (n + 1) * slots)
+        hidden_ref[place] = hidden[n][...]
+        for side, source in enumerate((mine, other)):
+            rows_ref[side, place] = source[0][part] if n == 0 else source[n][...]
+    for out, k in zip(outs, ks):
+        j = slice_for(owner_ref, me, me ^ k, experts)
+        side = jnp.where(j // per_half == core, 0, 1)
+        at = lax.rem(j, per_half) * height
+        for m, offset in enumerate((0, 0, half)):
+            columns = pl.ds(pl.multiple_of(at + offset, height), height)
+            total = lax.dot_general(
+                rows_ref[side, :, columns],
+                hidden_ref[:, m * units : (m + 1) * units],
+                (((0,), (0,)), ((), ())),
                 preferred_element_type=F32,
             )
-            * (1.0 / dp_count)
-            for at, low, high in (
-                (0, 0, units), (0, units, 2 * units), (half, 2 * units, 3 * units),
-            )
-        ]
-        for i in range(per_half):
-            for m in range(3):
-                held[m] = sums[m][i * height : (i + 1) * height].astype(BF16)
-            k_of = owner_ref[me, side * per_half + i] ^ me
-            for k in range(experts):
-
-                @pl.when(k_of == k)
-                def _():
-                    outs[k][:3] = held[...]
-
-
-def adam_kernel(k, places, grad_ref, *refs):
+            out[m] = (total * (1.0 / dp_count)).astype(BF16)
+        if k in with_piece:
+            out[3] = packed[with_piece.index(k)][0]
+
+
+def adam_kernel(tasks, *refs):
     outs, held, sems = refs[-7:-4], refs[-4:-1], refs[-1]
-    block = lax.axis_index("expert") ^ k
-    copies = []
-    for m in range(3):
-        master, first, second = [refs[ref][3 * n + m] for ref, n in places]
-        values = adam_update(master.astype(F32), first, second, grad_ref[m].astype(F32))
-        for i in range(3):
-            held[i][m] = values[i].astype(held[i].dtype)
-            copies.append(
-                pltpu.make_async_copy(held[i].at[m], outs[i].at[block, m], sems.at[m, i])
-            )
-            copies[-1].start()
+    me = lax.axis_index("expert")
+    copies, at = [], 0
+    for t, (k, places) in enumerate(tasks):
+        grad_ref, states = refs[at], refs[at + 1 :]
+        at += 2 + max(ref for ref, _ in places)
+        for m in range(3):
+            master, first, second = [states[ref][3 * n + m] for ref, n in places]
+            values = adam_update(master.astype(F32), first, second, grad_ref[m].astype(F32))
+            for i in range(3):
+                held[i][t, m] = values[i].astype(held[i].dtype)
+                copies.append(
+                    pltpu.make_async_copy(
+                        held[i].at[t, m], outs[i].at[me ^ k, m], sems.at[t, m, i]
+                    )
+                )
+                copies[-1].start()
     for copy in copies:
         copy.wait()
 
@@ -283,25 +280,25 @@
     return jax.ShapeDtypeStruct(dims, dtype)
 
 
-def adam_step(states, places, grad, k, buffers, experts):
+def adam_step(tasks, buffers, experts):
     parts = 3
-    height, units = grad.shape[1:]
+    height, units = tasks[0][2].shape[1:]
     types = (F32, BF16, BF16)
+    inputs = [t for _, _, grad, states in tasks for t in (grad, *states)]
+    size = len(tasks) * parts * height * units
     return pl.pallas_call(
-        functools.partial(adam_kernel, k, places),
+        functools.partial(adam_kernel, [(k, places) for k, places, _, _ in tasks]),
         out_shape=[shape(experts, parts, height, units, dtype=t) for t in types],
-        in_specs=[VMEM] * (1 + len(states)) + [HBM] * len(buffers),
+        in_specs=[VMEM] * len(inputs) + [HBM] * len(buffers),
         out_specs=[HBM] * 3,
-        scratch_shapes=[pltpu.VMEM((parts, height, units), t) for t in types]
-        + [pltpu.SemaphoreType.DMA((parts, 3))],
-        input_output_aliases={1 + len(states) + i: i for i in range(len(buffers))},
+        scratch_shapes=[pltpu.VMEM((len(tasks), parts, height, units), t) for t in types]
+        + [pltpu.SemaphoreType.DMA((len(tasks), parts, 3))],
+        input_output_aliases={len(inputs) + i: i for i in range(len(buffers))},
         compiler_params=pltpu.CompilerParams(vmem_limit_bytes=16 * MIB),
         cost_estimate=pl.CostEstimate(
-            flops=20 * parts * height * units,
-            bytes_accessed=16 * parts * height * units,
-            transcendentals=2 * parts * height * units,
+            flops=20 * size, bytes_accessed=16 * size, transcendentals=2 * size
         ),
-    )(grad, *states, *buffers)
+    )(*inputs, *buffers)
 
 
 def exchange(tensor, axis, k, count):
@@ -355,8 +352,8 @@
 
     near = [k for k in range(1, experts) if k.bit_count() == 1]
     far = [k for k in range(1, experts) if k.bit_count() > 1]
-    early = [(k, (0, 1, 2), 0) for k in near]
-    carriers = [(k, (0, 1, 2), 1) for k in far]
+    early = [(k, (0, 1, 2), 0) for k in far]
+    carriers = [(k, (0, 1, 2), 1) for k in near]
     groups = [(0, (0, 1, 2), 0)] + early + carriers
     stored = [t[0].transpose(1, 0, 2) for t in (master_weight, first_moment, second_moment)]
     states = call(
@@ -411,45 +408,49 @@
     for group in carriers:
         summed[group[0]] = shape(*states[group].shape)
     summed = pl.pallas_call(
-        functools.partial(split_kernel, experts, capacity, far),
+        functools.partial(split_kernel, experts, capacity, near),
         out_shape=summed,
-        in_specs=[VMEM] * (2 + len(far)),
+        in_specs=[VMEM] * (2 + len(near)),
         out_specs=[VMEM] * experts,
-        input_output_aliases={2 + i: k for i, k in enumerate(far)},
+        input_output_aliases={2 + i: k for i, k in enumerate(near)},
         compiler_params=pltpu.CompilerParams(vmem_limit_bytes=16 * MIB),
         cost_estimate=pl.CostEstimate(
             flops=slots * model_width, bytes_accessed=6 * slots * model_width, transcendentals=0
         ),
     )(keep, taken, *[states[group] for group in carriers])
+    summed = list(summed)
     for group in carriers:
         states[group] = summed[group[0]]
-    send_states(carriers, sent_states)
 
     hiddens = {0: hidden, 2: exchange(hidden, "dp", 2, dp_count)}
     hiddens[1] = exchange(hidden, "dp", 1, dp_count)
+    send_states(carriers, sent_states)
     passed = call(pass_kernel, shape(*hidden.shape), 1, flops=PASS_FLOPS)(
         after(hiddens[2], hiddens[1], rows[1])
     )
     hiddens[3] = exchange(passed, "dp", 1, dp_count)
-    for k in range(2, dp_count):
-        rows[k] = exchange(parts[k - 1], "dp", k, dp_count)
+    rows[3] = exchange(parts[2], "dp", 3, dp_count)
+    rows[2] = exchange(after(parts[1], rows[3]), "dp", 2, dp_count)
     hiddens = [hiddens[k] for k in range(dp_count)]
     rows_mine = [mine] + [rows[k] for k in range(1, dp_count)]
     rows_other = [other] + [exchange(rows[k], "cuts", 1, cores) for k in range(1, dp_count)]
 
-    grads = call(
-        functools.partial(weight_kernel, experts, dp_count, near),
-        [shape(3 + (k in near), height, units) for k in range(experts)],
-        1 + 3 * dp_count + len(near),
-        smem=(0,),
-        scratch=[
-            pltpu.VMEM((slots * dp_count, 2 * half), BF16),
-            pltpu.VMEM((slots * dp_count, 3 * units), BF16),
-            pltpu.VMEM((3, height, units), BF16),
-        ],
-        flops=6 * slots * dp_count * shard_rows * units,
-        moved=4 * slots * dp_count * (shard_rows + units),
-    )(new_owner, *rows_mine, *rows_other, *hiddens, *[summed[k] for k in near])
+    grads = {}
+    for ks in (near, far + [0]):
+        some = [k for k in ks if k in far]
+        made = call(
+            functools.partial(weight_kernel, experts, dp_count, ks, some),
+            [shape(3 + (k in some), height, units) for k in ks],
+            1 + 3 * dp_count + len(some),
+            smem=(0,),
+            scratch=[
+                pltpu.VMEM((2, slots * dp_count, 2 * half), BF16),
+                pltpu.VMEM((slots * dp_count, 3 * units), BF16),
+            ],
+            flops=6 * slots * dp_count * height * len(ks) * units,
+            moved=4 * slots * dp_count * (shard_rows + units),
+        )(new_owner, *rows_mine, *rows_other, *hiddens, *[summed[k] for k in some])
+        grads.update(zip(ks, made))
     moved_grads = {0: grads[0]}
     for k in near + far:
         moved_grads[k] = exchange(grads[k], "expert", k, experts)
@@ -465,15 +466,16 @@
     )(masks, *[returned[k] for k in range(experts)])
 
     buffers = ()
-    for k in range(experts):
-        held = [group for group in groups if group[0] == k]
-        places = [
-            next((n, group[1].index(i)) for n, group in enumerate(held) if i in group[1])
-            for i in range(3)
-        ]
-        buffers = adam_step(
-            [states[group] for group in held], places, moved_grads[k], k, buffers, experts
-        )
+    for ks in ([0], far, near):
+        tasks = []
+        for k in ks:
+            held = [group for group in groups if group[0] == k]
+            places = [
+                next((n, group[1].index(i)) for n, group in enumerate(held) if i in group[1])
+                for i in range(3)
+            ]
+            tasks.append((k, places, moved_grads[k], [states[group] for group in held]))
+        buffers = adam_step(tasks, buffers, experts)
     outs = [b.transpose(0, 2, 1, 3)[None] for b in buffers]
     return (input_grad, *outs)
 
@@ -576,7 +578,8 @@
     height = model_width // (dp_count * experts)
     whole_tiles = (
         experts & (experts - 1) == 0
-        and dp_count & (dp_count - 1) == 0
+        and experts >= 4
+        and dp_count == 4
         and cores == 2
         and capacity % 8 == 0
         and (experts * capacity) % 16 == 0

time: 83.2 us -> 80 us (0.962)
  waiting for transfers between devices: 42.8 us -> 35.9 us
  starting transfers between devices: 21.5 us -> 25.2 us
    ppermute x20, waiting for transfers between devices: 42.8 us -> 35.9 us  [exchange(): return lax.ppermute(tensor, axis, [(i, i ^ k) for i in range(count)])]
    ppermute x20, starting transfers between devices: 21.5 us -> 25.2 us  [exchange(): return lax.ppermute(tensor, axis, [(i, i ^ k) for i in range(count)])]
  transfers between devices with their start and end apart: 20 -> 20, of which waited for: 10 -> 8; matrix products, arithmetic and copies ran while one was open for 3% -> 3% of each run, Pallas kernels for 13% -> 13%
where the time goes in v4:
time: 80 us; the launch traced here: 79.8 us
  waiting for transfers between devices  35.9 us (45%)
  starting transfers between devices  25.2 us (32%)
  Pallas kernels  14.7 us (18%)
  local copies, waits for them, and re-layouts  3.28 us (4%)
    ppermute x20, waiting for transfers between devices, exchange(): return lax.ppermute(tensor, axis, [(i, i ^ k) for i in range(count)])  35.9 us
    ppermute x20, starting transfers between devices, exchange(): return lax.ppermute(tensor, axis, [(i, i ^ k) for i in range(count)])  25.2 us
    pallas_call x3, Pallas kernels, adam_step(): pl.pallas_call(functools.partial(adam_kernel, [(k, places) for k, places,...  4.65 us
    unnamed x15, local copies, waits for them, and re-layouts  3.28 us
    pallas_call x2, Pallas kernels, aligned_local(): call(functools.partial(weight_kernel, experts, dp_count, ks, some), [shap...  3.06 us
    pallas_call x1, Pallas kernels, aligned_local(): call(functools.partial(dispatch_kernel, experts, capacity, dp_count), [sh...  2.36 us
  transfers between devices with their start and end apart: 20, of which 8 were waited for; matrix products, arithmetic and copies ran while one was open for 3% of the time, Pallas kernels for 13%

profile of v4, /device:TPU:0, one launch (start us, length us, event | category | flops | bytes accessed | tf_op | source)
XLA Modules:
  0.0 79.8 jit_solution(1026021244401894068)
XLA Ops:
  0.6 2.4 %shard_map.120 = (bf16[4,40,512]{2,1,0:T(8,128)(2,1)}, bf16[4,40,512]{2,1,0:T(8,128)(2,1)}, bf16[4,40,512]{2,1,0:T(8,128)(2,1)}, bf16[4,40,512]{2,1,0:T(8,128)(2,1)}, bf16[160,128]{1,0:T(8,128)(2,1)}) custom-call(s32[1,128]{1,0:T(1,128)} %bitcast.33, bf16[128,2048]{1,0:T(8,128)(2,1)} %in_any.1, bf16[128,2048]{1,0:T(8,128)(2,1)} %grad_any.1), custom_call_target="tpu_custom_call" | custom-call | flops 83886080 | bytes 1835008 | tf_op jit(solution)/shard_map/pallas_call | solution.py:337
  3.0 3.0 %collective-permute-start = (bf16[4,40,512]{2,1,0:T(8,128)(2,1)}, bf16[4,40,512]{2,1,0:T(8,128)(2,1)S(1)}, u32[]{:S(2)}, u32[]{:S(2)}) collective-permute-start(bf16[4,40,512]{2,1,0:T(8,128)(2,1)} %get-tuple-element.52), channel_id=1, source_target_pairs={{0,8},{8,0},{16,24},{24,16},{1,9},{9,1},{17,25},{25,17},{2,10},{10... | collective-permute-start | bytes 491528 | tf_op jit(solution)/shard_map/ppermute | solution.py:305
  6.0 1.5 %collective-permute-start.1 = (bf16[4,40,512]{2,1,0:T(8,128)(2,1)}, bf16[4,40,512]{2,1,0:T(8,128)(2,1)S(1)}, u32[]{:S(2)}, u32[]{:S(2)}) collective-permute-start(bf16[4,40,512]{2,1,0:T(8,128)(2,1)} %get-tuple-element.53), channel_id=1, source_target_pairs={{0,16},{8,24},{16,0},{24,8},{1,17},{9,25},{17,1},{25,9},{2,18},{10... | collective-permute-start | bytes 491528 | tf_op jit(solution)/shard_map/ppermute | solution.py:305
  7.6 2.7 %copy.21 = bf16[256,8,2,384]{3,1,2,0:T(8,128)(2,1)S(1)} copy(bf16[256,8,2,384]{3,2,1,0:T(2,128)(2,1)} %bitcast.32) | data formatting | bytes 6291456
  12.1 3.3 %collective-permute-done.1.refs_2_ = bf16[4,40,512]{2,1,0:T(8,128)(2,1)S(1)} collective-permute-done((bf16[4,40,512]{2,1,0:T(8,128)(2,1)}, bf16[4,40,512]{2,1,0:T(8,128)(2,1)S(1)}, u32[]{:S(2)}, u32[]{:S(2)}) %collective-permute-start.1) | collective-permute-done | bytes 163872 | tf_op jit(solution)/shard_map/ppermute | solution.py:305
  15.6 1.6 %collective-permute-start.6 = (bf16[9,128,384]{2,1,0:T(8,128)(2,1)S(1)}, bf16[9,128,384]{2,1,0:T(8,128)(2,1)S(1)}, u32[]{:S(2)}, u32[]{:S(2)}) collective-permute-start(bf16[9,128,384]{2,1,0:T(8,128)(2,1)S(1)} %get-tuple-element.73), channel_id=1, source_target_pairs={{0,24},{8,16},{16,8},{24,0},{1,25},{9,17},{17,9},{25,1},{2,26},{10... | collective-permute-start | bytes 2654216 | tf_op jit(solution)/shard_map/ppermute | solution.py:305
  17.1 1.6 %collective-permute-start.4 = (bf16[160,512]{1,0:T(8,128)(2,1)S(1)}, bf16[160,512]{1,0:T(8,128)(2,1)S(1)}, u32[]{:S(2)}, u32[]{:S(2)}) collective-permute-start(bf16[160,512]{1,0:T(8,128)(2,1)S(1)} %get-tuple-element.65), channel_id=1, source_target_pairs={{0,1},{1,0},{2,3},{3,2},{4,5},{5,4},{6,7},{7,6},{8,9},{9,8},{10,11... | collective-permute-start | bytes 491528 | tf_op jit(solution)/shard_map/ppermute | solution.py:305
  19.8 2.7 %collective-permute-start.15 = (bf16[160,1152]{1,0:T(8,128)(2,1)S(1)}, bf16[160,1152]{1,0:T(8,128)(2,1)S(1)}, u32[]{:S(2)}, u32[]{:S(2)}) collective-permute-start(bf16[160,1152]{1,0:T(8,128)(2,1)S(1)} %shard_map.123.pair_ref.refs_8_), channel_id=1, source_target_pairs={{0,2},{1,3},{2,0},{3,1},{4,6},{5,7},{6,4},{7,5},{8,10},{9,11},{10,... | collective-permute-start | bytes 1105928 | tf_op jit(solution)/shard_map/ppermute | solution.py:305
  23.0 1.9 %collective-permute-done.4.refs_1_ = bf16[160,512]{1,0:T(8,128)(2,1)S(1)} collective-permute-done((bf16[160,512]{1,0:T(8,128)(2,1)S(1)}, bf16[160,512]{1,0:T(8,128)(2,1)S(1)}, u32[]{:S(2)}, u32[]{:S(2)}) %collective-permute-start.4) | collective-permute-done | bytes 163872 | tf_op jit(solution)/shard_map/ppermute | solution.py:305
  26.1 3.8 %collective-permute-start.9 = (bf16[160,512]{1,0:T(8,128)(2,1)S(1)}, bf16[160,512]{1,0:T(8,128)(2,1)S(1)}, u32[]{:S(2)}, u32[]{:S(2)}) collective-permute-start(bf16[160,512]{1,0:T(8,128)(2,1)S(1)} %get-tuple-element.78), channel_id=1, source_target_pairs={{0,3},{1,2},{2,1},{3,0},{4,7},{5,6},{6,5},{7,4},{8,11},{9,10},{10,... | collective-permute-start | bytes 491528 | tf_op jit(solution)/shard_map/ppermute | solution.py:305
  30.0 8.5 %collective-permute-done.6.refs_1_ = bf16[9,128,384]{2,1,0:T(8,128)(2,1)S(1)} collective-permute-done((bf16[9,128,384]{2,1,0:T(8,128)(2,1)S(1)}, bf16[9,128,384]{2,1,0:T(8,128)(2,1)S(1)}, u32[]{:S(2)}, u32[]{:S(2)}) %collective-permute-start.6) | collective-permute-done | bytes 884768 | tf_op jit(solution)/shard_map/ppermute | solution.py:305
  40.6 1.6 %collective-permute-start.16 = (bf16[160,1152]{1,0:T(8,128)(2,1)S(1)}, bf16[160,1152]{1,0:T(8,128)(2,1)S(1)}, u32[]{:S(2)}, u32[]{:S(2)}) collective-permute-start(bf16[160,1152]{1,0:T(8,128)(2,1)S(1)} %shard_map.126), channel_id=1, source_target_pairs={{0,1},{1,0},{2,3},{3,2},{4,5},{5,4},{6,7},{7,6},{8,9},{9,8},{10,11... | collective-permute-start | bytes 1105928 | tf_op jit(solution)/shard_map/ppermute | solution.py:305
  42.3 2.9 %collective-permute-done.9.refs_3_ = bf16[160,512]{1,0:T(8,128)(2,1)S(1)} collective-permute-done((bf16[160,512]{1,0:T(8,128)(2,1)S(1)}, bf16[160,512]{1,0:T(8,128)(2,1)S(1)}, u32[]{:S(2)}, u32[]{:S(2)}) %collective-permute-start.9) | collective-permute-done | bytes 163872 | tf_op jit(solution)/shard_map/ppermute | solution.py:305
  45.1 2.9 %collective-permute-start.10 = (bf16[160,512]{1,0:T(8,128)(2,1)S(1)}, bf16[160,512]{1,0:T(8,128)(2,1)S(1)}, u32[]{:S(2)}, u32[]{:S(2)}) collective-permute-start(bf16[160,512]{1,0:T(8,128)(2,1)S(1)} %get-tuple-element.79), channel_id=1, source_target_pairs={{0,2},{1,3},{2,0},{3,1},{4,6},{5,7},{6,4},{7,5},{8,10},{9,11},{10,... | collective-permute-start | bytes 491528 | tf_op jit(solution)/shard_map/ppermute | solution.py:305
  48.2 8.1 %collective-permute-done.10.refs_2_ = bf16[160,512]{1,0:T(8,128)(2,1)S(1)} collective-permute-done((bf16[160,512]{1,0:T(8,128)(2,1)S(1)}, bf16[160,512]{1,0:T(8,128)(2,1)S(1)}, u32[]{:S(2)}, u32[]{:S(2)}) %collective-permute-start.10) | collective-permute-done | bytes 163872 | tf_op jit(solution)/shard_map/ppermute | solution.py:305
  56.4 1.4 %collective-permute-done.12.refs_6_ = bf16[160,512]{1,0:T(8,128)(2,1)S(1)} collective-permute-done((bf16[160,512]{1,0:T(8,128)(2,1)S(1)}, bf16[160,512]{1,0:T(8,128)(2,1)S(1)}, u32[]{:S(2)}, u32[]{:S(2)}) %collective-permute-start.12) | collective-permute-done | bytes 163872 | tf_op jit(solution)/shard_map/ppermute | solution.py:305
  57.8 1.5 %shard_map.127 = (bf16[4,128,384]{2,1,0:T(8,128)(2,1)S(1)}, bf16[3,128,384]{2,1,0:T(8,128)(2,1)S(1)}) custom-call(s32[4,4]{1,0:T(4,128)S(1)} %copy-done.6, bf16[4,160,512]{2,1,0:T(8,128)(2,1)S(1)} %get-tuple-element.63.mine_ref.refs_0_, bf16[160,512]{1,0:T(8,128)(2,1)S(1)} %collective-permute-done.4.refs_1_, ...), custom_call_target="tpu_custom_call" | custom-call | flops 377487360 | bytes 2293760 | tf_op jit(solution)/shard_map/pallas_call | solution.py:441
  59.3 1.6 %collective-permute-start.17 = (bf16[4,128,384]{2,1,0:T(8,128)(2,1)S(1)}, bf16[4,128,384]{2,1,0:T(8,128)(2,1)S(1)}, u32[]{:S(2)}, u32[]{:S(2)}) collective-permute-start(bf16[4,128,384]{2,1,0:T(8,128)(2,1)S(1)} %get-tuple-element.82), channel_id=1, source_target_pairs={{0,24},{8,16},{16,8},{24,0},{1,25},{9,17},{17,9},{25,1},{2,26},{10... | collective-permute-start | bytes 1179656 | tf_op jit(solution)/shard_map/ppermute | solution.py:305
  60.9 1.5 %shard_map.129 = (bf16[3,128,384]{2,1,0:T(8,128)(2,1)S(1)}, bf16[3,128,384]{2,1,0:T(8,128)(2,1)S(1)}) custom-call(s32[4,4]{1,0:T(4,128)S(1)} %copy-done.6, bf16[4,160,512]{2,1,0:T(8,128)(2,1)S(1)} %get-tuple-element.63.mine_ref.refs_0_, bf16[160,512]{1,0:T(8,128)(2,1)S(1)} %collective-permute-done.4.refs_1_, ...), custom_call_target="tpu_custom_call" | custom-call | flops 377487360 | bytes 2293760 | tf_op jit(solution)/shard_map/pallas_call | solution.py:441
  62.4 1.6 %collective-permute-start.18 = (bf16[3,128,384]{2,1,0:T(8,128)(2,1)S(1)}, bf16[3,128,384]{2,1,0:T(8,128)(2,1)S(1)}, u32[]{:S(2)}, u32[]{:S(2)}) collective-permute-start(bf16[3,128,384]{2,1,0:T(8,128)(2,1)S(1)} %get-tuple-element.83), channel_id=1, source_target_pairs={{0,8},{8,0},{16,24},{24,16},{1,9},{9,1},{17,25},{25,17},{2,10},{10... | collective-permute-start | bytes 884744 | tf_op jit(solution)/shard_map/ppermute | solution.py:305
  64.5 1.3 %shard_map.130 = (f32[4,3,128,384]{3,2,1,0:T(8,128)}, bf16[4,3,128,384]{3,2,1,0:T(8,128)(2,1)}, bf16[4,3,128,384]{3,2,1,0:T(8,128)(2,1)}) custom-call(bf16[3,128,384]{2,1,0:T(8,128)(2,1)S(1)} %get-tuple-element.85.refs_0_, bf16[9,128,384]{2,1,0:T(8,128)(2,1)S(1)} %get-tuple-element.86.refs_1_), custom_call_target="tpu_custom_call" | custom-call | flops 2949120 | bytes 2359296 | tf_op jit(solution)/shard_map/pallas_call | solution.py:289
  65.8 6.5 %collective-permute-done.17.refs_3_.refs_0_ = bf16[4,128,384]{2,1,0:T(8,128)(2,1)S(1)} collective-permute-done((bf16[4,128,384]{2,1,0:T(8,128)(2,1)S(1)}, bf16[4,128,384]{2,1,0:T(8,128)(2,1)S(1)}, u32[]{:S(2)}, u32[]{:S(2)}) %collective-permute-start.17) | collective-permute-done | bytes 393248 | tf_op jit(solution)/shard_map/ppermute | solution.py:305
  74.6 3.2 %collective-permute-done.18.refs_0_ = bf16[3,128,384]{2,1,0:T(8,128)(2,1)S(1)} collective-permute-done((bf16[3,128,384]{2,1,0:T(8,128)(2,1)S(1)}, bf16[3,128,384]{2,1,0:T(8,128)(2,1)S(1)}, u32[]{:S(2)}, u32[]{:S(2)}) %collective-permute-start.18) | collective-permute-done | bytes 294944 | tf_op jit(solution)/shard_map/ppermute | solution.py:305
  77.9 2.0 %shard_map.132 = (f32[4,3,128,384]{3,2,1,0:T(8,128)}, bf16[4,3,128,384]{3,2,1,0:T(8,128)(2,1)}, bf16[4,3,128,384]{3,2,1,0:T(8,128)(2,1)}) custom-call(bf16[3,128,384]{2,1,0:T(8,128)(2,1)S(1)} %collective-permute-done.18.refs_0_, bf16[10,128,384]{2,1,0:T(8,128)(2,1)S(1)} %collective-permute-done.7.refs_1_, ...), custom_call_target="tpu_custom_call", output_to_operand_aliasing={{0}: (4, {}), {1}: (5, {}), {2}: (6, {})} | custom-call | flops 5898240 | bytes 4718592 | tf_op jit(solution)/shard_map/pallas_call | solution.py:289
  (44 shorter events, 10.0 us)
Async XLA Ops:
  3.0 9.0 %collective-permute-start = (bf16[4,40,512]{2,1,0:T(8,128)(2,1)}, bf16[4,40,512]{2,1,0:T(8,128)(2,1)S(1)}, u32[]{:S(2)}, u32[]{:S(2)}) collective-permute-start(bf16[4,40,512]{2,1,0:T(8,128)(2,1)} %get-tuple-element.52), channel_id=1, source_target_pairs={{0,8},{8,0},{16,24},{24,16},{1,9},{9,1},{17,25},{25,17},{2,10},{10... | collective-permute-start | bytes 491528 | tf_op jit(solution)/shard_map/ppermute | solution.py:305
  6.0 9.4 %collective-permute-start.1 = (bf16[4,40,512]{2,1,0:T(8,128)(2,1)}, bf16[4,40,512]{2,1,0:T(8,128)(2,1)S(1)}, u32[]{:S(2)}, u32[]{:S(2)}) collective-permute-start(bf16[4,40,512]{2,1,0:T(8,128)(2,1)} %get-tuple-element.53), channel_id=1, source_target_pairs={{0,16},{8,24},{16,0},{24,8},{1,17},{9,25},{17,1},{25,9},{2,18},{10... | collective-permute-start | bytes 491528 | tf_op jit(solution)/shard_map/ppermute | solution.py:305
  7.5 7.9 %collective-permute-start.2 = (bf16[4,40,512]{2,1,0:T(8,128)(2,1)}, bf16[4,40,512]{2,1,0:T(8,128)(2,1)S(1)}, u32[]{:S(2)}, u32[]{:S(2)}) collective-permute-start(bf16[4,40,512]{2,1,0:T(8,128)(2,1)} %get-tuple-element.54), channel_id=1, source_target_pairs={{0,24},{8,16},{16,8},{24,0},{1,25},{9,17},{17,9},{25,1},{2,26},{10... | collective-permute-start | bytes 491528 | tf_op jit(solution)/shard_map/ppermute | solution.py:305
  7.6 3.3 %copy-start.3 = (bf16[1,512,3,384]{3,1,2,0:T(8,128)(2,1)S(1)}, bf16[1,512,3,384]{3,1,2,0:T(8,128)(2,1)}, u32[]{:S(2)}) copy-start(bf16[1,512,3,384]{3,1,2,0:T(8,128)(2,1)} %param.16) | copy-start | bytes 3538948
  7.6 3.3 %copy-start.6 = (s32[4,4]{1,0:T(4,128)S(1)}, s32[4,4]{1,0:T(4,128)}, u32[]{:S(2)}) copy-start(s32[4,4]{1,0:T(4,128)} %owner_ref.5) | copy-start | bytes 196
  10.8 4.6 %copy-start.4 = (bf16[4,40,512]{2,1,0:T(8,128)(2,1)S(1)}, bf16[4,40,512]{2,1,0:T(8,128)(2,1)}, u32[]{:S(2)}) copy-start(bf16[4,40,512]{2,1,0:T(8,128)(2,1)} %get-tuple-element.59.refs_0_) | copy-start | bytes 491524
  10.8 7.9 %copy-start.1 = (bf16[1,2048,384]{2,1,0:T(8,128)(2,1)S(1)}, bf16[1,2048,384]{2,1,0:T(8,128)(2,1)}, u32[]{:S(2)}) copy-start(bf16[1,2048,384]{2,1,0:T(8,128)(2,1)} %param.13) | copy-start | bytes 4718596
  15.5 3.2 %collective-permute-start.3 = (bf16[4,160,512]{2,1,0:T(8,128)(2,1)S(1)}, bf16[4,160,512]{2,1,0:T(8,128)(2,1)S(1)}, u32[]{:S(2)}, u32[]{:S(2)}) collective-permute-start(bf16[4,160,512]{2,1,0:T(8,128)(2,1)S(1)} %get-tuple-element.63.mine_ref.refs_0_), channel_id=1, source_target_pairs={{0,4},{4,0},{1,5},{5,1},{2,6},{6,2},{3,7},{7,3},{8,12},{12,8},{9,1... | collective-permute-start | bytes 1966088 | tf_op jit(solution)/shard_map/ppermute | solution.py:305
  15.6 23.0 %collective-permute-start.6 = (bf16[9,128,384]{2,1,0:T(8,128)(2,1)S(1)}, bf16[9,128,384]{2,1,0:T(8,128)(2,1)S(1)}, u32[]{:S(2)}, u32[]{:S(2)}) collective-permute-start(bf16[9,128,384]{2,1,0:T(8,128)(2,1)S(1)} %get-tuple-element.73), channel_id=1, source_target_pairs={{0,24},{8,16},{16,8},{24,0},{1,25},{9,17},{17,9},{25,1},{2,26},{10... | collective-permute-start | bytes 2654216 | tf_op jit(solution)/shard_map/ppermute | solution.py:305
  17.1 7.7 %collective-permute-start.4 = (bf16[160,512]{1,0:T(8,128)(2,1)S(1)}, bf16[160,512]{1,0:T(8,128)(2,1)S(1)}, u32[]{:S(2)}, u32[]{:S(2)}) collective-permute-start(bf16[160,512]{1,0:T(8,128)(2,1)S(1)} %get-tuple-element.65), channel_id=1, source_target_pairs={{0,1},{1,0},{2,3},{3,2},{4,5},{5,4},{6,7},{7,6},{8,9},{9,8},{10,11... | collective-permute-start | bytes 491528 | tf_op jit(solution)/shard_map/ppermute | solution.py:305
  19.8 20.8 %collective-permute-start.15 = (bf16[160,1152]{1,0:T(8,128)(2,1)S(1)}, bf16[160,1152]{1,0:T(8,128)(2,1)S(1)}, u32[]{:S(2)}, u32[]{:S(2)}) collective-permute-start(bf16[160,1152]{1,0:T(8,128)(2,1)S(1)} %shard_map.123.pair_ref.refs_8_), channel_id=1, source_target_pairs={{0,2},{1,3},{2,0},{3,1},{4,6},{5,7},{6,4},{7,5},{8,10},{9,11},{10,... | collective-permute-start | bytes 1105928 | tf_op jit(solution)/shard_map/ppermute | solution.py:305
  22.4 18.1 %collective-permute-start.14 = (bf16[160,1152]{1,0:T(8,128)(2,1)S(1)}, bf16[160,1152]{1,0:T(8,128)(2,1)S(1)}, u32[]{:S(2)}, u32[]{:S(2)}) collective-permute-start(bf16[160,1152]{1,0:T(8,128)(2,1)S(1)} %shard_map.123.pair_ref.refs_8_), channel_id=1, source_target_pairs={{0,1},{1,0},{2,3},{3,2},{4,5},{5,4},{6,7},{7,6},{8,9},{9,8},{10,11... | collective-permute-start | bytes 1105928 | tf_op jit(solution)/shard_map/ppermute | solution.py:305
  26.0 3.9 %collective-permute-start.5 = (bf16[160,1024]{1,0:T(8,128)(2,1)S(1)}, bf16[160,1024]{1,0:T(8,128)(2,1)S(1)}, u32[]{:S(2)}, u32[]{:S(2)}) collective-permute-start(bf16[160,1024]{1,0:T(8,128)(2,1)S(1)} %get-tuple-element.68), channel_id=1, source_target_pairs={{0,4},{4,0},{1,5},{5,1},{2,6},{6,2},{3,7},{7,3},{8,12},{12,8},{9,1... | collective-permute-start | bytes 983048 | tf_op jit(solution)/shard_map/ppermute | solution.py:305
  26.1 19.1 %collective-permute-start.9 = (bf16[160,512]{1,0:T(8,128)(2,1)S(1)}, bf16[160,512]{1,0:T(8,128)(2,1)S(1)}, u32[]{:S(2)}, u32[]{:S(2)}) collective-permute-start(bf16[160,512]{1,0:T(8,128)(2,1)S(1)} %get-tuple-element.78), channel_id=1, source_target_pairs={{0,3},{1,2},{2,1},{3,0},{4,7},{5,6},{6,5},{7,4},{8,11},{9,10},{10,... | collective-permute-start | bytes 491528 | tf_op jit(solution)/shard_map/ppermute | solution.py:305
  38.5 35.1 %collective-permute-start.7 = (bf16[10,128,384]{2,1,0:T(8,128)(2,1)S(1)}, bf16[10,128,384]{2,1,0:T(8,128)(2,1)S(1)}, u32[]{:S(2)}, u32[]{:S(2)}) collective-permute-start(bf16[10,128,384]{2,1,0:T(8,128)(2,1)S(1)} %get-tuple-element.74), channel_id=1, source_target_pairs={{0,8},{8,0},{16,24},{24,16},{1,9},{9,1},{17,25},{25,17},{2,10},{10... | collective-permute-start | bytes 2949128 | tf_op jit(solution)/shard_map/ppermute | solution.py:305
  39.7 33.9 %collective-permute-start.8 = (bf16[10,128,384]{2,1,0:T(8,128)(2,1)S(1)}, bf16[10,128,384]{2,1,0:T(8,128)(2,1)S(1)}, u32[]{:S(2)}, u32[]{:S(2)}) collective-permute-start(bf16[10,128,384]{2,1,0:T(8,128)(2,1)S(1)} %get-tuple-element.76), channel_id=1, source_target_pairs={{0,16},{8,24},{16,0},{24,8},{1,17},{9,25},{17,1},{25,9},{2,18},{10... | collective-permute-start | bytes 2949128 | tf_op jit(solution)/shard_map/ppermute | solution.py:305
  40.6 17.2 %collective-permute-start.16 = (bf16[160,1152]{1,0:T(8,128)(2,1)S(1)}, bf16[160,1152]{1,0:T(8,128)(2,1)S(1)}, u32[]{:S(2)}, u32[]{:S(2)}) collective-permute-start(bf16[160,1152]{1,0:T(8,128)(2,1)S(1)} %shard_map.126), channel_id=1, source_target_pairs={{0,1},{1,0},{2,3},{3,2},{4,5},{5,4},{6,7},{7,6},{8,9},{9,8},{10,11... | collective-permute-start | bytes 1105928 | tf_op jit(solution)/shard_map/ppermute | solution.py:305
  45.1 2.9 %collective-permute-start.11 = (bf16[160,512]{1,0:T(8,128)(2,1)S(1)}, bf16[160,512]{1,0:T(8,128)(2,1)S(1)}, u32[]{:S(2)}, u32[]{:S(2)}) collective-permute-start(bf16[160,512]{1,0:T(8,128)(2,1)S(1)} %collective-permute-done.4.refs_1_), channel_id=1, source_target_pairs={{0,4},{4,0},{1,5},{5,1},{2,6},{6,2},{3,7},{7,3},{8,12},{12,8},{9,1... | collective-permute-start | bytes 491528 | tf_op jit(solution)/shard_map/ppermute | solution.py:305
  45.1 11.2 %collective-permute-start.10 = (bf16[160,512]{1,0:T(8,128)(2,1)S(1)}, bf16[160,512]{1,0:T(8,128)(2,1)S(1)}, u32[]{:S(2)}, u32[]{:S(2)}) collective-permute-start(bf16[160,512]{1,0:T(8,128)(2,1)S(1)} %get-tuple-element.79), channel_id=1, source_target_pairs={{0,2},{1,3},{2,0},{3,1},{4,6},{5,7},{6,4},{7,5},{8,10},{9,11},{10,... | collective-permute-start | bytes 491528 | tf_op jit(solution)/shard_map/ppermute | solution.py:305
  48.0 8.4 %collective-permute-start.13 = (bf16[160,512]{1,0:T(8,128)(2,1)S(1)}, bf16[160,512]{1,0:T(8,128)(2,1)S(1)}, u32[]{:S(2)}, u32[]{:S(2)}) collective-permute-start(bf16[160,512]{1,0:T(8,128)(2,1)S(1)} %collective-permute-done.9.refs_3_), channel_id=1, source_target_pairs={{0,4},{4,0},{1,5},{5,1},{2,6},{6,2},{3,7},{7,3},{8,12},{12,8},{9,1... | collective-permute-start | bytes 491528 | tf_op jit(solution)/shard_map/ppermute | solution.py:305
  56.4 1.4 %collective-permute-start.12 = (bf16[160,512]{1,0:T(8,128)(2,1)S(1)}, bf16[160,512]{1,0:T(8,128)(2,1)S(1)}, u32[]{:S(2)}, u32[]{:S(2)}) collective-permute-start(bf16[160,512]{1,0:T(8,128)(2,1)S(1)} %collective-permute-done.10.refs_2_), channel_id=1, source_target_pairs={{0,4},{4,0},{1,5},{5,1},{2,6},{6,2},{3,7},{7,3},{8,12},{12,8},{9,1... | collective-permute-start | bytes 491528 | tf_op jit(solution)/shard_map/ppermute | solution.py:305
  59.3 13.0 %collective-permute-start.17 = (bf16[4,128,384]{2,1,0:T(8,128)(2,1)S(1)}, bf16[4,128,384]{2,1,0:T(8,128)(2,1)S(1)}, u32[]{:S(2)}, u32[]{:S(2)}) collective-permute-start(bf16[4,128,384]{2,1,0:T(8,128)(2,1)S(1)} %get-tuple-element.82), channel_id=1, source_target_pairs={{0,24},{8,16},{16,8},{24,0},{1,25},{9,17},{17,9},{25,1},{2,26},{10... | collective-permute-start | bytes 1179656 | tf_op jit(solution)/shard_map/ppermute | solution.py:305
  62.4 15.5 %collective-permute-start.18 = (bf16[3,128,384]{2,1,0:T(8,128)(2,1)S(1)}, bf16[3,128,384]{2,1,0:T(8,128)(2,1)S(1)}, u32[]{:S(2)}, u32[]{:S(2)}) collective-permute-start(bf16[3,128,384]{2,1,0:T(8,128)(2,1)S(1)} %get-tuple-element.83), channel_id=1, source_target_pairs={{0,8},{8,0},{16,24},{24,16},{1,9},{9,1},{17,25},{25,17},{2,10},{10... | collective-permute-start | bytes 884744 | tf_op jit(solution)/shard_map/ppermute | solution.py:305
  64.0 13.9 %collective-permute-start.19 = (bf16[3,128,384]{2,1,0:T(8,128)(2,1)S(1)}, bf16[3,128,384]{2,1,0:T(8,128)(2,1)S(1)}, u32[]{:S(2)}, u32[]{:S(2)}) collective-permute-start(bf16[3,128,384]{2,1,0:T(8,128)(2,1)S(1)} %get-tuple-element.84), channel_id=1, source_target_pairs={{0,16},{8,24},{16,0},{24,8},{1,17},{9,25},{17,1},{25,9},{2,18},{10... | collective-permute-start | bytes 884744 | tf_op jit(solution)/shard_map/ppermute | solution.py:305
  (3 other events, 7.0 us)

commit v5 on v4

--- a/solution.py
+++ b/solution.py
@@ -90,7 +90,7 @@
 
 
 def collect_kernel(experts, dp_count, *refs):
-    got, whole, parts = refs[:experts], refs[experts], refs[experts + 1 :]
+    got, whole, parts = refs[:experts][::-1], refs[experts], refs[experts + 1 :]
     part = lax.axis_index("dp")
     for q in range(dp_count):
         joined = jnp.concatenate([got[k][q].astype(F32) for k in range(experts)], axis=0)
@@ -368,7 +368,7 @@
         ],
         moved=14 * shard_rows * 3 * units,
     )(new_owner, *stored)
-    got, states, gate_up = lax.optimization_barrier((got, states, gate_up))
+    got, states, gate_up = lax.optimization_barrier((got[::-1], states, gate_up))
     states = dict(zip(groups, states))
 
     def send_states(some, *others):
@@ -424,7 +424,8 @@
 
     hiddens = {0: hidden, 2: exchange(hidden, "dp", 2, dp_count)}
     hiddens[1] = exchange(hidden, "dp", 1, dp_count)
-    send_states(carriers, sent_states)
+    send_states(carriers[:1])
+    send_states(carriers[1:], sent_states)
     passed = call(pass_kernel, shape(*hidden.shape), 1, flops=PASS_FLOPS)(
         after(hiddens[2], hiddens[1], rows[1])
     )

time: 80 us -> 79.7 us (level)
  waiting for transfers between devices: 35.9 us -> 32.8 us
  starting transfers between devices: 25.2 us -> 28 us
    ppermute x20, waiting for transfers between devices: 35.9 us -> 32.8 us  [exchange(): return lax.ppermute(tensor, axis, [(i, i ^ k) for i in range(count)])]
    ppermute x20, starting transfers between devices: 25.2 us -> 28 us  [exchange(): return lax.ppermute(tensor, axis, [(i, i ^ k) for i in range(count)])]
  transfers between devices with their start and end apart: 20 -> 20, of which waited for: 8 -> 11; matrix products, arithmetic and copies ran while one was open for 3% -> 3% of each run, Pallas kernels for 13% -> 13%
where the time goes in v5:
time: 79.7 us; the launch traced here: 79.5 us
  waiting for transfers between devices  32.8 us (41%)
  starting transfers between devices  28 us (35%)
  Pallas kernels  14.7 us (18%)
  local copies, waits for them, and re-layouts  3.28 us (4%)
    ppermute x20, waiting for transfers between devices, exchange(): return lax.ppermute(tensor, axis, [(i, i ^ k) for i in range(count)])  32.8 us
    ppermute x20, starting transfers between devices, exchange(): return lax.ppermute(tensor, axis, [(i, i ^ k) for i in range(count)])  28 us
    pallas_call x3, Pallas kernels, adam_step(): pl.pallas_call(functools.partial(adam_kernel, [(k, places) for k, places,...  4.65 us
    unnamed x15, local copies, waits for them, and re-layouts  3.28 us
    pallas_call x2, Pallas kernels, aligned_local(): call(functools.partial(weight_kernel, experts, dp_count, ks, some), [shap...  3.04 us
    pallas_call x1, Pallas kernels, aligned_local(): call(functools.partial(dispatch_kernel, experts, capacity, dp_count), [sh...  2.36 us
  transfers between devices with their start and end apart: 20, of which 11 were waited for; matrix products, arithmetic and copies ran while one was open for 3% of the time, Pallas kernels for 13%

profile of v5, /device:TPU:0, one launch (start us, length us, event | category | flops | bytes accessed | tf_op | source)
XLA Modules:
  0.0 79.5 jit_solution(1141912641257629451)
XLA Ops:
  0.6 2.4 %shard_map.120 = (bf16[4,40,512]{2,1,0:T(8,128)(2,1)}, bf16[4,40,512]{2,1,0:T(8,128)(2,1)}, bf16[4,40,512]{2,1,0:T(8,128)(2,1)}, bf16[4,40,512]{2,1,0:T(8,128)(2,1)}, bf16[160,128]{1,0:T(8,128)(2,1)}) custom-call(s32[1,128]{1,0:T(1,128)} %bitcast.33, bf16[128,2048]{1,0:T(8,128)(2,1)} %in_any.1, bf16[128,2048]{1,0:T(8,128)(2,1)} %grad_any.1), custom_call_target="tpu_custom_call" | custom-call | flops 83886080 | bytes 1835008 | tf_op jit(solution)/shard_map/pallas_call | solution.py:337
  3.0 4.0 %collective-permute-start = (bf16[4,40,512]{2,1,0:T(8,128)(2,1)}, bf16[4,40,512]{2,1,0:T(8,128)(2,1)S(1)}, u32[]{:S(2)}, u32[]{:S(2)}) collective-permute-start(bf16[4,40,512]{2,1,0:T(8,128)(2,1)} %get-tuple-element.50), channel_id=1, source_target_pairs={{0,24},{8,16},{16,8},{24,0},{1,25},{9,17},{17,9},{25,1},{2,26},{10... | collective-permute-start | bytes 491528 | tf_op jit(solution)/shard_map/ppermute | solution.py:305
  7.6 2.7 %copy.21 = bf16[256,8,2,384]{3,1,2,0:T(8,128)(2,1)S(1)} copy(bf16[256,8,2,384]{3,2,1,0:T(2,128)(2,1)} %bitcast.32) | data formatting | bytes 6291456
  12.2 2.7 %collective-permute-done.1.refs_1_ = bf16[4,40,512]{2,1,0:T(8,128)(2,1)S(1)} collective-permute-done((bf16[4,40,512]{2,1,0:T(8,128)(2,1)}, bf16[4,40,512]{2,1,0:T(8,128)(2,1)S(1)}, u32[]{:S(2)}, u32[]{:S(2)}) %collective-permute-start.1) | collective-permute-done | bytes 163872 | tf_op jit(solution)/shard_map/ppermute | solution.py:305
  15.3 1.6 %collective-permute-start.7 = (bf16[9,128,384]{2,1,0:T(8,128)(2,1)S(1)}, bf16[9,128,384]{2,1,0:T(8,128)(2,1)S(1)}, u32[]{:S(2)}, u32[]{:S(2)}) collective-permute-start(bf16[9,128,384]{2,1,0:T(8,128)(2,1)S(1)} %get-tuple-element.73), channel_id=1, source_target_pairs={{0,24},{8,16},{16,8},{24,0},{1,25},{9,17},{17,9},{25,1},{2,26},{10... | collective-permute-start | bytes 2654216 | tf_op jit(solution)/shard_map/ppermute | solution.py:305
  16.9 1.7 %collective-permute-start.4 = (bf16[160,512]{1,0:T(8,128)(2,1)S(1)}, bf16[160,512]{1,0:T(8,128)(2,1)S(1)}, u32[]{:S(2)}, u32[]{:S(2)}) collective-permute-start(bf16[160,512]{1,0:T(8,128)(2,1)S(1)} %get-tuple-element.64), channel_id=1, source_target_pairs={{0,1},{1,0},{2,3},{3,2},{4,5},{5,4},{6,7},{7,6},{8,9},{9,8},{10,11... | collective-permute-start | bytes 491528 | tf_op jit(solution)/shard_map/ppermute | solution.py:305
  19.7 2.7 %collective-permute-start.15 = (bf16[160,1152]{1,0:T(8,128)(2,1)S(1)}, bf16[160,1152]{1,0:T(8,128)(2,1)S(1)}, u32[]{:S(2)}, u32[]{:S(2)}) collective-permute-start(bf16[160,1152]{1,0:T(8,128)(2,1)S(1)} %shard_map.123.pair_ref.refs_8_), channel_id=1, source_target_pairs={{0,2},{1,3},{2,0},{3,1},{4,6},{5,7},{6,4},{7,5},{8,10},{9,11},{10,... | collective-permute-start | bytes 1105928 | tf_op jit(solution)/shard_map/ppermute | solution.py:305
  24.5 5.5 %collective-permute-start.9 = (bf16[160,512]{1,0:T(8,128)(2,1)S(1)}, bf16[160,512]{1,0:T(8,128)(2,1)S(1)}, u32[]{:S(2)}, u32[]{:S(2)}) collective-permute-start(bf16[160,512]{1,0:T(8,128)(2,1)S(1)} %get-tuple-element.76), channel_id=1, source_target_pairs={{0,3},{1,2},{2,1},{3,0},{4,7},{5,6},{6,5},{7,4},{8,11},{9,10},{10,... | collective-permute-start | bytes 491528 | tf_op jit(solution)/shard_map/ppermute | solution.py:305
  30.1 8.2 %collective-permute-done.7.refs_1_ = bf16[9,128,384]{2,1,0:T(8,128)(2,1)S(1)} collective-permute-done((bf16[9,128,384]{2,1,0:T(8,128)(2,1)S(1)}, bf16[9,128,384]{2,1,0:T(8,128)(2,1)S(1)}, u32[]{:S(2)}, u32[]{:S(2)}) %collective-permute-start.7) | collective-permute-done | bytes 884768 | tf_op jit(solution)/shard_map/ppermute | solution.py:305
  38.3 1.4 %collective-permute-start.8 = (bf16[10,128,384]{2,1,0:T(8,128)(2,1)S(1)}, bf16[10,128,384]{2,1,0:T(8,128)(2,1)S(1)}, u32[]{:S(2)}, u32[]{:S(2)}) collective-permute-start(bf16[10,128,384]{2,1,0:T(8,128)(2,1)S(1)} %get-tuple-element.74), channel_id=1, source_target_pairs={{0,16},{8,24},{16,0},{24,8},{1,17},{9,25},{17,1},{25,9},{2,18},{10... | collective-permute-start | bytes 2949128 | tf_op jit(solution)/shard_map/ppermute | solution.py:305
  40.4 1.8 %collective-permute-start.16 = (bf16[160,1152]{1,0:T(8,128)(2,1)S(1)}, bf16[160,1152]{1,0:T(8,128)(2,1)S(1)}, u32[]{:S(2)}, u32[]{:S(2)}) collective-permute-start(bf16[160,1152]{1,0:T(8,128)(2,1)S(1)} %shard_map.126), channel_id=1, source_target_pairs={{0,1},{1,0},{2,3},{3,2},{4,5},{5,4},{6,7},{7,6},{8,9},{9,8},{10,11... | collective-permute-start | bytes 1105928 | tf_op jit(solution)/shard_map/ppermute | solution.py:305
  42.2 2.9 %collective-permute-done.9.refs_3_ = bf16[160,512]{1,0:T(8,128)(2,1)S(1)} collective-permute-done((bf16[160,512]{1,0:T(8,128)(2,1)S(1)}, bf16[160,512]{1,0:T(8,128)(2,1)S(1)}, u32[]{:S(2)}, u32[]{:S(2)}) %collective-permute-start.9) | collective-permute-done | bytes 163872 | tf_op jit(solution)/shard_map/ppermute | solution.py:305
  45.1 2.7 %collective-permute-start.10 = (bf16[160,512]{1,0:T(8,128)(2,1)S(1)}, bf16[160,512]{1,0:T(8,128)(2,1)S(1)}, u32[]{:S(2)}, u32[]{:S(2)}) collective-permute-start(bf16[160,512]{1,0:T(8,128)(2,1)S(1)} %get-tuple-element.77), channel_id=1, source_target_pairs={{0,2},{1,3},{2,0},{3,1},{4,6},{5,7},{6,4},{7,5},{8,10},{9,11},{10,... | collective-permute-start | bytes 491528 | tf_op jit(solution)/shard_map/ppermute | solution.py:305
  48.0 6.4 %collective-permute-done.10.refs_2_ = bf16[160,512]{1,0:T(8,128)(2,1)S(1)} collective-permute-done((bf16[160,512]{1,0:T(8,128)(2,1)S(1)}, bf16[160,512]{1,0:T(8,128)(2,1)S(1)}, u32[]{:S(2)}, u32[]{:S(2)}) %collective-permute-start.10) | collective-permute-done | bytes 163872 | tf_op jit(solution)/shard_map/ppermute | solution.py:305
  54.5 1.4 %collective-permute-done.12.refs_6_ = bf16[160,512]{1,0:T(8,128)(2,1)S(1)} collective-permute-done((bf16[160,512]{1,0:T(8,128)(2,1)S(1)}, bf16[160,512]{1,0:T(8,128)(2,1)S(1)}, u32[]{:S(2)}, u32[]{:S(2)}) %collective-permute-start.12) | collective-permute-done | bytes 163872 | tf_op jit(solution)/shard_map/ppermute | solution.py:305
  56.2 1.5 %shard_map.127 = (bf16[4,128,384]{2,1,0:T(8,128)(2,1)S(1)}, bf16[3,128,384]{2,1,0:T(8,128)(2,1)S(1)}) custom-call(s32[4,4]{1,0:T(4,128)S(1)} %copy-done.6, bf16[4,160,512]{2,1,0:T(8,128)(2,1)S(1)} %get-tuple-element.62.mine_ref.refs_0_, bf16[160,512]{1,0:T(8,128)(2,1)S(1)} %collective-permute-done.4.refs_1_, ...), custom_call_target="tpu_custom_call" | custom-call | flops 377487360 | bytes 2293760 | tf_op jit(solution)/shard_map/pallas_call | solution.py:442
  57.7 3.1 %collective-permute-start.17 = (bf16[4,128,384]{2,1,0:T(8,128)(2,1)S(1)}, bf16[4,128,384]{2,1,0:T(8,128)(2,1)S(1)}, u32[]{:S(2)}, u32[]{:S(2)}) collective-permute-start(bf16[4,128,384]{2,1,0:T(8,128)(2,1)S(1)} %get-tuple-element.80), channel_id=1, source_target_pairs={{0,24},{8,16},{16,8},{24,0},{1,25},{9,17},{17,9},{25,1},{2,26},{10... | collective-permute-start | bytes 1179656 | tf_op jit(solution)/shard_map/ppermute | solution.py:305
  60.8 1.5 %shard_map.129 = (bf16[3,128,384]{2,1,0:T(8,128)(2,1)S(1)}, bf16[3,128,384]{2,1,0:T(8,128)(2,1)S(1)}) custom-call(s32[4,4]{1,0:T(4,128)S(1)} %copy-done.6, bf16[4,160,512]{2,1,0:T(8,128)(2,1)S(1)} %get-tuple-element.62.mine_ref.refs_0_, bf16[160,512]{1,0:T(8,128)(2,1)S(1)} %collective-permute-done.4.refs_1_, ...), custom_call_target="tpu_custom_call" | custom-call | flops 377487360 | bytes 2293760 | tf_op jit(solution)/shard_map/pallas_call | solution.py:442
  62.4 1.3 %collective-permute-start.18 = (bf16[3,128,384]{2,1,0:T(8,128)(2,1)S(1)}, bf16[3,128,384]{2,1,0:T(8,128)(2,1)S(1)}, u32[]{:S(2)}, u32[]{:S(2)}) collective-permute-start(bf16[3,128,384]{2,1,0:T(8,128)(2,1)S(1)} %get-tuple-element.81), channel_id=1, source_target_pairs={{0,8},{8,0},{16,24},{24,16},{1,9},{9,1},{17,25},{25,17},{2,10},{10... | collective-permute-start | bytes 884744 | tf_op jit(solution)/shard_map/ppermute | solution.py:305
  63.8 1.3 %shard_map.130 = (f32[4,3,128,384]{3,2,1,0:T(8,128)}, bf16[4,3,128,384]{3,2,1,0:T(8,128)(2,1)}, bf16[4,3,128,384]{3,2,1,0:T(8,128)(2,1)}) custom-call(bf16[3,128,384]{2,1,0:T(8,128)(2,1)S(1)} %get-tuple-element.83.refs_0_, bf16[9,128,384]{2,1,0:T(8,128)(2,1)S(1)} %get-tuple-element.84.refs_1_), custom_call_target="tpu_custom_call" | custom-call | flops 2949120 | bytes 2359296 | tf_op jit(solution)/shard_map/pallas_call | solution.py:289
  65.2 7.0 %collective-permute-done.17.refs_3_.refs_0_ = bf16[4,128,384]{2,1,0:T(8,128)(2,1)S(1)} collective-permute-done((bf16[4,128,384]{2,1,0:T(8,128)(2,1)S(1)}, bf16[4,128,384]{2,1,0:T(8,128)(2,1)S(1)}, u32[]{:S(2)}, u32[]{:S(2)}) %collective-permute-start.17) | collective-permute-done | bytes 393248 | tf_op jit(solution)/shard_map/ppermute | solution.py:305
  72.2 1.3 %shard_map.131 = (f32[4,3,128,384]{3,2,1,0:T(8,128)}, bf16[4,3,128,384]{3,2,1,0:T(8,128)(2,1)}, bf16[4,3,128,384]{3,2,1,0:T(8,128)(2,1)}) custom-call(bf16[4,128,384]{2,1,0:T(8,128)(2,1)S(1)} %collective-permute-done.17.refs_3_.refs_0_, ...), custom_call_target="tpu_custom_call", output_to_operand_aliasing={{0}: (2, {}), {1}: (3, {}), {2}: (4, {})} | custom-call | flops 2949120 | bytes 2359296 | tf_op jit(solution)/shard_map/pallas_call | solution.py:289
  74.5 3.0 %collective-permute-done.18.refs_0_ = bf16[3,128,384]{2,1,0:T(8,128)(2,1)S(1)} collective-permute-done((bf16[3,128,384]{2,1,0:T(8,128)(2,1)S(1)}, bf16[3,128,384]{2,1,0:T(8,128)(2,1)S(1)}, u32[]{:S(2)}, u32[]{:S(2)}) %collective-permute-start.18) | collective-permute-done | bytes 294944 | tf_op jit(solution)/shard_map/ppermute | solution.py:305
  77.6 2.0 %shard_map.132 = (f32[4,3,128,384]{3,2,1,0:T(8,128)}, bf16[4,3,128,384]{3,2,1,0:T(8,128)(2,1)}, bf16[4,3,128,384]{3,2,1,0:T(8,128)(2,1)}) custom-call(bf16[3,128,384]{2,1,0:T(8,128)(2,1)S(1)} %collective-permute-done.18.refs_0_, bf16[10,128,384]{2,1,0:T(8,128)(2,1)S(1)} %collective-permute-done.6.refs_1_, ...), custom_call_target="tpu_custom_call", output_to_operand_aliasing={{0}: (4, {}), {1}: (5, {}), {2}: (6, {})} | custom-call | flops 5898240 | bytes 4718592 | tf_op jit(solution)/shard_map/pallas_call | solution.py:289
  (44 shorter events, 8.6 us)
Async XLA Ops:
  3.0 9.2 %collective-permute-start = (bf16[4,40,512]{2,1,0:T(8,128)(2,1)}, bf16[4,40,512]{2,1,0:T(8,128)(2,1)S(1)}, u32[]{:S(2)}, u32[]{:S(2)}) collective-permute-start(bf16[4,40,512]{2,1,0:T(8,128)(2,1)} %get-tuple-element.50), channel_id=1, source_target_pairs={{0,24},{8,16},{16,8},{24,0},{1,25},{9,17},{17,9},{25,1},{2,26},{10... | collective-permute-start | bytes 491528 | tf_op jit(solution)/shard_map/ppermute | solution.py:305
  7.0 7.9 %collective-permute-start.1 = (bf16[4,40,512]{2,1,0:T(8,128)(2,1)}, bf16[4,40,512]{2,1,0:T(8,128)(2,1)S(1)}, u32[]{:S(2)}, u32[]{:S(2)}) collective-permute-start(bf16[4,40,512]{2,1,0:T(8,128)(2,1)} %get-tuple-element.51), channel_id=1, source_target_pairs={{0,16},{8,24},{16,0},{24,8},{1,17},{9,25},{17,1},{25,9},{2,18},{10... | collective-permute-start | bytes 491528 | tf_op jit(solution)/shard_map/ppermute | solution.py:305
  7.5 7.7 %collective-permute-start.2 = (bf16[4,40,512]{2,1,0:T(8,128)(2,1)}, bf16[4,40,512]{2,1,0:T(8,128)(2,1)S(1)}, u32[]{:S(2)}, u32[]{:S(2)}) collective-permute-start(bf16[4,40,512]{2,1,0:T(8,128)(2,1)} %get-tuple-element.52), channel_id=1, source_target_pairs={{0,8},{8,0},{16,24},{24,16},{1,9},{9,1},{17,25},{25,17},{2,10},{10... | collective-permute-start | bytes 491528 | tf_op jit(solution)/shard_map/ppermute | solution.py:305
  7.6 3.3 %copy-start.3 = (bf16[1,512,3,384]{3,1,2,0:T(8,128)(2,1)S(1)}, bf16[1,512,3,384]{3,1,2,0:T(8,128)(2,1)}, u32[]{:S(2)}) copy-start(bf16[1,512,3,384]{3,1,2,0:T(8,128)(2,1)} %param.16) | copy-start | bytes 3538948
  7.6 3.3 %copy-start.6 = (s32[4,4]{1,0:T(4,128)S(1)}, s32[4,4]{1,0:T(4,128)}, u32[]{:S(2)}) copy-start(s32[4,4]{1,0:T(4,128)} %owner_ref.5) | copy-start | bytes 196
  10.9 4.3 %copy-start.4 = (bf16[4,40,512]{2,1,0:T(8,128)(2,1)S(1)}, bf16[4,40,512]{2,1,0:T(8,128)(2,1)}, u32[]{:S(2)}) copy-start(bf16[4,40,512]{2,1,0:T(8,128)(2,1)} %get-tuple-element.61.refs_3_) | copy-start | bytes 491524
  10.9 7.7 %copy-start.1 = (bf16[1,2048,384]{2,1,0:T(8,128)(2,1)S(1)}, bf16[1,2048,384]{2,1,0:T(8,128)(2,1)}, u32[]{:S(2)}) copy-start(bf16[1,2048,384]{2,1,0:T(8,128)(2,1)} %param.13) | copy-start | bytes 4718596
  15.3 3.4 %collective-permute-start.3 = (bf16[4,160,512]{2,1,0:T(8,128)(2,1)S(1)}, bf16[4,160,512]{2,1,0:T(8,128)(2,1)S(1)}, u32[]{:S(2)}, u32[]{:S(2)}) collective-permute-start(bf16[4,160,512]{2,1,0:T(8,128)(2,1)S(1)} %get-tuple-element.62.mine_ref.refs_0_), channel_id=1, source_target_pairs={{0,4},{4,0},{1,5},{5,1},{2,6},{6,2},{3,7},{7,3},{8,12},{12,8},{9,1... | collective-permute-start | bytes 1966088 | tf_op jit(solution)/shard_map/ppermute | solution.py:305
  15.3 23.0 %collective-permute-start.7 = (bf16[9,128,384]{2,1,0:T(8,128)(2,1)S(1)}, bf16[9,128,384]{2,1,0:T(8,128)(2,1)S(1)}, u32[]{:S(2)}, u32[]{:S(2)}) collective-permute-start(bf16[9,128,384]{2,1,0:T(8,128)(2,1)S(1)} %get-tuple-element.73), channel_id=1, source_target_pairs={{0,24},{8,16},{16,8},{24,0},{1,25},{9,17},{17,9},{25,1},{2,26},{10... | collective-permute-start | bytes 2654216 | tf_op jit(solution)/shard_map/ppermute | solution.py:305
  16.9 6.3 %collective-permute-start.4 = (bf16[160,512]{1,0:T(8,128)(2,1)S(1)}, bf16[160,512]{1,0:T(8,128)(2,1)S(1)}, u32[]{:S(2)}, u32[]{:S(2)}) collective-permute-start(bf16[160,512]{1,0:T(8,128)(2,1)S(1)} %get-tuple-element.64), channel_id=1, source_target_pairs={{0,1},{1,0},{2,3},{3,2},{4,5},{5,4},{6,7},{7,6},{8,9},{9,8},{10,11... | collective-permute-start | bytes 491528 | tf_op jit(solution)/shard_map/ppermute | solution.py:305
  19.7 20.7 %collective-permute-start.15 = (bf16[160,1152]{1,0:T(8,128)(2,1)S(1)}, bf16[160,1152]{1,0:T(8,128)(2,1)S(1)}, u32[]{:S(2)}, u32[]{:S(2)}) collective-permute-start(bf16[160,1152]{1,0:T(8,128)(2,1)S(1)} %shard_map.123.pair_ref.refs_8_), channel_id=1, source_target_pairs={{0,2},{1,3},{2,0},{3,1},{4,6},{5,7},{6,4},{7,5},{8,10},{9,11},{10,... | collective-permute-start | bytes 1105928 | tf_op jit(solution)/shard_map/ppermute | solution.py:305
  22.4 18.0 %collective-permute-start.14 = (bf16[160,1152]{1,0:T(8,128)(2,1)S(1)}, bf16[160,1152]{1,0:T(8,128)(2,1)S(1)}, u32[]{:S(2)}, u32[]{:S(2)}) collective-permute-start(bf16[160,1152]{1,0:T(8,128)(2,1)S(1)} %shard_map.123.pair_ref.refs_8_), channel_id=1, source_target_pairs={{0,1},{1,0},{2,3},{3,2},{4,5},{5,4},{6,7},{7,6},{8,9},{9,8},{10,11... | collective-permute-start | bytes 1105928 | tf_op jit(solution)/shard_map/ppermute | solution.py:305
  24.4 5.6 %collective-permute-start.5 = (bf16[160,1024]{1,0:T(8,128)(2,1)S(1)}, bf16[160,1024]{1,0:T(8,128)(2,1)S(1)}, u32[]{:S(2)}, u32[]{:S(2)}) collective-permute-start(bf16[160,1024]{1,0:T(8,128)(2,1)S(1)} %get-tuple-element.67), channel_id=1, source_target_pairs={{0,4},{4,0},{1,5},{5,1},{2,6},{6,2},{3,7},{7,3},{8,12},{12,8},{9,1... | collective-permute-start | bytes 983048 | tf_op jit(solution)/shard_map/ppermute | solution.py:305
  24.5 20.6 %collective-permute-start.9 = (bf16[160,512]{1,0:T(8,128)(2,1)S(1)}, bf16[160,512]{1,0:T(8,128)(2,1)S(1)}, u32[]{:S(2)}, u32[]{:S(2)}) collective-permute-start(bf16[160,512]{1,0:T(8,128)(2,1)S(1)} %get-tuple-element.76), channel_id=1, source_target_pairs={{0,3},{1,2},{2,1},{3,0},{4,7},{5,6},{6,5},{7,4},{8,11},{9,10},{10,... | collective-permute-start | bytes 491528 | tf_op jit(solution)/shard_map/ppermute | solution.py:305
  38.3 35.3 %collective-permute-start.8 = (bf16[10,128,384]{2,1,0:T(8,128)(2,1)S(1)}, bf16[10,128,384]{2,1,0:T(8,128)(2,1)S(1)}, u32[]{:S(2)}, u32[]{:S(2)}) collective-permute-start(bf16[10,128,384]{2,1,0:T(8,128)(2,1)S(1)} %get-tuple-element.74), channel_id=1, source_target_pairs={{0,16},{8,24},{16,0},{24,8},{1,17},{9,25},{17,1},{25,9},{2,18},{10... | collective-permute-start | bytes 2949128 | tf_op jit(solution)/shard_map/ppermute | solution.py:305
  39.7 33.8 %collective-permute-start.6 = (bf16[10,128,384]{2,1,0:T(8,128)(2,1)S(1)}, bf16[10,128,384]{2,1,0:T(8,128)(2,1)S(1)}, u32[]{:S(2)}, u32[]{:S(2)}) collective-permute-start(bf16[10,128,384]{2,1,0:T(8,128)(2,1)S(1)} %get-tuple-element.71), channel_id=1, source_target_pairs={{0,8},{8,0},{16,24},{24,16},{1,9},{9,1},{17,25},{25,17},{2,10},{10... | collective-permute-start | bytes 2949128 | tf_op jit(solution)/shard_map/ppermute | solution.py:305
  40.4 15.8 %collective-permute-start.16 = (bf16[160,1152]{1,0:T(8,128)(2,1)S(1)}, bf16[160,1152]{1,0:T(8,128)(2,1)S(1)}, u32[]{:S(2)}, u32[]{:S(2)}) collective-permute-start(bf16[160,1152]{1,0:T(8,128)(2,1)S(1)} %shard_map.126), channel_id=1, source_target_pairs={{0,1},{1,0},{2,3},{3,2},{4,5},{5,4},{6,7},{7,6},{8,9},{9,8},{10,11... | collective-permute-start | bytes 1105928 | tf_op jit(solution)/shard_map/ppermute | solution.py:305
  45.1 2.7 %collective-permute-start.11 = (bf16[160,512]{1,0:T(8,128)(2,1)S(1)}, bf16[160,512]{1,0:T(8,128)(2,1)S(1)}, u32[]{:S(2)}, u32[]{:S(2)}) collective-permute-start(bf16[160,512]{1,0:T(8,128)(2,1)S(1)} %collective-permute-done.4.refs_1_), channel_id=1, source_target_pairs={{0,4},{4,0},{1,5},{5,1},{2,6},{6,2},{3,7},{7,3},{8,12},{12,8},{9,1... | collective-permute-start | bytes 491528 | tf_op jit(solution)/shard_map/ppermute | solution.py:305
  45.1 9.4 %collective-permute-start.10 = (bf16[160,512]{1,0:T(8,128)(2,1)S(1)}, bf16[160,512]{1,0:T(8,128)(2,1)S(1)}, u32[]{:S(2)}, u32[]{:S(2)}) collective-permute-start(bf16[160,512]{1,0:T(8,128)(2,1)S(1)} %get-tuple-element.77), channel_id=1, source_target_pairs={{0,2},{1,3},{2,0},{3,1},{4,6},{5,7},{6,4},{7,5},{8,10},{9,11},{10,... | collective-permute-start | bytes 491528 | tf_op jit(solution)/shard_map/ppermute | solution.py:305
  47.8 6.7 %collective-permute-start.13 = (bf16[160,512]{1,0:T(8,128)(2,1)S(1)}, bf16[160,512]{1,0:T(8,128)(2,1)S(1)}, u32[]{:S(2)}, u32[]{:S(2)}) collective-permute-start(bf16[160,512]{1,0:T(8,128)(2,1)S(1)} %collective-permute-done.9.refs_3_), channel_id=1, source_target_pairs={{0,4},{4,0},{1,5},{5,1},{2,6},{6,2},{3,7},{7,3},{8,12},{12,8},{9,1... | collective-permute-start | bytes 491528 | tf_op jit(solution)/shard_map/ppermute | solution.py:305
  54.5 1.4 %collective-permute-start.12 = (bf16[160,512]{1,0:T(8,128)(2,1)S(1)}, bf16[160,512]{1,0:T(8,128)(2,1)S(1)}, u32[]{:S(2)}, u32[]{:S(2)}) collective-permute-start(bf16[160,512]{1,0:T(8,128)(2,1)S(1)} %collective-permute-done.10.refs_2_), channel_id=1, source_target_pairs={{0,4},{4,0},{1,5},{5,1},{2,6},{6,2},{3,7},{7,3},{8,12},{12,8},{9,1... | collective-permute-start | bytes 491528 | tf_op jit(solution)/shard_map/ppermute | solution.py:305
  57.7 14.5 %collective-permute-start.17 = (bf16[4,128,384]{2,1,0:T(8,128)(2,1)S(1)}, bf16[4,128,384]{2,1,0:T(8,128)(2,1)S(1)}, u32[]{:S(2)}, u32[]{:S(2)}) collective-permute-start(bf16[4,128,384]{2,1,0:T(8,128)(2,1)S(1)} %get-tuple-element.80), channel_id=1, source_target_pairs={{0,24},{8,16},{16,8},{24,0},{1,25},{9,17},{17,9},{25,1},{2,26},{10... | collective-permute-start | bytes 1179656 | tf_op jit(solution)/shard_map/ppermute | solution.py:305
  62.4 15.2 %collective-permute-start.18 = (bf16[3,128,384]{2,1,0:T(8,128)(2,1)S(1)}, bf16[3,128,384]{2,1,0:T(8,128)(2,1)S(1)}, u32[]{:S(2)}, u32[]{:S(2)}) collective-permute-start(bf16[3,128,384]{2,1,0:T(8,128)(2,1)S(1)} %get-tuple-element.81), channel_id=1, source_target_pairs={{0,8},{8,0},{16,24},{24,16},{1,9},{9,1},{17,25},{25,17},{2,10},{10... | collective-permute-start | bytes 884744 | tf_op jit(solution)/shard_map/ppermute | solution.py:305
  63.7 13.9 %collective-permute-start.19 = (bf16[3,128,384]{2,1,0:T(8,128)(2,1)S(1)}, bf16[3,128,384]{2,1,0:T(8,128)(2,1)S(1)}, u32[]{:S(2)}, u32[]{:S(2)}) collective-permute-start(bf16[3,128,384]{2,1,0:T(8,128)(2,1)S(1)} %get-tuple-element.82), channel_id=1, source_target_pairs={{0,16},{8,24},{16,0},{24,8},{1,17},{9,25},{17,1},{25,9},{2,18},{10... | collective-permute-start | bytes 884744 | tf_op jit(solution)/shard_map/ppermute | solution.py:305
  (3 other events, 7.0 us)

commit v6 on v5

--- a/solution.py
+++ b/solution.py
@@ -207,31 +207,32 @@
     mine, other = refs[:dp_count], refs[dp_count : 2 * dp_count]
     hidden = refs[2 * dp_count : 3 * dp_count]
     packed = refs[3 * dp_count : 3 * dp_count + len(with_piece)]
-    outs = refs[3 * dp_count + len(with_piece) : -2]
-    rows_ref, hidden_ref = refs[-2:]
+    outs = refs[3 * dp_count + len(with_piece) :]
     me = lax.axis_index("expert")
     core = lax.axis_index("cuts")
     part = lax.axis_index("dp")
     height, units = outs[0].shape[1:]
-    slots = hidden[0].shape[0]
     half = mine[0].shape[2] // 2
     per_half = half // height
-    for n in range(dp_count):
-        place = slice(n * slots, (n + 1) * slots)
-        hidden_ref[place] = hidden[n][...]
-        for side, source in enumerate((mine, other)):
-            rows_ref[side, place] = source[0][part] if n == 0 else source[n][...]
+    factors = [
+        jnp.concatenate([ref[:, m * units : (m + 1) * units] for ref in hidden], axis=0)
+        for m in range(3)
+    ]
     for out, k in zip(outs, ks):
         j = slice_for(owner_ref, me, me ^ k, experts)
-        side = jnp.where(j // per_half == core, 0, 1)
+        own_side = j // per_half == core
         at = lax.rem(j, per_half) * height
+        rows = {}
+        for offset in (0, half):
+            columns = pl.ds(pl.multiple_of(at + offset, height), height)
+            blocks = []
+            for n in range(dp_count):
+                place = (part, slice(None), columns) if n == 0 else (slice(None), columns)
+                blocks.append(jnp.where(own_side, mine[n][place], other[n][place]))
+            rows[offset] = jnp.concatenate(blocks, axis=0)
         for m, offset in enumerate((0, 0, half)):
-            columns = pl.ds(pl.multiple_of(at + offset, height), height)
             total = lax.dot_general(
-                rows_ref[side, :, columns],
-                hidden_ref[:, m * units : (m + 1) * units],
-                (((0,), (0,)), ((), ())),
-                preferred_element_type=F32,
+                rows[offset], factors[m], (((0,), (0,)), ((), ())), preferred_element_type=F32
             )
             out[m] = (total * (1.0 / dp_count)).astype(BF16)
         if k in with_piece:
@@ -444,10 +445,6 @@
             [shape(3 + (k in some), height, units) for k in ks],
             1 + 3 * dp_count + len(some),
             smem=(0,),
-            scratch=[
-                pltpu.VMEM((2, slots * dp_count, 2 * half), BF16),
-                pltpu.VMEM((slots * dp_count, 3 * units), BF16),
-            ],
             flops=6 * slots * dp_count * height * len(ks) * units,
             moved=4 * slots * dp_count * (shard_rows + units),
         )(new_owner, *rows_mine, *rows_other, *hiddens, *[summed[k] for k in some])

time: 79.7 us -> 79.7 us (level)
  no operation moved by 1% of the time
where the time goes in v6:
time: 79.7 us; the launch traced here: 79.5 us
  waiting for transfers between devices  33 us (41%)
  starting transfers between devices  28 us (35%)
  Pallas kernels  14.5 us (18%)
  local copies, waits for them, and re-layouts  3.28 us (4%)
    ppermute x20, waiting for transfers between devices, exchange(): return lax.ppermute(tensor, axis, [(i, i ^ k) for i in range(count)])  33 us
    ppermute x20, starting transfers between devices, exchange(): return lax.ppermute(tensor, axis, [(i, i ^ k) for i in range(count)])  28 us
    pallas_call x3, Pallas kernels, adam_step(): pl.pallas_call(functools.partial(adam_kernel, [(k, places) for k, places,...  4.65 us
    unnamed x15, local copies, waits for them, and re-layouts  3.28 us
    pallas_call x2, Pallas kernels, aligned_local(): call(functools.partial(weight_kernel, experts, dp_count, ks, some), [shap...  2.88 us
    pallas_call x1, Pallas kernels, aligned_local(): call(functools.partial(dispatch_kernel, experts, capacity, dp_count), [sh...  2.36 us
  transfers between devices with their start and end apart: 20, of which 11 were waited for; matrix products, arithmetic and copies ran while one was open for 3% of the time, Pallas kernels for 13%

profile of v6, /device:TPU:0, one launch (start us, length us, event | category | flops | bytes accessed | tf_op | source)
XLA Modules:
  0.0 79.5 jit_solution(301866320218458848)
XLA Ops:
  0.6 2.4 %shard_map.120 = (bf16[4,40,512]{2,1,0:T(8,128)(2,1)}, bf16[4,40,512]{2,1,0:T(8,128)(2,1)}, bf16[4,40,512]{2,1,0:T(8,128)(2,1)}, bf16[4,40,512]{2,1,0:T(8,128)(2,1)}, bf16[160,128]{1,0:T(8,128)(2,1)}) custom-call(s32[1,128]{1,0:T(1,128)} %bitcast.33, bf16[128,2048]{1,0:T(8,128)(2,1)} %in_any.1, bf16[128,2048]{1,0:T(8,128)(2,1)} %grad_any.1), custom_call_target="tpu_custom_call" | custom-call | flops 83886080 | bytes 1835008 | tf_op jit(solution)/shard_map/pallas_call | solution.py:338
  3.0 4.0 %collective-permute-start = (bf16[4,40,512]{2,1,0:T(8,128)(2,1)}, bf16[4,40,512]{2,1,0:T(8,128)(2,1)S(1)}, u32[]{:S(2)}, u32[]{:S(2)}) collective-permute-start(bf16[4,40,512]{2,1,0:T(8,128)(2,1)} %get-tuple-element.50), channel_id=1, source_target_pairs={{0,24},{8,16},{16,8},{24,0},{1,25},{9,17},{17,9},{25,1},{2,26},{10... | collective-permute-start | bytes 491528 | tf_op jit(solution)/shard_map/ppermute | solution.py:306
  7.6 2.7 %copy.21 = bf16[256,8,2,384]{3,1,2,0:T(8,128)(2,1)S(1)} copy(bf16[256,8,2,384]{3,2,1,0:T(2,128)(2,1)} %bitcast.32) | data formatting | bytes 6291456
  12.2 2.7 %collective-permute-done.1.refs_1_ = bf16[4,40,512]{2,1,0:T(8,128)(2,1)S(1)} collective-permute-done((bf16[4,40,512]{2,1,0:T(8,128)(2,1)}, bf16[4,40,512]{2,1,0:T(8,128)(2,1)S(1)}, u32[]{:S(2)}, u32[]{:S(2)}) %collective-permute-start.1) | collective-permute-done | bytes 163872 | tf_op jit(solution)/shard_map/ppermute | solution.py:306
  15.3 1.6 %collective-permute-start.7 = (bf16[9,128,384]{2,1,0:T(8,128)(2,1)S(1)}, bf16[9,128,384]{2,1,0:T(8,128)(2,1)S(1)}, u32[]{:S(2)}, u32[]{:S(2)}) collective-permute-start(bf16[9,128,384]{2,1,0:T(8,128)(2,1)S(1)} %get-tuple-element.73), channel_id=1, source_target_pairs={{0,24},{8,16},{16,8},{24,0},{1,25},{9,17},{17,9},{25,1},{2,26},{10... | collective-permute-start | bytes 2654216 | tf_op jit(solution)/shard_map/ppermute | solution.py:306
  16.9 1.7 %collective-permute-start.4 = (bf16[160,512]{1,0:T(8,128)(2,1)S(1)}, bf16[160,512]{1,0:T(8,128)(2,1)S(1)}, u32[]{:S(2)}, u32[]{:S(2)}) collective-permute-start(bf16[160,512]{1,0:T(8,128)(2,1)S(1)} %get-tuple-element.64), channel_id=1, source_target_pairs={{0,1},{1,0},{2,3},{3,2},{4,5},{5,4},{6,7},{7,6},{8,9},{9,8},{10,11... | collective-permute-start | bytes 491528 | tf_op jit(solution)/shard_map/ppermute | solution.py:306
  19.7 2.7 %collective-permute-start.15 = (bf16[160,1152]{1,0:T(8,128)(2,1)S(1)}, bf16[160,1152]{1,0:T(8,128)(2,1)S(1)}, u32[]{:S(2)}, u32[]{:S(2)}) collective-permute-start(bf16[160,1152]{1,0:T(8,128)(2,1)S(1)} %shard_map.123.pair_ref.refs_8_), channel_id=1, source_target_pairs={{0,2},{1,3},{2,0},{3,1},{4,6},{5,7},{6,4},{7,5},{8,10},{9,11},{10,... | collective-permute-start | bytes 1105928 | tf_op jit(solution)/shard_map/ppermute | solution.py:306
  24.5 5.5 %collective-permute-start.9 = (bf16[160,512]{1,0:T(8,128)(2,1)S(1)}, bf16[160,512]{1,0:T(8,128)(2,1)S(1)}, u32[]{:S(2)}, u32[]{:S(2)}) collective-permute-start(bf16[160,512]{1,0:T(8,128)(2,1)S(1)} %get-tuple-element.76), channel_id=1, source_target_pairs={{0,3},{1,2},{2,1},{3,0},{4,7},{5,6},{6,5},{7,4},{8,11},{9,10},{10,... | collective-permute-start | bytes 491528 | tf_op jit(solution)/shard_map/ppermute | solution.py:306
  30.1 8.2 %collective-permute-done.7.refs_1_ = bf16[9,128,384]{2,1,0:T(8,128)(2,1)S(1)} collective-permute-done((bf16[9,128,384]{2,1,0:T(8,128)(2,1)S(1)}, bf16[9,128,384]{2,1,0:T(8,128)(2,1)S(1)}, u32[]{:S(2)}, u32[]{:S(2)}) %collective-permute-start.7) | collective-permute-done | bytes 884768 | tf_op jit(solution)/shard_map/ppermute | solution.py:306
  38.3 1.4 %collective-permute-start.8 = (bf16[10,128,384]{2,1,0:T(8,128)(2,1)S(1)}, bf16[10,128,384]{2,1,0:T(8,128)(2,1)S(1)}, u32[]{:S(2)}, u32[]{:S(2)}) collective-permute-start(bf16[10,128,384]{2,1,0:T(8,128)(2,1)S(1)} %get-tuple-element.74), channel_id=1, source_target_pairs={{0,16},{8,24},{16,0},{24,8},{1,17},{9,25},{17,1},{25,9},{2,18},{10... | collective-permute-start | bytes 2949128 | tf_op jit(solution)/shard_map/ppermute | solution.py:306
  40.4 1.8 %collective-permute-start.16 = (bf16[160,1152]{1,0:T(8,128)(2,1)S(1)}, bf16[160,1152]{1,0:T(8,128)(2,1)S(1)}, u32[]{:S(2)}, u32[]{:S(2)}) collective-permute-start(bf16[160,1152]{1,0:T(8,128)(2,1)S(1)} %shard_map.126), channel_id=1, source_target_pairs={{0,1},{1,0},{2,3},{3,2},{4,5},{5,4},{6,7},{7,6},{8,9},{9,8},{10,11... | collective-permute-start | bytes 1105928 | tf_op jit(solution)/shard_map/ppermute | solution.py:306
  42.2 2.9 %collective-permute-done.9.refs_3_ = bf16[160,512]{1,0:T(8,128)(2,1)S(1)} collective-permute-done((bf16[160,512]{1,0:T(8,128)(2,1)S(1)}, bf16[160,512]{1,0:T(8,128)(2,1)S(1)}, u32[]{:S(2)}, u32[]{:S(2)}) %collective-permute-start.9) | collective-permute-done | bytes 163872 | tf_op jit(solution)/shard_map/ppermute | solution.py:306
  45.1 2.7 %collective-permute-start.10 = (bf16[160,512]{1,0:T(8,128)(2,1)S(1)}, bf16[160,512]{1,0:T(8,128)(2,1)S(1)}, u32[]{:S(2)}, u32[]{:S(2)}) collective-permute-start(bf16[160,512]{1,0:T(8,128)(2,1)S(1)} %get-tuple-element.77), channel_id=1, source_target_pairs={{0,2},{1,3},{2,0},{3,1},{4,6},{5,7},{6,4},{7,5},{8,10},{9,11},{10,... | collective-permute-start | bytes 491528 | tf_op jit(solution)/shard_map/ppermute | solution.py:306
  48.0 6.4 %collective-permute-done.10.refs_2_ = bf16[160,512]{1,0:T(8,128)(2,1)S(1)} collective-permute-done((bf16[160,512]{1,0:T(8,128)(2,1)S(1)}, bf16[160,512]{1,0:T(8,128)(2,1)S(1)}, u32[]{:S(2)}, u32[]{:S(2)}) %collective-permute-start.10) | collective-permute-done | bytes 163872 | tf_op jit(solution)/shard_map/ppermute | solution.py:306
  54.5 1.4 %collective-permute-done.12.refs_6_ = bf16[160,512]{1,0:T(8,128)(2,1)S(1)} collective-permute-done((bf16[160,512]{1,0:T(8,128)(2,1)S(1)}, bf16[160,512]{1,0:T(8,128)(2,1)S(1)}, u32[]{:S(2)}, u32[]{:S(2)}) %collective-permute-start.12) | collective-permute-done | bytes 163872 | tf_op jit(solution)/shard_map/ppermute | solution.py:306
  56.2 1.4 %shard_map.127 = (bf16[4,128,384]{2,1,0:T(8,128)(2,1)S(1)}, bf16[3,128,384]{2,1,0:T(8,128)(2,1)S(1)}) custom-call(s32[4,4]{1,0:T(4,128)S(1)} %copy-done.6, bf16[4,160,512]{2,1,0:T(8,128)(2,1)S(1)} %get-tuple-element.62.mine_ref.refs_0_, bf16[160,512]{1,0:T(8,128)(2,1)S(1)} %collective-permute-done.4.refs_1_, ...), custom_call_target="tpu_custom_call" | custom-call | flops 377487360 | bytes 2293760 | tf_op jit(solution)/shard_map/pallas_call | solution.py:443
  57.7 3.1 %collective-permute-start.17 = (bf16[4,128,384]{2,1,0:T(8,128)(2,1)S(1)}, bf16[4,128,384]{2,1,0:T(8,128)(2,1)S(1)}, u32[]{:S(2)}, u32[]{:S(2)}) collective-permute-start(bf16[4,128,384]{2,1,0:T(8,128)(2,1)S(1)} %get-tuple-element.80), channel_id=1, source_target_pairs={{0,24},{8,16},{16,8},{24,0},{1,25},{9,17},{17,9},{25,1},{2,26},{10... | collective-permute-start | bytes 1179656 | tf_op jit(solution)/shard_map/ppermute | solution.py:306
  60.7 1.4 %shard_map.129 = (bf16[3,128,384]{2,1,0:T(8,128)(2,1)S(1)}, bf16[3,128,384]{2,1,0:T(8,128)(2,1)S(1)}) custom-call(s32[4,4]{1,0:T(4,128)S(1)} %copy-done.6, bf16[4,160,512]{2,1,0:T(8,128)(2,1)S(1)} %get-tuple-element.62.mine_ref.refs_0_, bf16[160,512]{1,0:T(8,128)(2,1)S(1)} %collective-permute-done.4.refs_1_, ...), custom_call_target="tpu_custom_call" | custom-call | flops 377487360 | bytes 2293760 | tf_op jit(solution)/shard_map/pallas_call | solution.py:443
  62.2 1.3 %collective-permute-start.18 = (bf16[3,128,384]{2,1,0:T(8,128)(2,1)S(1)}, bf16[3,128,384]{2,1,0:T(8,128)(2,1)S(1)}, u32[]{:S(2)}, u32[]{:S(2)}) collective-permute-start(bf16[3,128,384]{2,1,0:T(8,128)(2,1)S(1)} %get-tuple-element.81), channel_id=1, source_target_pairs={{0,8},{8,0},{16,24},{24,16},{1,9},{9,1},{17,25},{25,17},{2,10},{10... | collective-permute-start | bytes 884744 | tf_op jit(solution)/shard_map/ppermute | solution.py:306
  63.6 1.3 %shard_map.130 = (f32[4,3,128,384]{3,2,1,0:T(8,128)}, bf16[4,3,128,384]{3,2,1,0:T(8,128)(2,1)}, bf16[4,3,128,384]{3,2,1,0:T(8,128)(2,1)}) custom-call(bf16[3,128,384]{2,1,0:T(8,128)(2,1)S(1)} %get-tuple-element.83.refs_0_, bf16[9,128,384]{2,1,0:T(8,128)(2,1)S(1)} %get-tuple-element.84.refs_1_), custom_call_target="tpu_custom_call" | custom-call | flops 2949120 | bytes 2359296 | tf_op jit(solution)/shard_map/pallas_call | solution.py:290
  65.0 7.3 %collective-permute-done.17.refs_3_.refs_0_ = bf16[4,128,384]{2,1,0:T(8,128)(2,1)S(1)} collective-permute-done((bf16[4,128,384]{2,1,0:T(8,128)(2,1)S(1)}, bf16[4,128,384]{2,1,0:T(8,128)(2,1)S(1)}, u32[]{:S(2)}, u32[]{:S(2)}) %collective-permute-start.17) | collective-permute-done | bytes 393248 | tf_op jit(solution)/shard_map/ppermute | solution.py:306
  72.3 1.3 %shard_map.131 = (f32[4,3,128,384]{3,2,1,0:T(8,128)}, bf16[4,3,128,384]{3,2,1,0:T(8,128)(2,1)}, bf16[4,3,128,384]{3,2,1,0:T(8,128)(2,1)}) custom-call(bf16[4,128,384]{2,1,0:T(8,128)(2,1)S(1)} %collective-permute-done.17.refs_3_.refs_0_, ...), custom_call_target="tpu_custom_call", output_to_operand_aliasing={{0}: (2, {}), {1}: (3, {}), {2}: (4, {})} | custom-call | flops 2949120 | bytes 2359296 | tf_op jit(solution)/shard_map/pallas_call | solution.py:290
  74.6 2.9 %collective-permute-done.18.refs_0_ = bf16[3,128,384]{2,1,0:T(8,128)(2,1)S(1)} collective-permute-done((bf16[3,128,384]{2,1,0:T(8,128)(2,1)S(1)}, bf16[3,128,384]{2,1,0:T(8,128)(2,1)S(1)}, u32[]{:S(2)}, u32[]{:S(2)}) %collective-permute-start.18) | collective-permute-done | bytes 294944 | tf_op jit(solution)/shard_map/ppermute | solution.py:306
  77.6 2.0 %shard_map.132 = (f32[4,3,128,384]{3,2,1,0:T(8,128)}, bf16[4,3,128,384]{3,2,1,0:T(8,128)(2,1)}, bf16[4,3,128,384]{3,2,1,0:T(8,128)(2,1)}) custom-call(bf16[3,128,384]{2,1,0:T(8,128)(2,1)S(1)} %collective-permute-done.18.refs_0_, bf16[10,128,384]{2,1,0:T(8,128)(2,1)S(1)} %collective-permute-done.6.refs_1_, ...), custom_call_target="tpu_custom_call", output_to_operand_aliasing={{0}: (4, {}), {1}: (5, {}), {2}: (6, {})} | custom-call | flops 5898240 | bytes 4718592 | tf_op jit(solution)/shard_map/pallas_call | solution.py:290
  (44 shorter events, 8.6 us)
Async XLA Ops:
  3.0 9.2 %collective-permute-start = (bf16[4,40,512]{2,1,0:T(8,128)(2,1)}, bf16[4,40,512]{2,1,0:T(8,128)(2,1)S(1)}, u32[]{:S(2)}, u32[]{:S(2)}) collective-permute-start(bf16[4,40,512]{2,1,0:T(8,128)(2,1)} %get-tuple-element.50), channel_id=1, source_target_pairs={{0,24},{8,16},{16,8},{24,0},{1,25},{9,17},{17,9},{25,1},{2,26},{10... | collective-permute-start | bytes 491528 | tf_op jit(solution)/shard_map/ppermute | solution.py:306
  7.0 7.9 %collective-permute-start.1 = (bf16[4,40,512]{2,1,0:T(8,128)(2,1)}, bf16[4,40,512]{2,1,0:T(8,128)(2,1)S(1)}, u32[]{:S(2)}, u32[]{:S(2)}) collective-permute-start(bf16[4,40,512]{2,1,0:T(8,128)(2,1)} %get-tuple-element.51), channel_id=1, source_target_pairs={{0,16},{8,24},{16,0},{24,8},{1,17},{9,25},{17,1},{25,9},{2,18},{10... | collective-permute-start | bytes 491528 | tf_op jit(solution)/shard_map/ppermute | solution.py:306
  7.5 7.7 %collective-permute-start.2 = (bf16[4,40,512]{2,1,0:T(8,128)(2,1)}, bf16[4,40,512]{2,1,0:T(8,128)(2,1)S(1)}, u32[]{:S(2)}, u32[]{:S(2)}) collective-permute-start(bf16[4,40,512]{2,1,0:T(8,128)(2,1)} %get-tuple-element.52), channel_id=1, source_target_pairs={{0,8},{8,0},{16,24},{24,16},{1,9},{9,1},{17,25},{25,17},{2,10},{10... | collective-permute-start | bytes 491528 | tf_op jit(solution)/shard_map/ppermute | solution.py:306
  7.6 3.3 %copy-start.3 = (bf16[1,512,3,384]{3,1,2,0:T(8,128)(2,1)S(1)}, bf16[1,512,3,384]{3,1,2,0:T(8,128)(2,1)}, u32[]{:S(2)}) copy-start(bf16[1,512,3,384]{3,1,2,0:T(8,128)(2,1)} %param.16) | copy-start | bytes 3538948
  7.6 3.3 %copy-start.6 = (s32[4,4]{1,0:T(4,128)S(1)}, s32[4,4]{1,0:T(4,128)}, u32[]{:S(2)}) copy-start(s32[4,4]{1,0:T(4,128)} %owner_ref.5) | copy-start | bytes 196
  10.9 4.3 %copy-start.4 = (bf16[4,40,512]{2,1,0:T(8,128)(2,1)S(1)}, bf16[4,40,512]{2,1,0:T(8,128)(2,1)}, u32[]{:S(2)}) copy-start(bf16[4,40,512]{2,1,0:T(8,128)(2,1)} %get-tuple-element.61.refs_3_) | copy-start | bytes 491524
  10.9 7.7 %copy-start.1 = (bf16[1,2048,384]{2,1,0:T(8,128)(2,1)S(1)}, bf16[1,2048,384]{2,1,0:T(8,128)(2,1)}, u32[]{:S(2)}) copy-start(bf16[1,2048,384]{2,1,0:T(8,128)(2,1)} %param.13) | copy-start | bytes 4718596
  15.3 3.4 %collective-permute-start.3 = (bf16[4,160,512]{2,1,0:T(8,128)(2,1)S(1)}, bf16[4,160,512]{2,1,0:T(8,128)(2,1)S(1)}, u32[]{:S(2)}, u32[]{:S(2)}) collective-permute-start(bf16[4,160,512]{2,1,0:T(8,128)(2,1)S(1)} %get-tuple-element.62.mine_ref.refs_0_), channel_id=1, source_target_pairs={{0,4},{4,0},{1,5},{5,1},{2,6},{6,2},{3,7},{7,3},{8,12},{12,8},{9,1... | collective-permute-start | bytes 1966088 | tf_op jit(solution)/shard_map/ppermute | solution.py:306
  15.3 23.0 %collective-permute-start.7 = (bf16[9,128,384]{2,1,0:T(8,128)(2,1)S(1)}, bf16[9,128,384]{2,1,0:T(8,128)(2,1)S(1)}, u32[]{:S(2)}, u32[]{:S(2)}) collective-permute-start(bf16[9,128,384]{2,1,0:T(8,128)(2,1)S(1)} %get-tuple-element.73), channel_id=1, source_target_pairs={{0,24},{8,16},{16,8},{24,0},{1,25},{9,17},{17,9},{25,1},{2,26},{10... | collective-permute-start | bytes 2654216 | tf_op jit(solution)/shard_map/ppermute | solution.py:306
  16.9 6.3 %collective-permute-start.4 = (bf16[160,512]{1,0:T(8,128)(2,1)S(1)}, bf16[160,512]{1,0:T(8,128)(2,1)S(1)}, u32[]{:S(2)}, u32[]{:S(2)}) collective-permute-start(bf16[160,512]{1,0:T(8,128)(2,1)S(1)} %get-tuple-element.64), channel_id=1, source_target_pairs={{0,1},{1,0},{2,3},{3,2},{4,5},{5,4},{6,7},{7,6},{8,9},{9,8},{10,11... | collective-permute-start | bytes 491528 | tf_op jit(solution)/shard_map/ppermute | solution.py:306
  19.7 20.7 %collective-permute-start.15 = (bf16[160,1152]{1,0:T(8,128)(2,1)S(1)}, bf16[160,1152]{1,0:T(8,128)(2,1)S(1)}, u32[]{:S(2)}, u32[]{:S(2)}) collective-permute-start(bf16[160,1152]{1,0:T(8,128)(2,1)S(1)} %shard_map.123.pair_ref.refs_8_), channel_id=1, source_target_pairs={{0,2},{1,3},{2,0},{3,1},{4,6},{5,7},{6,4},{7,5},{8,10},{9,11},{10,... | collective-permute-start | bytes 1105928 | tf_op jit(solution)/shard_map/ppermute | solution.py:306
  22.4 18.0 %collective-permute-start.14 = (bf16[160,1152]{1,0:T(8,128)(2,1)S(1)}, bf16[160,1152]{1,0:T(8,128)(2,1)S(1)}, u32[]{:S(2)}, u32[]{:S(2)}) collective-permute-start(bf16[160,1152]{1,0:T(8,128)(2,1)S(1)} %shard_map.123.pair_ref.refs_8_), channel_id=1, source_target_pairs={{0,1},{1,0},{2,3},{3,2},{4,5},{5,4},{6,7},{7,6},{8,9},{9,8},{10,11... | collective-permute-start | bytes 1105928 | tf_op jit(solution)/shard_map/ppermute | solution.py:306
  24.4 5.6 %collective-permute-start.5 = (bf16[160,1024]{1,0:T(8,128)(2,1)S(1)}, bf16[160,1024]{1,0:T(8,128)(2,1)S(1)}, u32[]{:S(2)}, u32[]{:S(2)}) collective-permute-start(bf16[160,1024]{1,0:T(8,128)(2,1)S(1)} %get-tuple-element.67), channel_id=1, source_target_pairs={{0,4},{4,0},{1,5},{5,1},{2,6},{6,2},{3,7},{7,3},{8,12},{12,8},{9,1... | collective-permute-start | bytes 983048 | tf_op jit(solution)/shard_map/ppermute | solution.py:306
  24.5 20.6 %collective-permute-start.9 = (bf16[160,512]{1,0:T(8,128)(2,1)S(1)}, bf16[160,512]{1,0:T(8,128)(2,1)S(1)}, u32[]{:S(2)}, u32[]{:S(2)}) collective-permute-start(bf16[160,512]{1,0:T(8,128)(2,1)S(1)} %get-tuple-element.76), channel_id=1, source_target_pairs={{0,3},{1,2},{2,1},{3,0},{4,7},{5,6},{6,5},{7,4},{8,11},{9,10},{10,... | collective-permute-start | bytes 491528 | tf_op jit(solution)/shard_map/ppermute | solution.py:306
  38.3 35.3 %collective-permute-start.8 = (bf16[10,128,384]{2,1,0:T(8,128)(2,1)S(1)}, bf16[10,128,384]{2,1,0:T(8,128)(2,1)S(1)}, u32[]{:S(2)}, u32[]{:S(2)}) collective-permute-start(bf16[10,128,384]{2,1,0:T(8,128)(2,1)S(1)} %get-tuple-element.74), channel_id=1, source_target_pairs={{0,16},{8,24},{16,0},{24,8},{1,17},{9,25},{17,1},{25,9},{2,18},{10... | collective-permute-start | bytes 2949128 | tf_op jit(solution)/shard_map/ppermute | solution.py:306
  39.7 33.9 %collective-permute-start.6 = (bf16[10,128,384]{2,1,0:T(8,128)(2,1)S(1)}, bf16[10,128,384]{2,1,0:T(8,128)(2,1)S(1)}, u32[]{:S(2)}, u32[]{:S(2)}) collective-permute-start(bf16[10,128,384]{2,1,0:T(8,128)(2,1)S(1)} %get-tuple-element.71), channel_id=1, source_target_pairs={{0,8},{8,0},{16,24},{24,16},{1,9},{9,1},{17,25},{25,17},{2,10},{10... | collective-permute-start | bytes 2949128 | tf_op jit(solution)/shard_map/ppermute | solution.py:306
  40.4 15.8 %collective-permute-start.16 = (bf16[160,1152]{1,0:T(8,128)(2,1)S(1)}, bf16[160,1152]{1,0:T(8,128)(2,1)S(1)}, u32[]{:S(2)}, u32[]{:S(2)}) collective-permute-start(bf16[160,1152]{1,0:T(8,128)(2,1)S(1)} %shard_map.126), channel_id=1, source_target_pairs={{0,1},{1,0},{2,3},{3,2},{4,5},{5,4},{6,7},{7,6},{8,9},{9,8},{10,11... | collective-permute-start | bytes 1105928 | tf_op jit(solution)/shard_map/ppermute | solution.py:306
  45.1 2.7 %collective-permute-start.11 = (bf16[160,512]{1,0:T(8,128)(2,1)S(1)}, bf16[160,512]{1,0:T(8,128)(2,1)S(1)}, u32[]{:S(2)}, u32[]{:S(2)}) collective-permute-start(bf16[160,512]{1,0:T(8,128)(2,1)S(1)} %collective-permute-done.4.refs_1_), channel_id=1, source_target_pairs={{0,4},{4,0},{1,5},{5,1},{2,6},{6,2},{3,7},{7,3},{8,12},{12,8},{9,1... | collective-permute-start | bytes 491528 | tf_op jit(solution)/shard_map/ppermute | solution.py:306
  45.1 9.4 %collective-permute-start.10 = (bf16[160,512]{1,0:T(8,128)(2,1)S(1)}, bf16[160,512]{1,0:T(8,128)(2,1)S(1)}, u32[]{:S(2)}, u32[]{:S(2)}) collective-permute-start(bf16[160,512]{1,0:T(8,128)(2,1)S(1)} %get-tuple-element.77), channel_id=1, source_target_pairs={{0,2},{1,3},{2,0},{3,1},{4,6},{5,7},{6,4},{7,5},{8,10},{9,11},{10,... | collective-permute-start | bytes 491528 | tf_op jit(solution)/shard_map/ppermute | solution.py:306
  47.8 6.7 %collective-permute-start.13 = (bf16[160,512]{1,0:T(8,128)(2,1)S(1)}, bf16[160,512]{1,0:T(8,128)(2,1)S(1)}, u32[]{:S(2)}, u32[]{:S(2)}) collective-permute-start(bf16[160,512]{1,0:T(8,128)(2,1)S(1)} %collective-permute-done.9.refs_3_), channel_id=1, source_target_pairs={{0,4},{4,0},{1,5},{5,1},{2,6},{6,2},{3,7},{7,3},{8,12},{12,8},{9,1... | collective-permute-start | bytes 491528 | tf_op jit(solution)/shard_map/ppermute | solution.py:306
  54.5 1.4 %collective-permute-start.12 = (bf16[160,512]{1,0:T(8,128)(2,1)S(1)}, bf16[160,512]{1,0:T(8,128)(2,1)S(1)}, u32[]{:S(2)}, u32[]{:S(2)}) collective-permute-start(bf16[160,512]{1,0:T(8,128)(2,1)S(1)} %collective-permute-done.10.refs_2_), channel_id=1, source_target_pairs={{0,4},{4,0},{1,5},{5,1},{2,6},{6,2},{3,7},{7,3},{8,12},{12,8},{9,1... | collective-permute-start | bytes 491528 | tf_op jit(solution)/shard_map/ppermute | solution.py:306
  57.7 14.6 %collective-permute-start.17 = (bf16[4,128,384]{2,1,0:T(8,128)(2,1)S(1)}, bf16[4,128,384]{2,1,0:T(8,128)(2,1)S(1)}, u32[]{:S(2)}, u32[]{:S(2)}) collective-permute-start(bf16[4,128,384]{2,1,0:T(8,128)(2,1)S(1)} %get-tuple-element.80), channel_id=1, source_target_pairs={{0,24},{8,16},{16,8},{24,0},{1,25},{9,17},{17,9},{25,1},{2,26},{10... | collective-permute-start | bytes 1179656 | tf_op jit(solution)/shard_map/ppermute | solution.py:306
  62.2 15.4 %collective-permute-start.18 = (bf16[3,128,384]{2,1,0:T(8,128)(2,1)S(1)}, bf16[3,128,384]{2,1,0:T(8,128)(2,1)S(1)}, u32[]{:S(2)}, u32[]{:S(2)}) collective-permute-start(bf16[3,128,384]{2,1,0:T(8,128)(2,1)S(1)} %get-tuple-element.81), channel_id=1, source_target_pairs={{0,8},{8,0},{16,24},{24,16},{1,9},{9,1},{17,25},{25,17},{2,10},{10... | collective-permute-start | bytes 884744 | tf_op jit(solution)/shard_map/ppermute | solution.py:306
  63.5 14.1 %collective-permute-start.19 = (bf16[3,128,384]{2,1,0:T(8,128)(2,1)S(1)}, bf16[3,128,384]{2,1,0:T(8,128)(2,1)S(1)}, u32[]{:S(2)}, u32[]{:S(2)}) collective-permute-start(bf16[3,128,384]{2,1,0:T(8,128)(2,1)S(1)} %get-tuple-element.82), channel_id=1, source_target_pairs={{0,16},{8,24},{16,0},{24,8},{1,17},{9,25},{17,1},{25,9},{2,18},{10... | collective-permute-start | bytes 884744 | tf_op jit(solution)/shard_map/ppermute | solution.py:306
  (3 other events, 7.0 us)
